TPU v7x, 256 devices: a whole 4x4x8 slice. The times are simulated.
256 devices in a mesh: blk: 128 (over z, x_lo, y, core), rep: 2 (over x_hi).
Axes of the slice: x: 4 (x_hi: 2, x_lo: 2; x = x_hi * 2 + x_lo), y: 4, z: 8, core: 2. Of those that a mesh axis runs over, the one named last changes fastest.
Arguments:
- pooled: bfloat16 [2, 16384, 1536], P('rep', 'blk'), may hold values from -6 to 6
- w_img: bfloat16 [1536, 1024], replicated, may hold values from -0.15625 to 0.15625
- text_emb: bfloat16 [2, 16384, 1024], P('rep', 'blk'), may hold values from -6 to 6
- pos_index: int32 [2, 16384], P('rep', 'blk'), may hold values from 0 to 16383, each once within a row
- log_scale: float32 [1], replicated, may hold values from 1.5 to 2.5
- bias: float32 [1], replicated, may hold values from -2 to -0.5
Outputs:
- row_loss: float32 [2, 16384], P('rep', 'blk')
- weight_grad: float32 [1536, 1024], P(('blk', 'rep'))
- text_grad: float32 [2, 16384, 1024], P('rep', 'blk')
Inputs may be any that keep to these rules, and one draw needn't show every extreme that they name: `pos_index`: each group's row is a permutation of 0 to 16383.
All inputs are finite; a program needn't handle non-finite values.
Results may differ from a plain program's by a relative error of at most 0.0052.
Values may be sent and summed in bfloat16 or wider, within the bound.
No kernel may reach another device: no remote copies, remote signals or barrier semaphores. Data moves between devices by JAX's collectives and lax.ppermute only.
A program may use at most 192 MiB of HBM per device.

v0:
```python
import jax
import jax.numpy as jnp
from jax import lax
from jax.sharding import PartitionSpec as P


def normalize(rows):
    squares = jnp.sum(rows * rows, axis=-1, keepdims=True)
    inverse = lax.rsqrt(squares + 1e-06)
    return (rows * inverse, inverse)


def pair_terms(left, right, left_pos, right_start, scale_value, shift):
    logits = scale_value * jnp.dot(left, right.T, preferred_element_type=jnp.float32) + shift
    columns = right_start + jnp.arange(right.shape[0], dtype=jnp.int32)
    sign = jnp.where(left_pos[:, None] == columns[None, :], 1.0, -1.0).astype(jnp.float32)
    losses = jax.nn.softplus(-sign * logits)
    coeffs = (-sign * jax.nn.sigmoid(-sign * logits) * scale_value).astype(jnp.bfloat16)
    return (jnp.sum(losses, axis=1), coeffs)


def transpose_dot(coeffs, rows):
    return lax.dot_general(
        coeffs, rows, (((0,), (0,)), ((), ())), preferred_element_type=jnp.float32
    )


def shards(pooled, w_img, text_emb, pos_index, log_scale, bias):
    scale_value = jnp.exp(log_scale[0])
    shift = bias[0]
    features = pooled[0]
    my_pos = pos_index[0]
    row_count = features.shape[0]
    group_size = row_count * lax.axis_size("blk")
    my_start = lax.axis_index("blk") * row_count
    projected = jnp.dot(features, w_img, preferred_element_type=jnp.float32)
    image_unit, image_inv = normalize(projected)
    image_low = image_unit.astype(jnp.bfloat16)
    text_unit, text_inv = normalize(text_emb[0].astype(jnp.float32))
    text_low = text_unit.astype(jnp.bfloat16)
    piece = lax.all_gather(text_low, "blk", axis=0, tiled=True)
    row_sums, coeffs = pair_terms(image_low, piece, my_pos, jnp.int32(0), scale_value, shift)
    loss_total = row_sums
    image_dir = jnp.dot(coeffs, piece, preferred_element_type=jnp.float32)
    pieces = (
        lax.all_gather(image_low, "blk", axis=0, tiled=True),
        lax.all_gather(my_pos, "blk", axis=0, tiled=True),
    )
    row_sums, coeffs = pair_terms(pieces[0], text_low, pieces[1], my_start, scale_value, shift)
    text_dir = transpose_dot(coeffs, pieces[0])
    image_back = (
        (image_dir - image_unit * jnp.sum(image_unit * image_dir, axis=-1, keepdims=True))
        * image_inv
    ).astype(jnp.bfloat16)
    text_back = (
        text_dir - text_unit * jnp.sum(text_unit * text_dir, axis=-1, keepdims=True)
    ) * text_inv
    weight_part = transpose_dot(features, image_back)
    weight_sum = lax.psum_scatter(weight_part, ("blk", "rep"), scatter_dimension=0, tiled=True)
    return ((loss_total / group_size)[None], weight_sum / 64.0, text_back[None])


def solution(mesh):
    return jax.shard_map(
        shards,
        mesh=mesh,
        in_specs=(P("rep", "blk", None), P(), P("rep", "blk", None), P("rep", "blk"), P(), P()),
        out_specs=(P("rep", "blk"), P(("blk", "rep"), None), P("rep", "blk", None)),
        check_vma=False,
    )
```

profile of v0, /device:TPU:1, one launch (start us, length us, event | category | flops | bytes accessed | tf_op | source)
XLA Modules:
  0.0 803.7 jit_solution(4236366834139593870)
XLA Ops:
  7.2 0.0 copy-start
  7.2 0.0 all-gather.4.cloned.1.call-start
  7.2 1.2 fusion.25
  8.5 1.8 fusion.20
  10.2 0.0 all-gather.4.cloned.1.call-update
  10.3 0.0 all-gather.6.cloned.1.call-start
  10.3 0.0 copy-done
  10.3 1.7 multiply_reduce_fusion.1
  12.0 0.0 copy-start.2
  12.0 0.8 copy-done.2
  12.8 0.8 multiply_convert_fusion.3
  13.6 0.0 all-gather.6.cloned.1.call-update
  13.6 0.0 all-reduce.3.cloned.1.call-start
  15.0 160.8 %all-gather = s32[1,16384]{1,0:T(1,128)S(1)} all-gather(s32[1,128]{1,0:T(1,128)} %param.9), channel_id=2, replica_groups=mesh['blk'=128,'rep'=2] {'blk'}, dimensions={1}, use_global_device_ids=true | all-gather | bytes 66048 | tf_op jit(solution)/shard_map/all_gather | solution.py:47
  175.8 89.1 %all-gather.4.cloned.1.call-done = bf16[16384,1024]{1,0:T(8,128)(2,1)} async-done(((bf16[128,1024]{1,0:T(8,128)(2,1)}), bf16[16384,1024]{1,0:T(8,128)(2,1)}) %all-gather.4.cloned.1.call-update) | async-done | bytes 33554448 | tf_op jit(solution)/shard_map/all_gather | solution.py:41
  264.9 0.0 copy-start.3
  264.9 0.0 copy-start.6
  264.9 20.4 %fusion.11 = (f32[128]{0:T(128)S(1)}, f32[128,16384]{1,0:T(8,128)}) fusion(f32[]{:T(128)} %bitcast.32, bf16[128,1024]{1,0:T(8,128)(2,1)} %multiply_convert_fusion.3, bf16[16384,1024]{1,0:T(8,128)(2,1)} %all-gather.4.cloned.1.call-done, f32[]{:T(128)} %bitcast.1, s32[128]{0:T(128)} %bitcast.35), kind=kOutput, calls=%fused_computation.14 | convolution fusion | flops 4322230272 | bytes 42206216 | tf_op jit(solution)/shard_map/dot_general | solution.py:14
  285.3 0.5 multiply_bitcast_fusion
  285.8 0.0 copy-done.3
  285.8 0.0 copy-done.6
  285.8 0.0 copy-start.5
  285.9 17.0 %multiply_reduce_fusion = (f32[128]{0:T(128)S(1)}, f32[128,1024]{1,0:T(8,128)S(1)}) fusion(f32[128,1024]{1,0:T(8,128)S(1)} %copy-done.3, f32[128]{0:T(128)S(1)} %add_rsqrt_fusion.1, bf16[16384,1024]{1,0:T(8,128)(2,1)} %all-gather.4.cloned.1.call-done, f32[128,16384]{1,0:T(8,128)} %get-tuple-element.12, f32[]{:T(128)} %bitcast.1, s32[128]{0:T(128)S(1)} %bitcast.36), kind=kOutput, calls=%fused_computation.37 | convolution fusion | flops 4314234880 | bytes 42993156 | tf_op jit(solution)/shard_map/dot_general | solution.py:44
  302.8 0.0 copy-done.5
  302.9 0.0 copy-start.4
  302.9 3.7 convolution_bitcast_fusion
  306.6 0.0 all-reduce.3.cloned.1.call-update
  306.6 210.3 %all-gather.6.cloned.1.call-done = bf16[16384,1024]{1,0:T(8,128)(2,1)} async-done(((bf16[128,1024]{1,0:T(8,128)(2,1)}), bf16[16384,1024]{1,0:T(8,128)(2,1)}) %all-gather.6.cloned.1.call-update) | async-done | bytes 33554448 | tf_op jit(solution)/shard_map/all_gather | solution.py:46
  516.9 0.0 copy-done.4
  516.9 0.0 copy-start.1
  516.9 34.6 %fusion.21 = (f32[128]{0:T(128)S(1)}, f32[128,1024]{1,0:T(8,128)}) fusion(bf16[1,128,1024]{2,1,0:T(8,128)(2,1)S(1)} %copy-done.4, f32[128]{0:T(128)S(1)} %add_rsqrt_fusion, bf16[16384,1024]{1,0:T(8,128)(2,1)} %all-gather.6.cloned.1.call-done, bf16[128,1024]{1,0:T(8,128)(2,1)} %fusion.20, f32[]{:T(128)} %bitcast.33, f32[]{:T(128)} %bitcast.1, ...), kind=kOutput, calls=%fused_computation.30 | convolution fusion | flops 8615624704 | bytes 34670088 | tf_op jit(solution)/shard_map/dot_general | solution.py:23
  551.5 2.1 fusion.24
  553.6 239.5 %all-reduce.3.cloned.1.call-done = f32[1536,1024]{0,1:T(8,128)} async-done(((f32[1536,1024]{0,1:T(8,128)}), f32[1536,1024]{0,1:T(8,128)}) %all-reduce.3.cloned.1.call-update) | async-done | bytes 6291472
  793.1 2.2 dynamic-slice_multiply_fusion
  795.4 1.8 copy.10
  797.2 0.0 copy-done.1
  (3 shorter events, 0.0 us)
Async XLA Ops:
  7.2 3.2 copy-start
  7.2 257.7 %all-gather.4.cloned.1.call-start = ((), (), s32[]{:S(2)}) async-start(), calls=%async_computation | async-start | bytes 33816576 | tf_op jit(solution)/shard_map/all_gather | solution.py:41
  10.3 506.7 %all-gather.6.cloned.1.call-start = ((), (), s32[]{:S(2)}) async-start(), calls=%async_computation.1 | async-start | bytes 33816576 | tf_op jit(solution)/shard_map/all_gather | solution.py:46
  12.0 0.8 copy-start.2
  13.6 779.5 %all-reduce.3.cloned.1.call-start = ((), (), s32[]{:S(2)}) async-start(), calls=%async_computation.2 | async-start | bytes 12582912
  264.9 20.9 %copy-start.3 = (f32[128,1024]{1,0:T(8,128)S(1)}, f32[128,1024]{1,0:T(8,128)}, u32[]{:S(2)}) copy-start(f32[128,1024]{1,0:T(8,128)} %copy-done.2) | copy-start | bytes 1572868
  264.9 20.9 %copy-start.6 = (s32[1,128]{1,0:T(1,128)S(1)}, s32[1,128]{1,0:T(1,128)}, u32[]{:S(2)}) copy-start(s32[1,128]{1,0:T(1,128)} %param.9) | copy-start | bytes 1540
  285.8 17.0 %copy-start.5 = (bf16[1,128,1536]{2,1,0:T(8,128)(2,1)S(1)}, bf16[1,128,1536]{2,1,0:T(8,128)(2,1)}, u32[]{:S(2)}) copy-start(bf16[1,128,1536]{2,1,0:T(8,128)(2,1)} %param.6) | copy-start | bytes 1179652
  302.9 214.1 %copy-start.4 = (bf16[1,128,1024]{2,1,0:T(8,128)(2,1)S(1)}, bf16[1,128,1024]{2,1,0:T(8,128)(2,1)}, u32[]{:S(2)}) copy-start(bf16[1,128,1024]{2,1,0:T(8,128)(2,1)} %param.8) | copy-start | bytes 786436
  516.9 280.3 %copy-start.1 = (bf16[1536,1024]{1,0:T(8,128)(2,1)S(1)}, bf16[1536,1024]{1,0:T(8,128)(2,1)}, u32[]{:S(2)}) copy-start(bf16[1536,1024]{1,0:T(8,128)(2,1)} %param.7) | copy-start | bytes 9437188
Sparse Core Ops, SparseCore 0:
  10.4 254.4 all-gather.3
  266.8 250.0 all-gather.5
  522.4 270.7 all-reduce.2
where the time goes:
time: 805 us; the launch traced here: 804 us
  waiting for transfers between devices  539 us (67%)
  blocking collectives  161 us (20%)
  matrix products  77.3 us (10%)
  between operations  15.1 us (2%)
  other arithmetic  8.64 us (1%)
    unnamed x4, waiting for transfers between devices  240 us
    all_gather x1, waiting for transfers between devices, shards(): lax.all_gather(image_low, 'blk', axis=0, tiled=True)  210 us
    all_gather x1, blocking collectives, shards(): lax.all_gather(my_pos, 'blk', axis=0, tiled=True)  161 us
    all_gather x1, waiting for transfers between devices, shards(): piece = lax.all_gather(text_low, 'blk', axis=0, tiled=True)  89.1 us
    dot_general x2, matrix products, transpose_dot(): lax.dot_general(coeffs, rows, (((0,), (0,)), ((), ())), preferred_element...  38.3 us
    dot_general x1, matrix products, pair_terms(): jnp.dot(left, right.T, preferred_element_type=jnp.float32)  20.4 us
    dot_general x1, matrix products, shards(): image_dir = jnp.dot(coeffs, piece, preferred_element_type=jnp.float32)  17 us
  transfers between devices with their start and end apart: 3, of which 3 were waited for; matrix products, arithmetic and copies ran while one was open for 10% of the time, Pallas kernels for 0%

commit v1 on v0

v1 whole, which is shorter than its diff:
```python
import jax
import jax.numpy as jnp
import numpy as np
from jax import lax
from jax.experimental import pallas as pl
from jax.experimental.pallas import tpu as pltpu
from jax.sharding import Mesh
from jax.sharding import PartitionSpec as P

NZ, NX, NY, NC, NR = 8, 2, 4, 2, 2
ROWS = 128
HALF = ROWS // 2
D_IMG = 1536
D_EMB = 1024
PAD = 128
IMGS = NZ * ROWS
TEXTS = NX * NY * NC * ROWS
STEP = 256
CHUNK = 512
BF, F32 = jnp.bfloat16, jnp.float32
Z_OFFSETS = (0, -1, 1, -2, 2, -3, 3, 4)


def shift(x, axis, n, by):
    return lax.ppermute(x, axis, [(i, (i + by) % n) for i in range(n)])


def flip(x, axis, n, bit=1):
    return lax.ppermute(x, axis, [(i, i ^ bit) for i in range(n)])


def exchange(x, axes):
    return lax.all_to_all(x, axes, 0, 0)


def gather(image, text):
    down, up = [image], [image]
    for k in range(3):
        down.append(shift(down[-1], "z", NZ, 1))
        up.append(shift(up[-1], "z", NZ, -1))
        if k == 0:
            copies = jnp.broadcast_to(text, (NX * NY, *text.shape))
            down[1], up[1], copies = lax.optimization_barrier((down[1], up[1], copies))
            near = exchange(copies, ("xl", "y")).reshape(NX * NY * ROWS, D_EMB)
        if k == 1:
            down[2], up[2] = lax.optimization_barrier((down[2], up[2]))
    down[3], up[3], near = lax.optimization_barrier((down[3], up[3], near))
    far = [shift(down[3][:HALF], "z", NZ, 1), shift(up[3][HALF:], "z", NZ, -1)]
    images = [image, down[1], up[1], down[2], up[2], down[3], up[3]] + far
    return images, [near, flip(near, "core", NC)]


def halve(w, dim, here, axis, n, bit, kind):
    mine = lax.dynamic_index_in_dim(w, here, dim, keepdims=False)
    other = lax.dynamic_index_in_dim(w, 1 - here, dim, keepdims=False)
    return mine + flip(other.astype(kind), axis, n, bit).astype(F32)


def halve_both(w, dim, losses, here, bit):
    mine = lax.dynamic_index_in_dim(w, here, dim, keepdims=False)
    other = lax.dynamic_index_in_dim(w, 1 - here, dim, keepdims=False)
    mine_l = lax.dynamic_index_in_dim(losses, here, 0, keepdims=False)
    other_l = lax.dynamic_index_in_dim(losses, 1 - here, 0, keepdims=False).reshape(-1)
    high = lax.reduce_precision(other_l, 8, 7)
    pair = jnp.concatenate([high, other_l - high]).astype(BF)
    wide, n = w.shape[-1], pair.shape[0]
    tail = jnp.pad(pair, (0, 16 * wide - n)).reshape(16, wide)
    got = flip(jnp.concatenate([other.astype(BF).reshape(-1, wide), tail]), "z", NZ, bit)
    got_w = got[:-16].reshape(other.shape).astype(F32)
    got_l = got[-16:].reshape(-1)[:n].astype(F32).reshape(2, *mine_l.shape)
    return mine + got_w, mine_l + got_l[0] + got_l[1]


def sum_weight(w, losses, beside):
    z, xl, y, core, rep = (lax.axis_index(a) for a in ("z", "xl", "y", "core", "rep"))
    w = w.reshape(2, 2, 2, NX, 2, 2, 24, D_EMB // 2)
    losses = losses.reshape(2, 2, 2, ROWS).transpose(2, 1, 0, 3)
    half = D_EMB // 4
    z_bits = z // 4, lax.rem(z // 2, 2), lax.rem(z, 2)
    a, b = w[..., :half], w[..., half:]
    a, losses = halve_both(a, 2, losses, z_bits[2], 1)
    b = halve(b, 3, xl, "xl", NX, 1, BF)
    a = halve(a, 2, xl, "xl", NX, 1, BF)
    b = halve(b, 2, z_bits[2], "z", NZ, 1, BF)
    w = jnp.concatenate([a, b], axis=-1)
    w, beside = lax.optimization_barrier((w, beside))
    w, losses = halve_both(w, 1, losses, z_bits[1], 2)
    w, losses = halve_both(w, 0, losses, z_bits[0], 4)
    w = halve(w, 0, y // 2, "y", NY, 2, F32)
    w = halve(w, 0, lax.rem(y, 2), "y", NY, 1, F32)
    w = halve(w.reshape(NC, NR, 6, D_EMB // 2), 1, rep, "rep", NR, 1, F32)
    own = lax.dynamic_index_in_dim(w, core, 0, keepdims=False)
    got = flip(lax.dynamic_index_in_dim(w, 1 - core, 0, keepdims=False), "core", NC)
    w = jnp.where(core == 0, jnp.concatenate([own, got], 1), jnp.concatenate([got, own], 1))
    return w, losses, beside


def in_order(losses, z):
    at = {o: losses[i * ROWS : (i + 1) * ROWS] for i, o in enumerate(Z_OFFSETS)}
    ring = [at[o if o < 5 else o - NZ] for o in range(NZ)]
    return lax.dynamic_slice_in_dim(jnp.stack(ring + ring), NZ - z, NZ, 0)


NN = (((1,), (0,)), ((), ()))
NT = (((1,), (1,)), ((), ()))
TN = (((0,), (0,)), ((), ()))


def dot(a, b, dims, precision=None):
    return lax.dot_general(a, b, dims, precision=precision, preferred_element_type=F32)


def reciprocal(x):
    return pltpu.reciprocal(x, approx=True)


def pair_terms(products, hit, scale, shift_value):
    signed = jnp.where(hit, -scale, scale)
    e = jnp.exp(products * signed + jnp.where(hit, -shift_value, shift_value))
    u = 1.0 + e
    coeffs = (e * reciprocal(u) * signed).astype(BF)
    w = e.shape[1] // 4
    e4 = [e[:, k * w : (k + 1) * w] for k in range(4)]
    p = e4[0] + e4[1] * u[:, :w]
    q = e4[2] + e4[3] * u[:, 2 * w : 3 * w]
    g = p + q * (1.0 + p)
    v = 1.0 + g
    losses = jnp.log(v) + (g - (v - 1.0)) * reciprocal(v)
    return coeffs, losses


def fold(x):
    total = x[:, :128]
    for k in range(1, x.shape[1] // 128):
        total = total + x[:, k * 128 : (k + 1) * 128]
    return total


def tile_kernel(scalars, numbers, *refs):
    images, (w_img, *texts) = refs[:9], refs[9:12]
    loss, t_mine, t_other, w_mine, w_other, image, back, low_all, coeffs = refs[12:]
    step = pl.program_id(0)
    scale, shift_value = scalars[0], scalars[1]

    @pl.when(step == 0)
    def _():
        at = 0
        for b in images:
            image[at : at + b.shape[0], :] = b[...]
            at += b.shape[0]

    rows = pl.ds(pl.multiple_of(step * STEP, STEP), STEP)
    codes = image[rows, D_IMG:].astype(F32)
    positive = (codes[:, 0:1] * 128.0 + codes[:, 1:2]).astype(jnp.int32)
    projected = dot(image[rows, :D_IMG], w_img[...], NN)
    inverse = lax.rsqrt(jnp.sum(projected * projected, axis=1, keepdims=True) + 1e-06)
    unit = projected * inverse
    low = unit.astype(BF)
    low_all[rows, :] = low
    lane = lax.broadcasted_iota(jnp.int32, (1, ROWS), 1)
    chunks = [slice(k * CHUNK, (k + 1) * CHUNK) for k in range(TEXTS // CHUNK)]
    text = [t[k : k + CHUNK, :] for t in texts for k in range(0, t.shape[0], CHUNK)]
    products = dot(low, text[0], NT)
    direction = total = None
    for k, at in enumerate(chunks):
        here = products
        if k + 1 < len(chunks):
            products = dot(low, text[k + 1], NT)
        per = CHUNK // ROWS
        columns = jnp.concatenate([numbers[k * per + j] + lane for j in range(per)], axis=1)
        c, losses = pair_terms(here, positive == columns, scale, shift_value)
        coeffs[rows, at] = c
        d = dot(c, text[k], NN)
        direction = d if direction is None else direction + d
        total = fold(losses) if total is None else total + fold(losses)
    loss[...] = dot(jnp.ones((8, 128), F32), total, NT, lax.Precision.HIGHEST)
    dots = jnp.sum(unit * direction, axis=1, keepdims=True)
    back[rows, :] = ((direction - unit * dots) * inverse).astype(BF)

    @pl.when(step == pl.num_programs(0) - 1)
    def _():
        core = numbers[NX * NY * NC]
        half = D_EMB // 2
        for ref, c in ((w_other, 1 - core), (w_mine, core)):
            right = back[:, pl.ds(pl.multiple_of(c * half, half), half)]
            for k in range(0, D_IMG, 512):
                ref[k : k + 512, :] = dot(image[:, k : k + 512], right, TN).astype(ref.dtype)
        for part, ref in ((1, t_other), (0, t_mine)):
            for k in range(0, TEXTS // 2, 512):
                left = coeffs[:, part * (TEXTS // 2) + k : part * (TEXTS // 2) + k + 512]
                ref[k : k + 512, :] = dot(left, low_all[...], TN).astype(ref.dtype)


def tile(scalars, numbers, images, w_img, texts):
    def whole(x):
        return pl.BlockSpec(x.shape, lambda i: (0,) * len(x.shape), pipeline_mode=pl.Buffered(1))

    smem = pl.BlockSpec(memory_space=pltpu.SMEM)
    out_shape = [
        jax.ShapeDtypeStruct((8, IMGS), F32),
        jax.ShapeDtypeStruct((TEXTS // 2, D_EMB), BF),
        jax.ShapeDtypeStruct((TEXTS // 2, D_EMB), BF),
        jax.ShapeDtypeStruct((D_IMG, D_EMB // 2), F32),
        jax.ShapeDtypeStruct((D_IMG, D_EMB // 2), BF),
    ]
    arrays = [*images, w_img, *texts]
    return pl.pallas_call(
        tile_kernel,
        grid=(IMGS // STEP,),
        in_specs=[smem, smem] + [whole(a) for a in arrays],
        out_specs=[
            pl.BlockSpec((8, STEP), lambda i: (0, i)),
            whole(out_shape[1]),
            whole(out_shape[2]),
            whole(out_shape[3]),
            whole(out_shape[4]),
        ],
        out_shape=out_shape,
        scratch_shapes=[
            pltpu.VMEM((IMGS, D_IMG + PAD), BF),
            pltpu.VMEM((IMGS, D_EMB), BF),
            pltpu.VMEM((IMGS, D_EMB), BF),
            pltpu.VMEM((IMGS, TEXTS), BF),
        ],
        compiler_params=pltpu.CompilerParams(vmem_limit_bytes=56 * 2**20),
        cost_estimate=pl.CostEstimate(
            flops=2 * IMGS * D_EMB * (3 * TEXTS + 2 * D_IMG),
            bytes_accessed=24 * 2**20,
            transcendentals=3 * IMGS * TEXTS,
        ),
    )(scalars, numbers, *arrays)


def shards(pooled, w_img, text_emb, pos_index, log_scale, bias):
    z, xl, y, core = (lax.axis_index(a) for a in ("z", "xl", "y", "core"))
    scalars = jnp.stack([jnp.exp(log_scale[0]), bias[0]])
    pos = pos_index[0]
    lane = lax.broadcasted_iota(jnp.int32, (ROWS, PAD), 1)
    codes = jnp.where(lane == 0, (pos // 128)[:, None], jnp.where(lane == 1, (pos % 128)[:, None], 0))
    own = jnp.concatenate([pooled[0], codes.astype(BF)], axis=1)

    raw = text_emb[0].astype(F32)
    text_inv = lax.rsqrt(jnp.sum(raw * raw, axis=-1, keepdims=True) + 1e-06)
    text_unit = raw * text_inv
    images, texts = gather(own, text_unit.astype(BF))

    plane = np.arange(NX * NY, dtype=np.int32)
    starts = lambda c: ((z * NX * NY + plane) * NC + c) * ROWS
    numbers = jnp.concatenate([starts(core), starts(1 - core), core[None]]).astype(jnp.int32)

    loss, t_mine, t_other, w_mine, w_other = tile(scalars, numbers, images, w_img, texts)
    t_sum = t_mine.astype(F32) + flip(t_other, "core", NC).astype(F32)
    w = w_mine + flip(w_other, "core", NC).astype(F32)
    blocks = exchange(t_sum.astype(BF).reshape(NX * NY, ROWS, D_EMB), ("xl", "y"))
    weight_sum, losses, blocks = sum_weight(w, in_order(loss[0], z), blocks)
    text_dir = jnp.sum(blocks.astype(F32), axis=0)
    weight_grad = weight_sum / 64.0
    text_grad = (
        text_dir - text_unit * jnp.sum(text_unit * text_dir, axis=-1, keepdims=True)
    ) * text_inv
    row_loss = losses / (NX * NY * NZ * NC * ROWS)
    return row_loss[None], weight_grad, text_grad[None]


def solution(mesh):
    names = ("z", "xl", "y", "core", "rep")
    fine = Mesh(mesh.devices.reshape(NZ, NX, NY, NC, NR), names)
    blk = names[:4]
    return jax.shard_map(
        shards,
        mesh=fine,
        in_specs=(P("rep", blk, None), P(), P("rep", blk, None), P("rep", blk), P(), P()),
        out_specs=(P("rep", blk), P(names, None), P("rep", blk, None)),
        check_vma=False,
    )
```

time: 805 us -> 196 us (0.24)
  waiting for transfers between devices: 539 us -> 87.9 us
  blocking collectives: 161 us -> 0 us
  matrix products: 77.3 us -> 0 us
  starting transfers between devices: 0.12 us -> 46.8 us
  Pallas kernels: 0 us -> 30.9 us
  between operations: 15.1 us -> 2.51 us
  other arithmetic: 8.64 us -> 19.9 us
    all_gather x2 -> x0, waiting for transfers between devices: 299 us -> none  [the longest x1 210 us: shards(): lax.all_gather(image_low, 'blk', axis=0, tiled=True)]
    unnamed x4 -> x0, waiting for transfers between devices: 240 us -> none
    all_gather x1 -> x0, blocking collectives: 161 us -> none  [shards(): lax.all_gather(my_pos, 'blk', axis=0, tiled=True)]
    ppermute x0 -> x21, waiting for transfers between devices: none -> 83 us  [the longest x13 56.1 us: flip(): return lax.ppermute(x, axis, [(i, i ^ bit) for i in range(n)])]
    dot_general x5 -> x0, matrix products: 77.3 us -> none  [the longest x2 38.3 us: transpose_dot(): lax.dot_general(coeffs, rows, (((0,), (0,)), ((), ())), preferred_element...]
    ppermute x0 -> x21, starting transfers between devices: none -> 37.9 us  [the longest x13 22.9 us: flip(): return lax.ppermute(x, axis, [(i, i ^ bit) for i in range(n)])]
    pallas_call x0 -> x1, Pallas kernels: none -> 30.9 us  [tile(): pl.pallas_call(tile_kernel, grid=(IMGS // STEP,), in_specs=[smem, smem] +...]
    all_to_all x0 -> x2, starting transfers between devices: none -> 8.85 us  [exchange(): return lax.all_to_all(x, axes, 0, 0)]
  transfers between devices with their start and end apart: 3 -> 23, of which waited for: 3 -> 14; matrix products, arithmetic and copies ran while one was open for 10% -> 10% of each run, Pallas kernels for 0% -> 0%
where the time goes in v1:
time: 196 us; the launch traced here: 195 us
  waiting for transfers between devices  87.9 us (45%)
  starting transfers between devices  46.8 us (24%)
  Pallas kernels  30.9 us (16%)
  other arithmetic  19.9 us (10%)
  local copies, waits for them, and re-layouts  7.49 us (4%)
  between operations  2.51 us (1%)
    ppermute x13, waiting for transfers between devices, flip(): return lax.ppermute(x, axis, [(i, i ^ bit) for i in range(n)])  56.1 us
    pallas_call x1, Pallas kernels, tile(): pl.pallas_call(tile_kernel, grid=(IMGS // STEP,), in_specs=[smem, smem] +...  30.9 us
    ppermute x8, waiting for transfers between devices, shift(): return lax.ppermute(x, axis, [(i, (i + by) % n) for i in range(n)])  26.9 us
    ppermute x13, starting transfers between devices, flip(): return lax.ppermute(x, axis, [(i, i ^ bit) for i in range(n)])  22.9 us
    ppermute x8, starting transfers between devices, shift(): return lax.ppermute(x, axis, [(i, (i + by) % n) for i in range(n)])  15.1 us
    all_to_all x2, starting transfers between devices, exchange(): return lax.all_to_all(x, axes, 0, 0)  8.85 us
    all_to_all x2, waiting for transfers between devices, exchange(): return lax.all_to_all(x, axes, 0, 0)  4.84 us
    convert_element_type x1, other arithmetic, shards(): t_sum.astype(BF).reshape(NX * NY, ROWS, D_EMB)  4.04 us
  transfers between devices with their start and end apart: 23, of which 14 were waited for; matrix products, arithmetic and copies ran while one was open for 10% of the time, Pallas kernels for 0%

profile of v1, /device:TPU:1, one launch (start us, length us, event | category | flops | bytes accessed | tf_op | source)
XLA Modules:
  0.0 195.5 jit_solution(12013557734243654975)
XLA Ops:
  0.6 0.7 and_select_fusion.1
  1.3 0.1 select_convert_fusion
  1.4 1.0 pad_maximum_fusion.1.refs_0_
  2.5 2.5 %collective-permute-start = (bf16[128,1664]{1,0:T(8,128)(2,1)S(1)}, bf16[128,1664]{1,0:T(8,128)(2,1)S(1)}, u32[]{:S(2)}, u32[]{:S(2)}) collective-permute-start(bf16[128,1664]{1,0:T(8,128)(2,1)S(1)} %pad_maximum_fusion.1.refs_0_), channel_id=1, source_target_pairs={{0,32},{32,64},{64,96},{96,128},{128,160},{160,192},{192,224},{224... | collective-permute-start | bytes 1277960 | tf_op jit(solution)/shard_map/ppermute | solution.py:25
  5.0 4.0 %collective-permute-start.1 = (bf16[128,1664]{1,0:T(8,128)(2,1)S(1)}, bf16[128,1664]{1,0:T(8,128)(2,1)S(1)}, u32[]{:S(2)}, u32[]{:S(2)}) collective-permute-start(bf16[128,1664]{1,0:T(8,128)(2,1)S(1)} %pad_maximum_fusion.1.refs_0_), channel_id=1, source_target_pairs={{0,224},{32,0},{64,32},{96,64},{128,96},{160,128},{192,160},{224,1... | collective-permute-start | bytes 1277960 | tf_op jit(solution)/shard_map/ppermute | solution.py:25
  9.0 1.1 fusion.6
  10.1 1.1 fusion.4
  11.2 7.3 %collective-permute-done.refs_1_ = bf16[128,1664]{1,0:T(8,128)(2,1)S(1)} collective-permute-done((bf16[128,1664]{1,0:T(8,128)(2,1)S(1)}, bf16[128,1664]{1,0:T(8,128)(2,1)S(1)}, u32[]{:S(2)}, u32[]{:S(2)}) %collective-permute-start) | collective-permute-done | bytes 426016 | tf_op jit(solution)/shard_map/ppermute | solution.py:25
  18.5 1.6 broadcast_in_dim.33
  20.1 5.1 %all-to-all-start = ((bf16[8,128,1024]{2,1,0:T(8,128)(2,1)}), bf16[8,128,1024]{2,1,0:T(8,128)(2,1)S(1)}, u32[]{:S(2)}, u32[]{:S(2)}) async-start(bf16[8,128,1024]{2,1,0:T(8,128)(2,1)} %broadcast_in_dim.33), calls=%async_computation | async-start | bytes 4194304 | tf_op jit(solution)/shard_map/all_to_all | solution.py:33
  25.3 2.7 %collective-permute-start.3 = (bf16[128,1664]{1,0:T(8,128)(2,1)S(1)}, bf16[128,1664]{1,0:T(8,128)(2,1)S(1)}, u32[]{:S(2)}, u32[]{:S(2)}) collective-permute-start(bf16[128,1664]{1,0:T(8,128)(2,1)S(1)} %collective-permute-done.1.refs_2_), channel_id=1, source_target_pairs={{0,224},{32,0},{64,32},{96,64},{128,96},{160,128},{192,160},{224,1... | collective-permute-start | bytes 1277960 | tf_op jit(solution)/shard_map/ppermute | solution.py:25
  28.0 8.3 %collective-permute-done.2.refs_3_ = bf16[128,1664]{1,0:T(8,128)(2,1)S(1)} collective-permute-done((bf16[128,1664]{1,0:T(8,128)(2,1)S(1)}, bf16[128,1664]{1,0:T(8,128)(2,1)S(1)}, u32[]{:S(2)}, u32[]{:S(2)}) %collective-permute-start.2) | collective-permute-done | bytes 426016 | tf_op jit(solution)/shard_map/ppermute | solution.py:25
  36.3 0.9 collective-permute-start.4
  37.2 1.8 collective-permute-start.5
  39.1 7.4 %collective-permute-done.4.refs_5_ = bf16[128,1664]{1,0:T(8,128)(2,1)S(1)} collective-permute-done((bf16[128,1664]{1,0:T(8,128)(2,1)S(1)}, bf16[128,1664]{1,0:T(8,128)(2,1)S(1)}, u32[]{:S(2)}, u32[]{:S(2)}) %collective-permute-start.4) | collective-permute-done | bytes 426016 | tf_op jit(solution)/shard_map/ppermute | solution.py:25
  46.5 4.8 %all-to-all-done = bf16[8,128,1024]{2,1,0:T(8,128)(2,1)S(1)} async-done(((bf16[8,128,1024]{2,1,0:T(8,128)(2,1)}), bf16[8,128,1024]{2,1,0:T(8,128)(2,1)S(1)}, u32[]{:S(2)}, u32[]{:S(2)}) %all-to-all-start) | async-done | bytes 2097184 | tf_op jit(solution)/shard_map/all_to_all | solution.py:33
  51.4 0.9 collective-permute-start.8
  53.7 2.9 %collective-permute-start.7 = (bf16[64,1664]{1,0:T(8,128)(2,1)S(1)}, bf16[64,1664]{1,0:T(8,128)(2,1)S(1)}, u32[]{:S(2)}, u32[]{:S(2)}) collective-permute-start(bf16[64,1664]{1,0:T(8,128)(2,1)S(1)} %slice.121), channel_id=1, source_target_pairs={{0,224},{32,0},{64,32},{96,64},{128,96},{160,128},{192,160},{224,1... | collective-permute-start | bytes 638984 | tf_op jit(solution)/shard_map/ppermute | solution.py:25
  56.6 0.6 pad_maximum_fusion.5.scalars
  57.2 0.6 pad_add_fusion.numbers
  57.9 3.9 %collective-permute-done.6.refs_7_ = bf16[64,1664]{1,0:T(8,128)(2,1)S(1)} collective-permute-done((bf16[64,1664]{1,0:T(8,128)(2,1)S(1)}, bf16[64,1664]{1,0:T(8,128)(2,1)S(1)}, u32[]{:S(2)}, u32[]{:S(2)}) %collective-permute-start.6) | collective-permute-done | bytes 213024 | tf_op jit(solution)/shard_map/ppermute | solution.py:25
  61.8 0.6 copy-done.18
  62.5 30.9 %shard_map.94 = (f32[8,1024]{1,0:T(8,128)}, bf16[1024,1024]{1,0:T(8,128)(2,1)}, bf16[1024,1024]{1,0:T(8,128)(2,1)}, f32[1536,512]{1,0:T(8,128)}, bf16[1536,512]{1,0:T(8,128)(2,1)}) custom-call(f32[2]{0:T(128)} %pad_maximum_fusion.5.scalars, s32[17]{0:T(128)} %pad_add_fusion.numbers, bf16[128,1664]{1,0:T(8,128)(2,1)} %copy-done.11, ...), custom_call_target="tpu_custom_call" | custom-call | flops 19327352832 | bytes 25165824 | tf_op jit(solution)/shard_map/pallas_call | solution.py:207
  93.5 0.9 collective-permute-start.9
  94.4 0.1 collective-permute-start.14
  94.5 0.8 fusion.34
  95.4 3.3 %collective-permute-done.9 = bf16[1536,512]{1,0:T(8,128)(2,1)S(1)} collective-permute-done((bf16[1536,512]{1,0:T(8,128)(2,1)}, bf16[1536,512]{1,0:T(8,128)(2,1)S(1)}, u32[]{:S(2)}, u32[]{:S(2)}) %collective-permute-start.9) | collective-permute-done | bytes 1572896 | tf_op jit(solution)/shard_map/ppermute | solution.py:29
  98.7 2.4 %convert_add_fusion = f32[1536,512]{1,0:T(8,128)S(1)} fusion(f32[1536,512]{1,0:T(8,128)} %get-tuple-element.27, bf16[1536,512]{1,0:T(8,128)(2,1)S(1)} %collective-permute-done.9), kind=kLoop, calls=%fused_computation.2 | loop fusion | flops 1572864 | bytes 7864320 | tf_op jit(solution)/shard_map/add | solution.py:253
  101.1 0.4 fusion.33
  101.5 0.9 fusion.10
  102.4 1.2 collective-permute-start.12
  103.7 0.8 pad_maximum_fusion.2
  104.4 1.7 collective-permute-start.10
  106.1 6.9 %collective-permute-done.12 = bf16[2,2,2,2,2,24,256]{6,5,4,3,1,0,2:T(8,128)(2,1)} collective-permute-done((bf16[2,2,2,2,2,24,256]{6,5,4,3,1,0,2:T(8,128)(2,1)}, bf16[2,2,2,2,2,24,256]{6,5,4,3,1,0,2:T(8,128)(2,1)}, u32[]{:S(2)}, u32[]{:S(2)}) %collective-permute-start.12) | collective-permute-done | bytes 393248 | tf_op jit(solution)/shard_map/ppermute | solution.py:29
  113.0 1.1 fusion
  114.2 0.8 fusion.12
  114.9 0.2 copy-done.2
  115.1 1.7 collective-permute-start.13
  116.8 4.0 %add_convert_fusion = bf16[1024,1024]{1,0:T(8,128)(2,1)} fusion(bf16[1024,1024]{1,0:T(8,128)(2,1)} %collective-permute-done.14, bf16[1024,1024]{1,0:T(8,128)(2,1)S(1)} %copy-done.7), kind=kLoop, calls=%fused_computation.1 | loop fusion | flops 4194304 | bytes 6291456 | tf_op jit(solution)/shard_map/convert_element_type | solution.py:254
  120.9 3.7 %all-to-all-start.1 = ((bf16[8,128,1024]{2,1,0:T(8,128)(2,1)}), bf16[8,128,1024]{2,1,0:T(8,128)(2,1)S(1)}, u32[]{:S(2)}, u32[]{:S(2)}) async-start(bf16[8,128,1024]{2,1,0:T(8,128)(2,1)} %bitcast.23), calls=%async_computation.1 | async-start | bytes 4194304 | tf_op jit(solution)/shard_map/all_to_all | solution.py:33
  124.6 1.3 convert_add_fusion.1
  126.0 0.9 copy-done.4
  126.9 1.4 collective-permute-start.11
  128.4 1.0 bitcast_add_fusion
  129.4 22.7 %collective-permute-done.11 = bf16[2,2,2,2,24,256]{5,4,3,2,1,0:T(8,128)(2,1)S(1)} collective-permute-done((bf16[2,2,2,2,24,256]{5,4,3,2,1,0:T(8,128)(2,1)S(1)}, bf16[2,2,2,2,24,256]{5,4,3,2,1,0:T(8,128)(2,1)S(1)}, u32[]{:S(2)}, u32[]{:S(2)}) %collective-permute-start.11) | collective-permute-done | bytes 196640 | tf_op jit(solution)/shard_map/ppermute | solution.py:29
  152.1 1.0 bitcast_add_fusion.1
  153.3 0.8 copy-done.5
  154.2 2.8 %collective-permute-start.15 = (bf16[208,512]{1,0:T(8,128)(2,1)S(1)}, bf16[208,512]{1,0:T(8,128)(2,1)S(1)}, u32[]{:S(2)}, u32[]{:S(2)}) collective-permute-start(bf16[208,512]{1,0:T(8,128)(2,1)S(1)} %pad_maximum_fusion.3), channel_id=1, source_target_pairs={{0,64},{32,96},{64,0},{96,32},{128,192},{160,224},{192,128},{224,1... | collective-permute-start | bytes 638984 | tf_op jit(solution)/shard_map/ppermute | solution.py:29
  157.0 0.3 convert_reduce_fusion
  157.3 9.5 %collective-permute-done.15 = bf16[208,512]{1,0:T(8,128)(2,1)S(1)} collective-permute-done((bf16[208,512]{1,0:T(8,128)(2,1)S(1)}, bf16[208,512]{1,0:T(8,128)(2,1)S(1)}, u32[]{:S(2)}, u32[]{:S(2)}) %collective-permute-start.15) | collective-permute-done | bytes 213024 | tf_op jit(solution)/shard_map/ppermute | solution.py:29
  167.1 1.3 collective-permute-start.16
  168.4 0.2 fusion.5
  168.6 8.6 %collective-permute-done.16 = bf16[112,512]{1,0:T(8,128)(2,1)S(1)} collective-permute-done((bf16[112,512]{1,0:T(8,128)(2,1)S(1)}, bf16[112,512]{1,0:T(8,128)(2,1)S(1)}, u32[]{:S(2)}, u32[]{:S(2)}) %collective-permute-start.16) | collective-permute-done | bytes 114720 | tf_op jit(solution)/shard_map/ppermute | solution.py:29
  177.3 2.8 %collective-permute-start.17 = (f32[2,24,512]{2,1,0:T(8,128)S(1)}, f32[2,24,512]{2,1,0:T(8,128)S(1)}, u32[]{:S(2)}, u32[]{:S(2)}) collective-permute-start(f32[2,24,512]{2,1,0:T(8,128)S(1)} %dynamic-slice_bitcast_fusion), channel_id=1, source_target_pairs={{0,8},{4,12},{8,0},{12,4},{1,9},{5,13},{9,1},{13,5},{2,10},{6,14},... | collective-permute-start | bytes 294920 | tf_op jit(solution)/shard_map/ppermute | solution.py:29
  180.1 1.0 fusion.9
  181.1 1.2 collective-permute-done.17
  182.4 1.3 collective-permute-start.18
  183.7 1.7 collective-permute-done.18
  185.5 2.5 %collective-permute-start.19 = (f32[2,6,512]{2,1,0:T(8,128)S(1)}, f32[2,6,512]{2,1,0:T(8,128)S(1)}, u32[]{:S(2)}, u32[]{:S(2)}) collective-permute-start(f32[2,6,512]{2,1,0:T(8,128)S(1)} %dynamic-slice_bitcast_fusion.2), channel_id=1, source_target_pairs={{0,1},{1,0},{2,3},{3,2},{4,5},{5,4},{6,7},{7,6},{8,9},{9,8},{10,11... | collective-permute-start | bytes 73736 | tf_op jit(solution)/shard_map/ppermute | solution.py:29
  188.0 1.8 collective-permute-done.19
  189.8 4.2 %collective-permute-start.20 = (f32[6,512]{1,0:T(8,128)S(1)}, f32[6,512]{1,0:T(8,128)S(1)}, u32[]{:S(2)}, u32[]{:S(2)}) collective-permute-start(f32[6,512]{1,0:T(8,128)S(1)} %get-tuple-element.36), channel_id=1, source_target_pairs={{0,2},{2,0},{1,3},{3,1},{4,6},{6,4},{5,7},{7,5},{8,10},{10,8},{9,1... | collective-permute-start | bytes 36872 | tf_op jit(solution)/shard_map/ppermute | solution.py:29
  194.0 0.5 fusion.32
  194.5 0.3 collective-permute-done.20
  194.9 0.6 fusion.17
  (95 shorter events, 1.1 us)
Async XLA Ops:
  2.4 17.7 %copy-start.11 = (bf16[128,1664]{1,0:T(8,128)(2,1)}, bf16[128,1664]{1,0:T(8,128)(2,1)S(1)}, u32[]{:S(2)}) copy-start(bf16[128,1664]{1,0:T(8,128)(2,1)S(1)} %pad_maximum_fusion.1.refs_0_) | copy-start | bytes 1277956
  2.5 16.0 %collective-permute-start = (bf16[128,1664]{1,0:T(8,128)(2,1)S(1)}, bf16[128,1664]{1,0:T(8,128)(2,1)S(1)}, u32[]{:S(2)}, u32[]{:S(2)}) collective-permute-start(bf16[128,1664]{1,0:T(8,128)(2,1)S(1)} %pad_maximum_fusion.1.refs_0_), channel_id=1, source_target_pairs={{0,32},{32,64},{64,96},{96,128},{128,160},{160,192},{192,224},{224... | collective-permute-start | bytes 1277960 | tf_op jit(solution)/shard_map/ppermute | solution.py:25
  5.0 13.5 %collective-permute-start.1 = (bf16[128,1664]{1,0:T(8,128)(2,1)S(1)}, bf16[128,1664]{1,0:T(8,128)(2,1)S(1)}, u32[]{:S(2)}, u32[]{:S(2)}) collective-permute-start(bf16[128,1664]{1,0:T(8,128)(2,1)S(1)} %pad_maximum_fusion.1.refs_0_), channel_id=1, source_target_pairs={{0,224},{32,0},{64,32},{96,64},{128,96},{160,128},{192,160},{224,1... | collective-permute-start | bytes 1277960 | tf_op jit(solution)/shard_map/ppermute | solution.py:25
  18.5 6.7 %copy-start.14 = (bf16[128,1664]{1,0:T(8,128)(2,1)}, bf16[128,1664]{1,0:T(8,128)(2,1)S(1)}, u32[]{:S(2)}) copy-start(bf16[128,1664]{1,0:T(8,128)(2,1)S(1)} %collective-permute-done.refs_1_) | copy-start | bytes 1277956
  18.5 6.8 %copy-start.15 = (bf16[128,1664]{1,0:T(8,128)(2,1)}, bf16[128,1664]{1,0:T(8,128)(2,1)S(1)}, u32[]{:S(2)}) copy-start(bf16[128,1664]{1,0:T(8,128)(2,1)S(1)} %collective-permute-done.1.refs_2_) | copy-start | bytes 1277956
  20.1 31.3 %all-to-all-start = ((bf16[8,128,1024]{2,1,0:T(8,128)(2,1)}), bf16[8,128,1024]{2,1,0:T(8,128)(2,1)S(1)}, u32[]{:S(2)}, u32[]{:S(2)}) async-start(bf16[8,128,1024]{2,1,0:T(8,128)(2,1)} %broadcast_in_dim.33), calls=%async_computation | async-start | bytes 4194304 | tf_op jit(solution)/shard_map/all_to_all | solution.py:33
  25.2 11.1 %collective-permute-start.2 = (bf16[128,1664]{1,0:T(8,128)(2,1)S(1)}, bf16[128,1664]{1,0:T(8,128)(2,1)S(1)}, u32[]{:S(2)}, u32[]{:S(2)}) collective-permute-start(bf16[128,1664]{1,0:T(8,128)(2,1)S(1)} %collective-permute-done.refs_1_), channel_id=1, source_target_pairs={{0,32},{32,64},{64,96},{96,128},{128,160},{160,192},{192,224},{224... | collective-permute-start | bytes 1277960 | tf_op jit(solution)/shard_map/ppermute | solution.py:25
  25.3 11.0 %collective-permute-start.3 = (bf16[128,1664]{1,0:T(8,128)(2,1)S(1)}, bf16[128,1664]{1,0:T(8,128)(2,1)S(1)}, u32[]{:S(2)}, u32[]{:S(2)}) collective-permute-start(bf16[128,1664]{1,0:T(8,128)(2,1)S(1)} %collective-permute-done.1.refs_2_), channel_id=1, source_target_pairs={{0,224},{32,0},{64,32},{96,64},{128,96},{160,128},{192,160},{224,1... | collective-permute-start | bytes 1277960 | tf_op jit(solution)/shard_map/ppermute | solution.py:25
  36.3 10.2 %copy-start.16 = (bf16[128,1664]{1,0:T(8,128)(2,1)}, bf16[128,1664]{1,0:T(8,128)(2,1)S(1)}, u32[]{:S(2)}) copy-start(bf16[128,1664]{1,0:T(8,128)(2,1)S(1)} %collective-permute-done.2.refs_3_) | copy-start | bytes 1277956
  36.3 10.2 %copy-start.17 = (bf16[128,1664]{1,0:T(8,128)(2,1)}, bf16[128,1664]{1,0:T(8,128)(2,1)S(1)}, u32[]{:S(2)}) copy-start(bf16[128,1664]{1,0:T(8,128)(2,1)S(1)} %collective-permute-done.3.refs_4_) | copy-start | bytes 1277956
  36.3 10.2 %collective-permute-start.4 = (bf16[128,1664]{1,0:T(8,128)(2,1)S(1)}, bf16[128,1664]{1,0:T(8,128)(2,1)S(1)}, u32[]{:S(2)}, u32[]{:S(2)}) collective-permute-start(bf16[128,1664]{1,0:T(8,128)(2,1)S(1)} %collective-permute-done.2.refs_3_), channel_id=1, source_target_pairs={{0,32},{32,64},{64,96},{96,128},{128,160},{160,192},{192,224},{224... | collective-permute-start | bytes 1277960 | tf_op jit(solution)/shard_map/ppermute | solution.py:25
  37.2 9.3 %collective-permute-start.5 = (bf16[128,1664]{1,0:T(8,128)(2,1)S(1)}, bf16[128,1664]{1,0:T(8,128)(2,1)S(1)}, u32[]{:S(2)}, u32[]{:S(2)}) collective-permute-start(bf16[128,1664]{1,0:T(8,128)(2,1)S(1)} %collective-permute-done.3.refs_4_), channel_id=1, source_target_pairs={{0,224},{32,0},{64,32},{96,64},{128,96},{160,128},{192,160},{224,1... | collective-permute-start | bytes 1277960 | tf_op jit(solution)/shard_map/ppermute | solution.py:25
  46.5 15.3 %copy-start.12 = (bf16[128,1664]{1,0:T(8,128)(2,1)}, bf16[128,1664]{1,0:T(8,128)(2,1)S(1)}, u32[]{:S(2)}) copy-start(bf16[128,1664]{1,0:T(8,128)(2,1)S(1)} %collective-permute-done.4.refs_5_) | copy-start | bytes 1277956
  46.5 15.3 %copy-start.13 = (bf16[128,1664]{1,0:T(8,128)(2,1)}, bf16[128,1664]{1,0:T(8,128)(2,1)S(1)}, u32[]{:S(2)}) copy-start(bf16[128,1664]{1,0:T(8,128)(2,1)S(1)} %collective-permute-done.5.refs_6_) | copy-start | bytes 1277956
  51.4 10.4 %copy-start.8 = (bf16[8,128,1024]{2,1,0:T(8,128)(2,1)}, bf16[8,128,1024]{2,1,0:T(8,128)(2,1)S(1)}, u32[]{:S(2)}) copy-start(bf16[8,128,1024]{2,1,0:T(8,128)(2,1)S(1)} %all-to-all-done) | copy-start | bytes 6291460
  51.4 10.4 %collective-permute-start.8 = (bf16[1024,1024]{1,0:T(8,128)(2,1)S(1)}, bf16[1024,1024]{1,0:T(8,128)(2,1)}, u32[]{:S(2)}, u32[]{:S(2)}) collective-permute-start(bf16[1024,1024]{1,0:T(8,128)(2,1)S(1)} %bitcast.120), channel_id=1, source_target_pairs={{0,2},{2,0},{1,3},{3,1},{4,6},{6,4},{5,7},{7,5},{8,10},{10,8},{9,1... | collective-permute-start | bytes 6291464 | tf_op jit(solution)/shard_map/ppermute | solution.py:29
  53.6 8.2 %collective-permute-start.6 = (bf16[64,1664]{1,0:T(8,128)(2,1)S(1)}, bf16[64,1664]{1,0:T(8,128)(2,1)S(1)}, u32[]{:S(2)}, u32[]{:S(2)}) collective-permute-start(bf16[64,1664]{1,0:T(8,128)(2,1)S(1)} %slice.120), channel_id=1, source_target_pairs={{0,32},{32,64},{64,96},{96,128},{128,160},{160,192},{192,224},{224... | collective-permute-start | bytes 638984 | tf_op jit(solution)/shard_map/ppermute | solution.py:25
  53.7 8.0 %collective-permute-start.7 = (bf16[64,1664]{1,0:T(8,128)(2,1)S(1)}, bf16[64,1664]{1,0:T(8,128)(2,1)S(1)}, u32[]{:S(2)}, u32[]{:S(2)}) collective-permute-start(bf16[64,1664]{1,0:T(8,128)(2,1)S(1)} %slice.121), channel_id=1, source_target_pairs={{0,224},{32,0},{64,32},{96,64},{128,96},{160,128},{192,160},{224,1... | collective-permute-start | bytes 638984 | tf_op jit(solution)/shard_map/ppermute | solution.py:25
  61.7 0.7 copy-start.18
  61.8 0.8 copy-start.19
  93.5 5.2 %collective-permute-start.9 = (bf16[1536,512]{1,0:T(8,128)(2,1)}, bf16[1536,512]{1,0:T(8,128)(2,1)S(1)}, u32[]{:S(2)}, u32[]{:S(2)}) collective-permute-start(bf16[1536,512]{1,0:T(8,128)(2,1)} %get-tuple-element.28), channel_id=1, source_target_pairs={{0,2},{2,0},{1,3},{3,1},{4,6},{6,4},{5,7},{7,5},{8,10},{10,8},{9,1... | collective-permute-start | bytes 4718600 | tf_op jit(solution)/shard_map/ppermute | solution.py:29
  94.4 22.4 %collective-permute-start.14 = (bf16[1024,1024]{1,0:T(8,128)(2,1)}, bf16[1024,1024]{1,0:T(8,128)(2,1)}, u32[]{:S(2)}, u32[]{:S(2)}) collective-permute-start(bf16[1024,1024]{1,0:T(8,128)(2,1)} %get-tuple-element.30), channel_id=1, source_target_pairs={{0,2},{2,0},{1,3},{3,1},{4,6},{6,4},{5,7},{7,5},{8,10},{10,8},{9,1... | collective-permute-start | bytes 6291464 | tf_op jit(solution)/shard_map/ppermute | solution.py:29
  101.5 12.6 %copy-start = (f32[2,2,2,2,2,2,24,256]{7,6,5,4,3,2,1,0:T(8,128)}, f32[2,2,2,2,2,2,24,256]{7,6,5,4,3,2,1,0:T(8,128)S(1)}, u32[]{:S(2)}) copy-start(f32[2,2,2,2,2,2,24,256]{7,6,5,4,3,2,1,0:T(8,128)S(1)} %get-tuple-element.34) | copy-start | bytes 4718596
  102.4 10.6 %collective-permute-start.12 = (bf16[2,2,2,2,2,24,256]{6,5,4,3,1,0,2:T(8,128)(2,1)}, bf16[2,2,2,2,2,24,256]{6,5,4,3,1,0,2:T(8,128)(2,1)}, u32[]{:S(2)}, u32[]{:S(2)}) collective-permute-start(bf16[2,2,2,2,2,24,256]{6,5,4,3,1,0,2:T(8,128)(2,1)} %fusion.10), channel_id=1, source_target_pairs={{0,16},{16,0},{1,17},{17,1},{2,18},{18,2},{3,19},{19,3},{4,20},{20... | collective-permute-start | bytes 1179656 | tf_op jit(solution)/shard_map/ppermute | solution.py:29
  104.4 12.4 %collective-permute-start.10 = (bf16[784,256]{1,0:T(8,128)(2,1)}, bf16[784,256]{1,0:T(8,128)(2,1)S(1)}, u32[]{:S(2)}, u32[]{:S(2)}) collective-permute-start(bf16[784,256]{1,0:T(8,128)(2,1)} %pad_maximum_fusion.2), channel_id=1, source_target_pairs={{0,32},{32,0},{64,96},{96,64},{128,160},{160,128},{192,224},{224,1... | collective-permute-start | bytes 1204232 | tf_op jit(solution)/shard_map/ppermute | solution.py:29
  106.1 10.7 %copy-start.7 = (bf16[1024,1024]{1,0:T(8,128)(2,1)S(1)}, bf16[1024,1024]{1,0:T(8,128)(2,1)}, u32[]{:S(2)}) copy-start(bf16[1024,1024]{1,0:T(8,128)(2,1)} %get-tuple-element.29) | copy-start | bytes 6291460
  114.2 0.9 copy-start.2
  115.1 13.3 %collective-permute-start.13 = (bf16[2,2,2,2,24,256]{5,4,3,2,1,0:T(8,128)(2,1)}, bf16[2,2,2,2,24,256]{5,4,3,2,1,0:T(8,128)(2,1)}, u32[]{:S(2)}, u32[]{:S(2)}) collective-permute-start(bf16[2,2,2,2,24,256]{5,4,3,2,1,0:T(8,128)(2,1)} %fusion.12), channel_id=1, source_target_pairs={{0,32},{32,0},{64,96},{96,64},{128,160},{160,128},{192,224},{224,1... | collective-permute-start | bytes 589832 | tf_op jit(solution)/shard_map/ppermute | solution.py:29
  116.8 4.1 %copy-start.9 = (bf16[784,256]{1,0:T(8,128)(2,1)}, bf16[784,256]{1,0:T(8,128)(2,1)S(1)}, u32[]{:S(2)}) copy-start(bf16[784,256]{1,0:T(8,128)(2,1)S(1)} %collective-permute-done.10) | copy-start | bytes 1204228
  120.9 3.8 %slice-start = ((bf16[784,256]{1,0:T(8,128)(2,1)}), bf16[768,256]{1,0:T(8,128)(2,1)S(1)}, s32[]{:S(2)}) async-start(bf16[784,256]{1,0:T(8,128)(2,1)} %copy-done.9), calls=%async_computation.2 | async-start | bytes 786432 | tf_op jit(solution)/shard_map/slice | solution.py:69
  120.9 32.4 %all-to-all-start.1 = ((bf16[8,128,1024]{2,1,0:T(8,128)(2,1)}), bf16[8,128,1024]{2,1,0:T(8,128)(2,1)S(1)}, u32[]{:S(2)}, u32[]{:S(2)}) async-start(bf16[8,128,1024]{2,1,0:T(8,128)(2,1)} %bitcast.23), calls=%async_computation.1 | async-start | bytes 4194304 | tf_op jit(solution)/shard_map/all_to_all | solution.py:33
  124.6 3.7 %copy-start.10 = (bf16[784,256]{1,0:T(8,128)(2,1)S(1)}, bf16[784,256]{1,0:T(8,128)(2,1)}, u32[]{:S(2)}) copy-start(bf16[784,256]{1,0:T(8,128)(2,1)} %copy-done.9) | copy-start | bytes 1204228
  124.6 3.8 %copy-start.3 = (f32[2,2,2,2,2,24,256]{6,5,4,3,1,0,2:T(8,128)S(1)}, f32[2,2,2,2,2,24,256]{6,5,4,3,1,0,2:T(8,128)}, u32[]{:S(2)}) copy-start(f32[2,2,2,2,2,24,256]{6,5,4,3,1,0,2:T(8,128)} %copy-done.2) | copy-start | bytes 2359300
  126.0 0.9 copy-start.4
  126.9 25.2 %collective-permute-start.11 = (bf16[2,2,2,2,24,256]{5,4,3,2,1,0:T(8,128)(2,1)S(1)}, bf16[2,2,2,2,24,256]{5,4,3,2,1,0:T(8,128)(2,1)S(1)}, u32[]{:S(2)}, u32[]{:S(2)}) collective-permute-start(bf16[2,2,2,2,24,256]{5,4,3,2,1,0:T(8,128)(2,1)S(1)} %fusion.11), channel_id=1, source_target_pairs={{0,16},{16,0},{1,17},{17,1},{2,18},{18,2},{3,19},{19,3},{4,20},{20... | collective-permute-start | bytes 589832 | tf_op jit(solution)/shard_map/ppermute | solution.py:29
  153.3 0.9 copy-start.5
  154.2 12.7 %copy-start.6 = (f32[2,2,2,2,24,512]{5,4,3,2,1,0:T(8,128)S(1)}, f32[2,2,2,2,24,512]{5,4,3,2,1,0:T(8,128)}, u32[]{:S(2)}) copy-start(f32[2,2,2,2,24,512]{5,4,3,2,1,0:T(8,128)} %copy-done.5) | copy-start | bytes 2359300
  154.2 14.2 %copy-start.1 = (bf16[1,128,1024]{2,1,0:T(8,128)(2,1)S(1)}, bf16[1,128,1024]{2,1,0:T(8,128)(2,1)}, u32[]{:S(2)}) copy-start(bf16[1,128,1024]{2,1,0:T(8,128)(2,1)} %param.9) | copy-start | bytes 786436
  154.2 12.7 %collective-permute-start.15 = (bf16[208,512]{1,0:T(8,128)(2,1)S(1)}, bf16[208,512]{1,0:T(8,128)(2,1)S(1)}, u32[]{:S(2)}, u32[]{:S(2)}) collective-permute-start(bf16[208,512]{1,0:T(8,128)(2,1)S(1)} %pad_maximum_fusion.3), channel_id=1, source_target_pairs={{0,64},{32,96},{64,0},{96,32},{128,192},{160,224},{192,128},{224,1... | collective-permute-start | bytes 638984 | tf_op jit(solution)/shard_map/ppermute | solution.py:29
  167.1 10.1 %collective-permute-start.16 = (bf16[112,512]{1,0:T(8,128)(2,1)S(1)}, bf16[112,512]{1,0:T(8,128)(2,1)S(1)}, u32[]{:S(2)}, u32[]{:S(2)}) collective-permute-start(bf16[112,512]{1,0:T(8,128)(2,1)S(1)} %pad_maximum_fusion.4), channel_id=1, source_target_pairs={{0,128},{32,160},{64,192},{96,224},{128,0},{160,32},{192,64},{224,... | collective-permute-start | bytes 344072 | tf_op jit(solution)/shard_map/ppermute | solution.py:29
  177.3 5.1 %collective-permute-start.17 = (f32[2,24,512]{2,1,0:T(8,128)S(1)}, f32[2,24,512]{2,1,0:T(8,128)S(1)}, u32[]{:S(2)}, u32[]{:S(2)}) collective-permute-start(f32[2,24,512]{2,1,0:T(8,128)S(1)} %dynamic-slice_bitcast_fusion), channel_id=1, source_target_pairs={{0,8},{4,12},{8,0},{12,4},{1,9},{5,13},{9,1},{13,5},{2,10},{6,14},... | collective-permute-start | bytes 294920 | tf_op jit(solution)/shard_map/ppermute | solution.py:29
  182.4 3.0 %collective-permute-start.18 = (f32[24,512]{1,0:T(8,128)S(1)}, f32[24,512]{1,0:T(8,128)S(1)}, u32[]{:S(2)}, u32[]{:S(2)}) collective-permute-start(f32[24,512]{1,0:T(8,128)S(1)} %dynamic-slice_bitcast_fusion.1), channel_id=1, source_target_pairs={{0,4},{4,0},{8,12},{12,8},{1,5},{5,1},{9,13},{13,9},{2,6},{6,2},{1... | collective-permute-start | bytes 147464 | tf_op jit(solution)/shard_map/ppermute | solution.py:29
  185.5 4.4 %collective-permute-start.19 = (f32[2,6,512]{2,1,0:T(8,128)S(1)}, f32[2,6,512]{2,1,0:T(8,128)S(1)}, u32[]{:S(2)}, u32[]{:S(2)}) collective-permute-start(f32[2,6,512]{2,1,0:T(8,128)S(1)} %dynamic-slice_bitcast_fusion.2), channel_id=1, source_target_pairs={{0,1},{1,0},{2,3},{3,2},{4,5},{5,4},{6,7},{7,6},{8,9},{9,8},{10,11... | collective-permute-start | bytes 73736 | tf_op jit(solution)/shard_map/ppermute | solution.py:29
  189.8 5.0 %collective-permute-start.20 = (f32[6,512]{1,0:T(8,128)S(1)}, f32[6,512]{1,0:T(8,128)S(1)}, u32[]{:S(2)}, u32[]{:S(2)}) collective-permute-start(f32[6,512]{1,0:T(8,128)S(1)} %get-tuple-element.36), channel_id=1, source_target_pairs={{0,2},{2,0},{1,3},{3,1},{4,6},{6,4},{5,7},{7,5},{8,10},{10,8},{9,1... | collective-permute-start | bytes 36872 | tf_op jit(solution)/shard_map/ppermute | solution.py:29

commit v2 on v1

--- a/solution.py
+++ b/solution.py
@@ -1,3 +1,5 @@
+import functools
+
 import jax
 import jax.numpy as jnp
 import numpy as np
@@ -56,43 +58,45 @@
     return mine + flip(other.astype(kind), axis, n, bit).astype(F32)
 
 
-def halve_both(w, dim, losses, here, bit):
+def halve_both(w, dim, losses, here, bit, kind):
     mine = lax.dynamic_index_in_dim(w, here, dim, keepdims=False)
     other = lax.dynamic_index_in_dim(w, 1 - here, dim, keepdims=False)
     mine_l = lax.dynamic_index_in_dim(losses, here, 0, keepdims=False)
     other_l = lax.dynamic_index_in_dim(losses, 1 - here, 0, keepdims=False).reshape(-1)
-    high = lax.reduce_precision(other_l, 8, 7)
-    pair = jnp.concatenate([high, other_l - high]).astype(BF)
-    wide, n = w.shape[-1], pair.shape[0]
-    tail = jnp.pad(pair, (0, 16 * wide - n)).reshape(16, wide)
-    got = flip(jnp.concatenate([other.astype(BF).reshape(-1, wide), tail]), "z", NZ, bit)
+    if kind == BF:
+        high = lax.reduce_precision(other_l, 8, 7)
+        other_l = jnp.concatenate([high, other_l - high]).astype(BF)
+    wide, n = w.shape[-1], other_l.shape[0]
+    tail = jnp.pad(other_l, (0, 16 * wide - n)).reshape(16, wide)
+    got = flip(jnp.concatenate([other.astype(kind).reshape(-1, wide), tail]), "z", NZ, bit)
     got_w = got[:-16].reshape(other.shape).astype(F32)
-    got_l = got[-16:].reshape(-1)[:n].astype(F32).reshape(2, *mine_l.shape)
-    return mine + got_w, mine_l + got_l[0] + got_l[1]
-
-
-def sum_weight(w, losses, beside):
+    got_l = got[-16:].reshape(-1)[:n].astype(F32).reshape(-1, *mine_l.shape)
+    return mine + got_w, mine_l + jnp.sum(got_l, axis=0)
+
+
+def sum_weight(w, losses, blocks):
     z, xl, y, core, rep = (lax.axis_index(a) for a in ("z", "xl", "y", "core", "rep"))
     w = w.reshape(2, 2, 2, NX, 2, 2, 24, D_EMB // 2)
     losses = losses.reshape(2, 2, 2, ROWS).transpose(2, 1, 0, 3)
     half = D_EMB // 4
     z_bits = z // 4, lax.rem(z // 2, 2), lax.rem(z, 2)
     a, b = w[..., :half], w[..., half:]
-    a, losses = halve_both(a, 2, losses, z_bits[2], 1)
-    b = halve(b, 3, xl, "xl", NX, 1, BF)
-    a = halve(a, 2, xl, "xl", NX, 1, BF)
+    a, losses = halve_both(a, 2, losses, z_bits[2], 1, BF)
+    b = halve(b, 4, y // 2, "y", NY, 2, BF)
+    a = halve(a, 3, y // 2, "y", NY, 2, BF)
     b = halve(b, 2, z_bits[2], "z", NZ, 1, BF)
     w = jnp.concatenate([a, b], axis=-1)
-    w, beside = lax.optimization_barrier((w, beside))
-    w, losses = halve_both(w, 1, losses, z_bits[1], 2)
-    w, losses = halve_both(w, 0, losses, z_bits[0], 4)
-    w = halve(w, 0, y // 2, "y", NY, 2, F32)
-    w = halve(w, 0, lax.rem(y, 2), "y", NY, 1, F32)
-    w = halve(w.reshape(NC, NR, 6, D_EMB // 2), 1, rep, "rep", NR, 1, F32)
+    blocks = exchange(blocks, ("xl", "y"))
+    w = halve(w, 3, lax.rem(y, 2), "y", NY, 1, BF)
+    w = halve(w, 2, xl, "xl", NX, 1, BF)
+    w = halve(w.reshape(2, 2, NC, NR, 6, D_EMB // 2), 3, rep, "rep", NR, 1, F32)
+    w, losses = halve_both(w, 1, losses, z_bits[1], 2, F32)
+    w, losses = halve_both(w, 0, losses, z_bits[0], 4, F32)
+    w, blocks = lax.optimization_barrier((w, blocks))
     own = lax.dynamic_index_in_dim(w, core, 0, keepdims=False)
     got = flip(lax.dynamic_index_in_dim(w, 1 - core, 0, keepdims=False), "core", NC)
     w = jnp.where(core == 0, jnp.concatenate([own, got], 1), jnp.concatenate([got, own], 1))
-    return w, losses, beside
+    return w, losses, blocks
 
 
 def in_order(losses, z):
@@ -136,9 +140,13 @@
     return total
 
 
-def tile_kernel(scalars, numbers, *refs):
-    images, (w_img, *texts) = refs[:9], refs[9:12]
-    loss, t_mine, t_other, w_mine, w_other, image, back, low_all, coeffs = refs[12:]
+def tile_kernel(n_images, weigh, scalars, numbers, *refs):
+    images, (w_img, *texts) = refs[:n_images], refs[n_images : n_images + 3]
+    refs = refs[n_images + 3 :]
+    if weigh:
+        early, (early_back, loss, coeffs, low_out, w_mine, w_other, image, back) = refs[:4], refs[4:]
+    else:
+        loss, coeffs, low_out, back_out, image = refs
     step = pl.program_id(0)
     scale, shift_value = scalars[0], scalars[1]
 
@@ -156,7 +164,7 @@
     inverse = lax.rsqrt(jnp.sum(projected * projected, axis=1, keepdims=True) + 1e-06)
     unit = projected * inverse
     low = unit.astype(BF)
-    low_all[rows, :] = low
+    low_out[...] = low
     lane = lax.broadcasted_iota(jnp.int32, (1, ROWS), 1)
     chunks = [slice(k * CHUNK, (k + 1) * CHUNK) for k in range(TEXTS // CHUNK)]
     text = [t[k : k + CHUNK, :] for t in texts for k in range(0, t.shape[0], CHUNK)]
@@ -169,66 +177,106 @@
         per = CHUNK // ROWS
         columns = jnp.concatenate([numbers[k * per + j] + lane for j in range(per)], axis=1)
         c, losses = pair_terms(here, positive == columns, scale, shift_value)
-        coeffs[rows, at] = c
+        coeffs[:, at] = c
         d = dot(c, text[k], NN)
         direction = d if direction is None else direction + d
         total = fold(losses) if total is None else total + fold(losses)
     loss[...] = dot(jnp.ones((8, 128), F32), total, NT, lax.Precision.HIGHEST)
     dots = jnp.sum(unit * direction, axis=1, keepdims=True)
-    back[rows, :] = ((direction - unit * dots) * inverse).astype(BF)
+    result = ((direction - unit * dots) * inverse).astype(BF)
+    if not weigh:
+        back_out[...] = result
+        return
+    back[rows, :] = result
 
     @pl.when(step == pl.num_programs(0) - 1)
     def _():
         core = numbers[NX * NY * NC]
         half = D_EMB // 2
         for ref, c in ((w_other, 1 - core), (w_mine, core)):
-            right = back[:, pl.ds(pl.multiple_of(c * half, half), half)]
+            columns = pl.ds(pl.multiple_of(c * half, half), half)
+            right, early_right = back[:, columns], early_back[:, columns]
             for k in range(0, D_IMG, 512):
-                ref[k : k + 512, :] = dot(image[:, k : k + 512], right, TN).astype(ref.dtype)
-        for part, ref in ((1, t_other), (0, t_mine)):
-            for k in range(0, TEXTS // 2, 512):
-                left = coeffs[:, part * (TEXTS // 2) + k : part * (TEXTS // 2) + k + 512]
-                ref[k : k + 512, :] = dot(left, low_all[...], TN).astype(ref.dtype)
-
-
-def tile(scalars, numbers, images, w_img, texts):
+                left = jnp.concatenate([e[:, k : k + 512] for e in early])
+                w = dot(image[:, k : k + 512], right, TN) + dot(left, early_right, TN)
+                ref[k : k + 512, :] = w.astype(ref.dtype)
+
+
+def tile(scalars, numbers, images, w_img, texts, early=None):
     def whole(x):
         return pl.BlockSpec(x.shape, lambda i: (0,) * len(x.shape), pipeline_mode=pl.Buffered(1))
 
+    rows = lambda n: pl.BlockSpec((STEP, n), lambda i: (i, 0))
     smem = pl.BlockSpec(memory_space=pltpu.SMEM)
+    half = IMGS // 2
     out_shape = [
-        jax.ShapeDtypeStruct((8, IMGS), F32),
-        jax.ShapeDtypeStruct((TEXTS // 2, D_EMB), BF),
-        jax.ShapeDtypeStruct((TEXTS // 2, D_EMB), BF),
-        jax.ShapeDtypeStruct((D_IMG, D_EMB // 2), F32),
-        jax.ShapeDtypeStruct((D_IMG, D_EMB // 2), BF),
+        jax.ShapeDtypeStruct((8, half), F32),
+        jax.ShapeDtypeStruct((half, TEXTS), BF),
+        jax.ShapeDtypeStruct((half, D_EMB), BF),
     ]
+    out_specs = [pl.BlockSpec((8, STEP), lambda i: (0, i)), rows(TEXTS), rows(D_EMB)]
+    scratch = [pltpu.VMEM((half, D_IMG + PAD), BF)]
     arrays = [*images, w_img, *texts]
+    flops = 2 * half * D_EMB * (2 * TEXTS + D_IMG)
+    if early is None:
+        out_shape += [jax.ShapeDtypeStruct((half, D_EMB), BF)]
+        out_specs += [rows(D_EMB)]
+    else:
+        arrays += [*early[0], early[1]]
+        out_shape += [
+            jax.ShapeDtypeStruct((D_IMG, D_EMB // 2), F32),
+            jax.ShapeDtypeStruct((D_IMG, D_EMB // 2), BF),
+        ]
+        out_specs += [whole(out_shape[3]), whole(out_shape[4])]
+        scratch += [pltpu.VMEM((half, D_EMB), BF)]
+        flops += 2 * IMGS * D_EMB * D_IMG
     return pl.pallas_call(
-        tile_kernel,
-        grid=(IMGS // STEP,),
+        functools.partial(tile_kernel, len(images), early is not None),
+        grid=(half // STEP,),
         in_specs=[smem, smem] + [whole(a) for a in arrays],
-        out_specs=[
-            pl.BlockSpec((8, STEP), lambda i: (0, i)),
-            whole(out_shape[1]),
-            whole(out_shape[2]),
-            whole(out_shape[3]),
-            whole(out_shape[4]),
-        ],
+        out_specs=out_specs,
         out_shape=out_shape,
-        scratch_shapes=[
-            pltpu.VMEM((IMGS, D_IMG + PAD), BF),
-            pltpu.VMEM((IMGS, D_EMB), BF),
-            pltpu.VMEM((IMGS, D_EMB), BF),
-            pltpu.VMEM((IMGS, TEXTS), BF),
-        ],
+        scratch_shapes=scratch,
         compiler_params=pltpu.CompilerParams(vmem_limit_bytes=56 * 2**20),
         cost_estimate=pl.CostEstimate(
-            flops=2 * IMGS * D_EMB * (3 * TEXTS + 2 * D_IMG),
-            bytes_accessed=24 * 2**20,
-            transcendentals=3 * IMGS * TEXTS,
+            flops=flops, bytes_accessed=16 * 2**20, transcendentals=2 * half * TEXTS
         ),
     )(scalars, numbers, *arrays)
+
+
+def text_kernel(coeffs_a, coeffs_b, low_a, low_b, mine, other):
+    total = dot(coeffs_a[...], low_a[...], TN) + dot(coeffs_b[...], low_b[...], TN)
+    step, half = pl.program_id(0), pl.num_programs(0) // 2
+
+    @pl.when(step < half)
+    def _():
+        other[...] = total.astype(BF)
+
+    @pl.when(step >= half)
+    def _():
+        mine[...] = total.astype(BF)
+
+
+def text_directions(coeffs, low):
+    block = 512
+    half = IMGS // 2
+    steps = TEXTS // block // 2
+    column = pl.BlockSpec((half, block), lambda i: (0, (i + steps) % (2 * steps)))
+    keep = pl.BlockSpec((half, D_EMB), lambda i: (0, 0), pipeline_mode=pl.Buffered(1))
+    return pl.pallas_call(
+        text_kernel,
+        grid=(TEXTS // block,),
+        in_specs=[column, column, keep, keep],
+        out_specs=[
+            pl.BlockSpec((block, D_EMB), lambda i: (jnp.maximum(i - steps, 0), 0)),
+            pl.BlockSpec((block, D_EMB), lambda i: (jnp.minimum(i, steps - 1), 0)),
+        ],
+        out_shape=[jax.ShapeDtypeStruct((TEXTS // 2, D_EMB), BF)] * 2,
+        compiler_params=pltpu.CompilerParams(vmem_limit_bytes=60 * 2**20),
+        cost_estimate=pl.CostEstimate(
+            flops=2 * IMGS * D_EMB * TEXTS, bytes_accessed=10 * 2**20, transcendentals=0
+        ),
+    )(*coeffs, *low)
 
 
 def shards(pooled, w_img, text_emb, pos_index, log_scale, bias):
@@ -248,11 +296,16 @@
     starts = lambda c: ((z * NX * NY + plane) * NC + c) * ROWS
     numbers = jnp.concatenate([starts(core), starts(1 - core), core[None]]).astype(jnp.int32)
 
-    loss, t_mine, t_other, w_mine, w_other = tile(scalars, numbers, images, w_img, texts)
+    early_loss, early_coeffs, early_low, early_back = tile(scalars, numbers, images[:4], w_img, texts)
+    late = tile(scalars, numbers, images[4:], w_img, texts, (images[:4], early_back))
+    late_loss, late_coeffs, late_low, w_mine, w_other = late
+    loss = jnp.concatenate([early_loss[0], late_loss[0]])
+    w = w_mine + flip(w_other, "core", NC).astype(F32)
+    late_coeffs, w = lax.optimization_barrier((late_coeffs, w))
+    t_mine, t_other = text_directions((early_coeffs, late_coeffs), (early_low, late_low))
     t_sum = t_mine.astype(F32) + flip(t_other, "core", NC).astype(F32)
-    w = w_mine + flip(w_other, "core", NC).astype(F32)
-    blocks = exchange(t_sum.astype(BF).reshape(NX * NY, ROWS, D_EMB), ("xl", "y"))
-    weight_sum, losses, blocks = sum_weight(w, in_order(loss[0], z), blocks)
+    blocks = t_sum.astype(BF).reshape(NX * NY, ROWS, D_EMB)
+    weight_sum, losses, blocks = sum_weight(w, in_order(loss, z), blocks)
     text_dir = jnp.sum(blocks.astype(F32), axis=0)
     weight_grad = weight_sum / 64.0
     text_grad = (

time: 196 us -> 168 us (0.86)
  waiting for transfers between devices: 87.9 us -> 54.9 us
  Pallas kernels: 30.9 us -> 39.3 us
  other arithmetic: 19.9 us -> 17.3 us
    ppermute x13, waiting for transfers between devices: 56.1 us -> 20.4 us  [flip(): return lax.ppermute(x, axis, [(i, i ^ bit) for i in range(n)])]
    pallas_call x1 -> x3, Pallas kernels: 30.9 us -> 39.3 us  [the longest x2 30.3 us: tile(): pl.pallas_call(functools.partial(tile_kernel, len(images), early is not N...]
    all_to_all x2, waiting for transfers between devices: 4.84 us -> 11.5 us  [exchange(): return lax.all_to_all(x, axes, 0, 0)]
    ppermute x8, waiting for transfers between devices: 26.9 us -> 23 us  [shift(): return lax.ppermute(x, axis, [(i, (i + by) % n) for i in range(n)])]
    convert_element_type x4 -> x3, other arithmetic: 4.05 us -> 4.62 us  [the longest x1 3.9 us: shards(): blocks = t_sum.astype(BF).reshape(NX * NY, ROWS, D_EMB)]
  transfers between devices with their start and end apart: 23 -> 23, of which waited for: 14 -> 13; matrix products, arithmetic and copies ran while one was open for 10% -> 9% of each run, Pallas kernels for 0% -> 13%
where the time goes in v2:
time: 168 us; the launch traced here: 167 us
  waiting for transfers between devices  54.9 us (33%)
  starting transfers between devices  46.7 us (28%)
  Pallas kernels  39.3 us (23%)
  other arithmetic  17.3 us (10%)
  local copies, waits for them, and re-layouts  6.57 us (4%)
  between operations  2.52 us (2%)
    pallas_call x2, Pallas kernels, tile(): pl.pallas_call(functools.partial(tile_kernel, len(images), early is not N...  30.3 us
    ppermute x8, waiting for transfers between devices, shift(): return lax.ppermute(x, axis, [(i, (i + by) % n) for i in range(n)])  23 us
    ppermute x13, starting transfers between devices, flip(): return lax.ppermute(x, axis, [(i, i ^ bit) for i in range(n)])  22.9 us
    ppermute x13, waiting for transfers between devices, flip(): return lax.ppermute(x, axis, [(i, i ^ bit) for i in range(n)])  20.4 us
    ppermute x8, starting transfers between devices, shift(): return lax.ppermute(x, axis, [(i, (i + by) % n) for i in range(n)])  15.1 us
    all_to_all x2, waiting for transfers between devices, exchange(): return lax.all_to_all(x, axes, 0, 0)  11.5 us
    pallas_call x1, Pallas kernels, text_directions(): pl.pallas_call(text_kernel, grid=(TEXTS // block,), in_specs=[column, col...  8.99 us
    all_to_all x2, starting transfers between devices, exchange(): return lax.all_to_all(x, axes, 0, 0)  8.72 us
  transfers between devices with their start and end apart: 23, of which 13 were waited for; matrix products, arithmetic and copies ran while one was open for 9% of the time, Pallas kernels for 13%

profile of v2, /device:TPU:1, one launch (start us, length us, event | category | flops | bytes accessed | tf_op | source)
XLA Modules:
  0.0 167.3 jit_solution(11484748006341444450)
XLA Ops:
  0.6 0.7 and_select_fusion.1
  1.3 0.1 select_convert_fusion
  1.4 1.0 pad_maximum_fusion.refs_0_.refs_8_
  2.5 2.5 %collective-permute-start = (bf16[128,1664]{1,0:T(8,128)(2,1)S(1)}, bf16[128,1664]{1,0:T(8,128)(2,1)S(1)}, u32[]{:S(2)}, u32[]{:S(2)}) collective-permute-start(bf16[128,1664]{1,0:T(8,128)(2,1)S(1)} %pad_maximum_fusion.refs_0_.refs_8_), channel_id=1, source_target_pairs={{0,32},{32,64},{64,96},{96,128},{128,160},{160,192},{192,224},{224... | collective-permute-start | bytes 1277960 | tf_op jit(solution)/shard_map/ppermute | solution.py:27
  5.0 4.0 %collective-permute-start.1 = (bf16[128,1664]{1,0:T(8,128)(2,1)S(1)}, bf16[128,1664]{1,0:T(8,128)(2,1)S(1)}, u32[]{:S(2)}, u32[]{:S(2)}) collective-permute-start(bf16[128,1664]{1,0:T(8,128)(2,1)S(1)} %pad_maximum_fusion.refs_0_.refs_8_), channel_id=1, source_target_pairs={{0,224},{32,0},{64,32},{96,64},{128,96},{160,128},{192,160},{224,1... | collective-permute-start | bytes 1277960 | tf_op jit(solution)/shard_map/ppermute | solution.py:27
  9.0 1.1 fusion.6
  10.1 1.1 fusion.4
  11.2 7.3 %collective-permute-done.refs_1_.refs_9_ = bf16[128,1664]{1,0:T(8,128)(2,1)S(1)} collective-permute-done((bf16[128,1664]{1,0:T(8,128)(2,1)S(1)}, bf16[128,1664]{1,0:T(8,128)(2,1)S(1)}, u32[]{:S(2)}, u32[]{:S(2)}) %collective-permute-start) | collective-permute-done | bytes 426016 | tf_op jit(solution)/shard_map/ppermute | solution.py:27
  18.5 1.6 broadcast_in_dim.33
  20.1 5.1 %all-to-all-start = ((bf16[8,128,1024]{2,1,0:T(8,128)(2,1)}), bf16[8,128,1024]{2,1,0:T(8,128)(2,1)S(1)}, u32[]{:S(2)}, u32[]{:S(2)}) async-start(bf16[8,128,1024]{2,1,0:T(8,128)(2,1)} %broadcast_in_dim.33), calls=%async_computation | async-start | bytes 4194304 | tf_op jit(solution)/shard_map/all_to_all | solution.py:35
  25.3 0.1 collective-permute-start.2
  25.4 2.7 %collective-permute-start.3 = (bf16[128,1664]{1,0:T(8,128)(2,1)S(1)}, bf16[128,1664]{1,0:T(8,128)(2,1)S(1)}, u32[]{:S(2)}, u32[]{:S(2)}) collective-permute-start(bf16[128,1664]{1,0:T(8,128)(2,1)S(1)} %collective-permute-done.1.refs_2_.refs_10_), channel_id=1, source_target_pairs={{0,224},{32,0},{64,32},{96,64},{128,96},{160,128},{192,160},{224,1... | collective-permute-start | bytes 1277960 | tf_op jit(solution)/shard_map/ppermute | solution.py:27
  28.0 8.3 %collective-permute-done.2.refs_3_.refs_11_ = bf16[128,1664]{1,0:T(8,128)(2,1)S(1)} collective-permute-done((bf16[128,1664]{1,0:T(8,128)(2,1)S(1)}, bf16[128,1664]{1,0:T(8,128)(2,1)S(1)}, u32[]{:S(2)}, u32[]{:S(2)}) %collective-permute-start.2) | collective-permute-done | bytes 426016 | tf_op jit(solution)/shard_map/ppermute | solution.py:27
  36.4 0.9 collective-permute-start.4
  37.2 1.9 %collective-permute-start.5 = (bf16[128,1664]{1,0:T(8,128)(2,1)S(1)}, bf16[128,1664]{1,0:T(8,128)(2,1)S(1)}, u32[]{:S(2)}, u32[]{:S(2)}) collective-permute-start(bf16[128,1664]{1,0:T(8,128)(2,1)S(1)} %collective-permute-done.3.refs_0_), channel_id=1, source_target_pairs={{0,224},{32,0},{64,32},{96,64},{128,96},{160,128},{192,160},{224,1... | collective-permute-start | bytes 1277960 | tf_op jit(solution)/shard_map/ppermute | solution.py:27
  39.1 7.4 %collective-permute-done.4.refs_1_ = bf16[128,1664]{1,0:T(8,128)(2,1)S(1)} collective-permute-done((bf16[128,1664]{1,0:T(8,128)(2,1)S(1)}, bf16[128,1664]{1,0:T(8,128)(2,1)S(1)}, u32[]{:S(2)}, u32[]{:S(2)}) %collective-permute-start.4) | collective-permute-done | bytes 426016 | tf_op jit(solution)/shard_map/ppermute | solution.py:27
  46.5 4.8 %all-to-all-done = bf16[8,128,1024]{2,1,0:T(8,128)(2,1)S(1)} async-done(((bf16[8,128,1024]{2,1,0:T(8,128)(2,1)}), bf16[8,128,1024]{2,1,0:T(8,128)(2,1)S(1)}, u32[]{:S(2)}, u32[]{:S(2)}) %all-to-all-start) | async-done | bytes 2097184 | tf_op jit(solution)/shard_map/all_to_all | solution.py:35
  51.4 0.9 collective-permute-start.6
  53.6 0.6 pad_maximum_fusion.4.scalars
  54.2 0.7 pad_add_fusion.numbers
  54.9 0.1 collective-permute-start.7
  55.0 2.9 %collective-permute-start.8 = (bf16[64,1664]{1,0:T(8,128)(2,1)S(1)}, bf16[64,1664]{1,0:T(8,128)(2,1)S(1)}, u32[]{:S(2)}, u32[]{:S(2)}) collective-permute-start(bf16[64,1664]{1,0:T(8,128)(2,1)S(1)} %slice.87), channel_id=1, source_target_pairs={{0,224},{32,0},{64,32},{96,64},{128,96},{160,128},{192,160},{224,1... | collective-permute-start | bytes 638984 | tf_op jit(solution)/shard_map/ppermute | solution.py:27
  57.9 12.1 %shard_map.94 = (f32[8,512]{1,0:T(8,128)}, bf16[512,2048]{1,0:T(8,128)(2,1)}, bf16[512,1024]{1,0:T(8,128)(2,1)}, bf16[512,1024]{1,0:T(8,128)(2,1)}) custom-call(f32[2]{0:T(128)} %pad_maximum_fusion.4.scalars, s32[17]{0:T(128)} %pad_add_fusion.numbers, bf16[128,1664]{1,0:T(8,128)(2,1)} %copy-done.3, bf16[128,1664]{1,0:T(8,128)(2,1)} %copy-done.9, ...), custom_call_target="tpu_custom_call" | custom-call | flops 5905580032 | bytes 16777216 | tf_op jit(solution)/shard_map/pallas_call | solution.py:233
  70.1 0.7 copy-done.13
  70.8 18.2 %shard_map.95 = (f32[8,512]{1,0:T(8,128)}, bf16[512,2048]{1,0:T(8,128)(2,1)}, bf16[512,1024]{1,0:T(8,128)(2,1)}, f32[1536,512]{1,0:T(8,128)}, bf16[1536,512]{1,0:T(8,128)(2,1)}) custom-call(f32[2]{0:T(128)} %pad_maximum_fusion.4.scalars, s32[17]{0:T(128)} %pad_add_fusion.numbers, bf16[128,1664]{1,0:T(8,128)(2,1)} %copy-done.12, bf16[128,1664]{1,0:T(8,128)(2,1)} %copy-done.4, ...), custom_call_target="tpu_custom_call" | custom-call | flops 9126805504 | bytes 16777216 | tf_op jit(solution)/shard_map/pallas_call | solution.py:233
  89.0 0.7 collective-permute-start.9
  89.7 0.7 fusion.34
  90.5 0.7 fusion.35
  91.2 0.6 constant_dynamic-slice_fusion.13
  91.9 1.1 collective-permute-done.9
  93.0 2.4 %convert_add_fusion = f32[1536,512]{1,0:T(8,128)S(1)} fusion(f32[1536,512]{1,0:T(8,128)} %get-tuple-element.38, bf16[1536,512]{1,0:T(8,128)(2,1)S(1)} %collective-permute-done.9), kind=kLoop, calls=%fused_computation.2 | loop fusion | flops 1572864 | bytes 7864320 | tf_op jit(solution)/shard_map/add | solution.py:303
  95.4 0.4 fusion.33
  95.8 0.8 pad_maximum_fusion.1
  96.7 1.9 %collective-permute-start.12 = (bf16[2,2,2,2,2,24,256]{6,5,4,3,1,0,2:T(8,128)(2,1)S(1)}, bf16[2,2,2,2,2,24,256]{6,5,4,3,1,0,2:T(8,128)(2,1)}, u32[]{:S(2)}, u32[]{:S(2)}) collective-permute-start(bf16[2,2,2,2,2,24,256]{6,5,4,3,1,0,2:T(8,128)(2,1)S(1)} %fusion.10), channel_id=1, source_target_pairs={{0,8},{4,12},{8,0},{12,4},{1,9},{5,13},{9,1},{13,5},{2,10},{6,14},... | collective-permute-start | bytes 1179656 | tf_op jit(solution)/shard_map/ppermute | solution.py:31
  98.5 9.0 %shard_map.96 = (bf16[1024,1024]{1,0:T(8,128)(2,1)}, bf16[1024,1024]{1,0:T(8,128)(2,1)}) custom-call(bf16[512,2048]{1,0:T(8,128)(2,1)} %get-tuple-element.41.coeffs_a, bf16[512,2048]{1,0:T(8,128)(2,1)} %get-tuple-element.42.coeffs_b, bf16[512,1024]{1,0:T(8,128)(2,1)} %get-tuple-element.43.low_a, bf16[512,1024]{1,0:T(8,128)(2,1)} %get-tuple-element.44.low_b), custom_call_target="tpu_custom_call" | custom-call | flops 4294967296 | bytes 10485760 | tf_op jit(solution)/shard_map/pallas_call | solution.py:266
  107.5 0.6 collective-permute-start.19
  108.2 0.7 collective-permute-done.12
  108.9 1.1 fusion
  110.1 1.2 collective-permute-start.13
  111.3 1.0 slice.107
  112.3 0.1 convert_add_fusion.1
  112.4 0.7 slice_convert_fusion
  113.2 1.6 collective-permute-start.11
  114.8 0.5 collective-permute-done.13
  115.4 3.9 %collective-permute-done.11 = bf16[2,2,2,2,24,256]{5,4,3,2,1,0:T(8,128)(2,1)S(1)} collective-permute-done((bf16[2,2,2,2,24,256]{5,4,3,2,1,0:T(8,128)(2,1)S(1)}, bf16[2,2,2,2,24,256]{5,4,3,2,1,0:T(8,128)(2,1)S(1)}, u32[]{:S(2)}, u32[]{:S(2)}) %collective-permute-start.11) | collective-permute-done | bytes 196640 | tf_op jit(solution)/shard_map/ppermute | solution.py:31
  119.4 0.7 collective-permute-start.14
  120.0 3.9 %collective-permute-done.14 = bf16[2,2,2,24,512]{4,3,2,1,0:T(8,128)(2,1)S(1)} collective-permute-done((bf16[2,2,2,24,512]{4,3,2,1,0:T(8,128)(2,1)S(1)}, bf16[2,2,2,24,512]{4,3,2,1,0:T(8,128)(2,1)S(1)}, u32[]{:S(2)}, u32[]{:S(2)}) %collective-permute-start.14) | collective-permute-done | bytes 196640 | tf_op jit(solution)/shard_map/ppermute | solution.py:31
  124.1 1.3 collective-permute-start.15
  125.4 2.3 %collective-permute-done.15 = bf16[2,2,24,512]{3,2,1,0:T(8,128)(2,1)S(1)} collective-permute-done((bf16[2,2,24,512]{3,2,1,0:T(8,128)(2,1)S(1)}, bf16[2,2,24,512]{3,2,1,0:T(8,128)(2,1)S(1)}, u32[]{:S(2)}, u32[]{:S(2)}) %collective-permute-start.15) | collective-permute-done | bytes 98336 | tf_op jit(solution)/shard_map/ppermute | solution.py:31
  127.7 0.2 copy.38
  128.0 2.5 %collective-permute-start.16 = (f32[2,2,2,6,512]{4,2,3,1,0:T(2,128)S(1)}, f32[2,2,2,6,512]{4,2,3,1,0:T(2,128)S(1)}, u32[]{:S(2)}, u32[]{:S(2)}) collective-permute-start(f32[2,2,2,6,512]{4,2,3,1,0:T(2,128)S(1)} %bitcast.118), channel_id=1, source_target_pairs={{0,1},{1,0},{2,3},{3,2},{4,5},{5,4},{6,7},{7,6},{8,9},{9,8},{10,11... | collective-permute-start | bytes 294920 | tf_op jit(solution)/shard_map/ppermute | solution.py:31
  130.5 3.9 %add_convert_fusion = bf16[1024,1024]{1,0:T(8,128)(2,1)} fusion(bf16[1024,1024]{1,0:T(8,128)(2,1)} %collective-permute-done.19, bf16[1024,1024]{1,0:T(8,128)(2,1)S(1)} %copy-done.1), kind=kLoop, calls=%fused_computation.1 | loop fusion | flops 4194304 | bytes 6291456 | tf_op jit(solution)/shard_map/convert_element_type | solution.py:307
  134.4 3.6 %all-to-all-start.1 = ((bf16[8,128,1024]{2,1,0:T(8,128)(2,1)}), bf16[8,128,1024]{2,1,0:T(8,128)(2,1)S(1)}, u32[]{:S(2)}, u32[]{:S(2)}) async-start(bf16[8,128,1024]{2,1,0:T(8,128)(2,1)} %bitcast.33), calls=%async_computation.1 | async-start | bytes 4194304 | tf_op jit(solution)/shard_map/all_to_all | solution.py:35
  138.2 1.8 %collective-permute-start.17 = (f32[40,512]{1,0:T(8,128)S(1)}, f32[40,512]{1,0:T(8,128)S(1)}, u32[]{:S(2)}, u32[]{:S(2)}) collective-permute-start(f32[40,512]{1,0:T(8,128)S(1)} %pad_maximum_fusion.2), channel_id=1, source_target_pairs={{0,64},{32,96},{64,0},{96,32},{128,192},{160,224},{192,128},{224,1... | collective-permute-start | bytes 245768 | tf_op jit(solution)/shard_map/ppermute | solution.py:31
  140.0 3.3 %collective-permute-done.17 = f32[40,512]{1,0:T(8,128)S(1)} collective-permute-done((f32[40,512]{1,0:T(8,128)S(1)}, f32[40,512]{1,0:T(8,128)S(1)}, u32[]{:S(2)}, u32[]{:S(2)}) %collective-permute-start.17) | collective-permute-done | bytes 81952 | tf_op jit(solution)/shard_map/ppermute | solution.py:31
  143.6 3.8 %collective-permute-start.18 = (f32[28,512]{1,0:T(8,128)S(1)}, f32[28,512]{1,0:T(8,128)S(1)}, u32[]{:S(2)}, u32[]{:S(2)}) collective-permute-start(f32[28,512]{1,0:T(8,128)S(1)} %pad_maximum_fusion.3), channel_id=1, source_target_pairs={{0,128},{32,160},{64,192},{96,224},{128,0},{160,32},{192,64},{224,... | collective-permute-start | bytes 172040 | tf_op jit(solution)/shard_map/ppermute | solution.py:31
  147.4 4.5 %collective-permute-done.18 = f32[28,512]{1,0:T(8,128)S(1)} collective-permute-done((f32[28,512]{1,0:T(8,128)S(1)}, f32[28,512]{1,0:T(8,128)S(1)}, u32[]{:S(2)}, u32[]{:S(2)}) %collective-permute-start.18) | collective-permute-done | bytes 57376 | tf_op jit(solution)/shard_map/ppermute | solution.py:31
  151.9 0.5 fusion.31
  152.5 6.6 %all-to-all-done.1 = bf16[8,128,1024]{2,1,0:T(8,128)(2,1)S(1)} async-done(((bf16[8,128,1024]{2,1,0:T(8,128)(2,1)}), bf16[8,128,1024]{2,1,0:T(8,128)(2,1)S(1)}, u32[]{:S(2)}, u32[]{:S(2)}) %all-to-all-start.1) | async-done | bytes 2097184 | tf_op jit(solution)/shard_map/all_to_all | solution.py:35
  159.2 5.9 %collective-permute-start.20 = (f32[6,512]{1,0:T(8,128)S(1)}, f32[6,512]{1,0:T(8,128)S(1)}, u32[]{:S(2)}, u32[]{:S(2)}) collective-permute-start(f32[6,512]{1,0:T(8,128)S(1)} %bitcast.121), channel_id=1, source_target_pairs={{0,2},{2,0},{1,3},{3,1},{4,6},{6,4},{5,7},{7,5},{8,10},{10,8},{9,1... | collective-permute-start | bytes 36872 | tf_op jit(solution)/shard_map/ppermute | solution.py:31
  165.1 0.3 convert_reduce_fusion
  165.4 0.2 fusion.5
  165.7 1.0 fusion.9
  166.7 0.6 fusion.20
  (95 shorter events, 1.2 us)
Async XLA Ops:
  2.4 17.7 %copy-start.3 = (bf16[128,1664]{1,0:T(8,128)(2,1)}, bf16[128,1664]{1,0:T(8,128)(2,1)S(1)}, u32[]{:S(2)}) copy-start(bf16[128,1664]{1,0:T(8,128)(2,1)S(1)} %pad_maximum_fusion.refs_0_.refs_8_) | copy-start | bytes 1277956
  2.5 16.0 %collective-permute-start = (bf16[128,1664]{1,0:T(8,128)(2,1)S(1)}, bf16[128,1664]{1,0:T(8,128)(2,1)S(1)}, u32[]{:S(2)}, u32[]{:S(2)}) collective-permute-start(bf16[128,1664]{1,0:T(8,128)(2,1)S(1)} %pad_maximum_fusion.refs_0_.refs_8_), channel_id=1, source_target_pairs={{0,32},{32,64},{64,96},{96,128},{128,160},{160,192},{192,224},{224... | collective-permute-start | bytes 1277960 | tf_op jit(solution)/shard_map/ppermute | solution.py:27
  5.0 13.5 %collective-permute-start.1 = (bf16[128,1664]{1,0:T(8,128)(2,1)S(1)}, bf16[128,1664]{1,0:T(8,128)(2,1)S(1)}, u32[]{:S(2)}, u32[]{:S(2)}) collective-permute-start(bf16[128,1664]{1,0:T(8,128)(2,1)S(1)} %pad_maximum_fusion.refs_0_.refs_8_), channel_id=1, source_target_pairs={{0,224},{32,0},{64,32},{96,64},{128,96},{160,128},{192,160},{224,1... | collective-permute-start | bytes 1277960 | tf_op jit(solution)/shard_map/ppermute | solution.py:27
  10.1 8.4 %copy-start.7 = (f32[128]{0:T(128)}, f32[128]{0:T(128)S(1)}, u32[]{:S(2)}) copy-start(f32[128]{0:T(128)S(1)} %add_rsqrt_fusion) | copy-start | bytes 1540
  18.5 6.8 %copy-start.9 = (bf16[128,1664]{1,0:T(8,128)(2,1)}, bf16[128,1664]{1,0:T(8,128)(2,1)S(1)}, u32[]{:S(2)}) copy-start(bf16[128,1664]{1,0:T(8,128)(2,1)S(1)} %collective-permute-done.refs_1_.refs_9_) | copy-start | bytes 1277956
  18.5 6.8 %copy-start.10 = (bf16[128,1664]{1,0:T(8,128)(2,1)}, bf16[128,1664]{1,0:T(8,128)(2,1)S(1)}, u32[]{:S(2)}) copy-start(bf16[128,1664]{1,0:T(8,128)(2,1)S(1)} %collective-permute-done.1.refs_2_.refs_10_) | copy-start | bytes 1277956
  20.1 31.3 %all-to-all-start = ((bf16[8,128,1024]{2,1,0:T(8,128)(2,1)}), bf16[8,128,1024]{2,1,0:T(8,128)(2,1)S(1)}, u32[]{:S(2)}, u32[]{:S(2)}) async-start(bf16[8,128,1024]{2,1,0:T(8,128)(2,1)} %broadcast_in_dim.33), calls=%async_computation | async-start | bytes 4194304 | tf_op jit(solution)/shard_map/all_to_all | solution.py:35
  25.3 11.1 %collective-permute-start.2 = (bf16[128,1664]{1,0:T(8,128)(2,1)S(1)}, bf16[128,1664]{1,0:T(8,128)(2,1)S(1)}, u32[]{:S(2)}, u32[]{:S(2)}) collective-permute-start(bf16[128,1664]{1,0:T(8,128)(2,1)S(1)} %collective-permute-done.refs_1_.refs_9_), channel_id=1, source_target_pairs={{0,32},{32,64},{64,96},{96,128},{128,160},{160,192},{192,224},{224... | collective-permute-start | bytes 1277960 | tf_op jit(solution)/shard_map/ppermute | solution.py:27
  25.4 11.0 %collective-permute-start.3 = (bf16[128,1664]{1,0:T(8,128)(2,1)S(1)}, bf16[128,1664]{1,0:T(8,128)(2,1)S(1)}, u32[]{:S(2)}, u32[]{:S(2)}) collective-permute-start(bf16[128,1664]{1,0:T(8,128)(2,1)S(1)} %collective-permute-done.1.refs_2_.refs_10_), channel_id=1, source_target_pairs={{0,224},{32,0},{64,32},{96,64},{128,96},{160,128},{192,160},{224,1... | collective-permute-start | bytes 1277960 | tf_op jit(solution)/shard_map/ppermute | solution.py:27
  36.3 10.2 %copy-start.11 = (bf16[128,1664]{1,0:T(8,128)(2,1)}, bf16[128,1664]{1,0:T(8,128)(2,1)S(1)}, u32[]{:S(2)}) copy-start(bf16[128,1664]{1,0:T(8,128)(2,1)S(1)} %collective-permute-done.2.refs_3_.refs_11_) | copy-start | bytes 1277956
  36.3 10.2 %copy-start.12 = (bf16[128,1664]{1,0:T(8,128)(2,1)}, bf16[128,1664]{1,0:T(8,128)(2,1)S(1)}, u32[]{:S(2)}) copy-start(bf16[128,1664]{1,0:T(8,128)(2,1)S(1)} %collective-permute-done.3.refs_0_) | copy-start | bytes 1277956
  36.4 10.2 %collective-permute-start.4 = (bf16[128,1664]{1,0:T(8,128)(2,1)S(1)}, bf16[128,1664]{1,0:T(8,128)(2,1)S(1)}, u32[]{:S(2)}, u32[]{:S(2)}) collective-permute-start(bf16[128,1664]{1,0:T(8,128)(2,1)S(1)} %collective-permute-done.2.refs_3_.refs_11_), channel_id=1, source_target_pairs={{0,32},{32,64},{64,96},{96,128},{128,160},{160,192},{192,224},{224... | collective-permute-start | bytes 1277960 | tf_op jit(solution)/shard_map/ppermute | solution.py:27
  37.2 9.3 %collective-permute-start.5 = (bf16[128,1664]{1,0:T(8,128)(2,1)S(1)}, bf16[128,1664]{1,0:T(8,128)(2,1)S(1)}, u32[]{:S(2)}, u32[]{:S(2)}) collective-permute-start(bf16[128,1664]{1,0:T(8,128)(2,1)S(1)} %collective-permute-done.3.refs_0_), channel_id=1, source_target_pairs={{0,224},{32,0},{64,32},{96,64},{128,96},{160,128},{192,160},{224,1... | collective-permute-start | bytes 1277960 | tf_op jit(solution)/shard_map/ppermute | solution.py:27
  46.5 23.5 %copy-start.4 = (bf16[128,1664]{1,0:T(8,128)(2,1)}, bf16[128,1664]{1,0:T(8,128)(2,1)S(1)}, u32[]{:S(2)}) copy-start(bf16[128,1664]{1,0:T(8,128)(2,1)S(1)} %collective-permute-done.4.refs_1_) | copy-start | bytes 1277956
  46.5 23.5 %copy-start.5 = (bf16[128,1664]{1,0:T(8,128)(2,1)}, bf16[128,1664]{1,0:T(8,128)(2,1)S(1)}, u32[]{:S(2)}) copy-start(bf16[128,1664]{1,0:T(8,128)(2,1)S(1)} %collective-permute-done.5.refs_2_) | copy-start | bytes 1277956
  51.4 6.5 %copy-start.2 = (bf16[8,128,1024]{2,1,0:T(8,128)(2,1)}, bf16[8,128,1024]{2,1,0:T(8,128)(2,1)S(1)}, u32[]{:S(2)}) copy-start(bf16[8,128,1024]{2,1,0:T(8,128)(2,1)S(1)} %all-to-all-done) | copy-start | bytes 6291460
  51.4 6.5 %collective-permute-start.6 = (bf16[1024,1024]{1,0:T(8,128)(2,1)S(1)}, bf16[1024,1024]{1,0:T(8,128)(2,1)}, u32[]{:S(2)}, u32[]{:S(2)}) collective-permute-start(bf16[1024,1024]{1,0:T(8,128)(2,1)S(1)} %bitcast.111), channel_id=1, source_target_pairs={{0,2},{2,0},{1,3},{3,1},{4,6},{6,4},{5,7},{7,5},{8,10},{10,8},{9,1... | collective-permute-start | bytes 6291464 | tf_op jit(solution)/shard_map/ppermute | solution.py:31
  54.9 15.2 %collective-permute-start.7 = (bf16[64,1664]{1,0:T(8,128)(2,1)S(1)}, bf16[64,1664]{1,0:T(8,128)(2,1)S(1)}, u32[]{:S(2)}, u32[]{:S(2)}) collective-permute-start(bf16[64,1664]{1,0:T(8,128)(2,1)S(1)} %slice.86), channel_id=1, source_target_pairs={{0,32},{32,64},{64,96},{96,128},{128,160},{160,192},{192,224},{224... | collective-permute-start | bytes 638984 | tf_op jit(solution)/shard_map/ppermute | solution.py:27
  55.0 15.1 %collective-permute-start.8 = (bf16[64,1664]{1,0:T(8,128)(2,1)S(1)}, bf16[64,1664]{1,0:T(8,128)(2,1)S(1)}, u32[]{:S(2)}, u32[]{:S(2)}) collective-permute-start(bf16[64,1664]{1,0:T(8,128)(2,1)S(1)} %slice.87), channel_id=1, source_target_pairs={{0,224},{32,0},{64,32},{96,64},{128,96},{160,128},{192,160},{224,1... | collective-permute-start | bytes 638984 | tf_op jit(solution)/shard_map/ppermute | solution.py:27
  70.0 0.7 copy-start.13
  70.1 0.8 copy-start.14
  89.0 4.0 %collective-permute-start.9 = (bf16[1536,512]{1,0:T(8,128)(2,1)}, bf16[1536,512]{1,0:T(8,128)(2,1)S(1)}, u32[]{:S(2)}, u32[]{:S(2)}) collective-permute-start(bf16[1536,512]{1,0:T(8,128)(2,1)} %get-tuple-element.39), channel_id=1, source_target_pairs={{0,2},{2,0},{1,3},{3,1},{4,6},{6,4},{5,7},{7,5},{8,10},{10,8},{9,1... | collective-permute-start | bytes 4718600 | tf_op jit(solution)/shard_map/ppermute | solution.py:31
  96.6 14.7 %collective-permute-start.10 = (bf16[784,256]{1,0:T(8,128)(2,1)}, bf16[784,256]{1,0:T(8,128)(2,1)}, u32[]{:S(2)}, u32[]{:S(2)}) collective-permute-start(bf16[784,256]{1,0:T(8,128)(2,1)} %pad_maximum_fusion.1), channel_id=1, source_target_pairs={{0,32},{32,0},{64,96},{96,64},{128,160},{160,128},{192,224},{224,1... | collective-permute-start | bytes 1204232 | tf_op jit(solution)/shard_map/ppermute | solution.py:31
  96.7 12.2 %collective-permute-start.12 = (bf16[2,2,2,2,2,24,256]{6,5,4,3,1,0,2:T(8,128)(2,1)S(1)}, bf16[2,2,2,2,2,24,256]{6,5,4,3,1,0,2:T(8,128)(2,1)}, u32[]{:S(2)}, u32[]{:S(2)}) collective-permute-start(bf16[2,2,2,2,2,24,256]{6,5,4,3,1,0,2:T(8,128)(2,1)S(1)} %fusion.10), channel_id=1, source_target_pairs={{0,8},{4,12},{8,0},{12,4},{1,9},{5,13},{9,1},{13,5},{2,10},{6,14},... | collective-permute-start | bytes 1179656 | tf_op jit(solution)/shard_map/ppermute | solution.py:31
  107.5 23.0 %collective-permute-start.19 = (bf16[1024,1024]{1,0:T(8,128)(2,1)}, bf16[1024,1024]{1,0:T(8,128)(2,1)}, u32[]{:S(2)}, u32[]{:S(2)}) collective-permute-start(bf16[1024,1024]{1,0:T(8,128)(2,1)} %get-tuple-element.46), channel_id=1, source_target_pairs={{0,2},{2,0},{1,3},{3,1},{4,6},{6,4},{5,7},{7,5},{8,10},{10,8},{9,1... | collective-permute-start | bytes 6291464 | tf_op jit(solution)/shard_map/ppermute | solution.py:31
  110.1 5.3 %collective-permute-start.13 = (bf16[2,2,2,2,24,256]{5,4,3,2,1,0:T(8,128)(2,1)S(1)}, bf16[2,2,2,2,24,256]{5,4,3,2,1,0:T(8,128)(2,1)S(1)}, u32[]{:S(2)}, u32[]{:S(2)}) collective-permute-start(bf16[2,2,2,2,24,256]{5,4,3,2,1,0:T(8,128)(2,1)S(1)} %fusion.17), channel_id=1, source_target_pairs={{0,32},{32,0},{64,96},{96,64},{128,160},{160,128},{192,224},{224,1... | collective-permute-start | bytes 589832 | tf_op jit(solution)/shard_map/ppermute | solution.py:31
  112.4 7.6 %copy-start.6 = (f32[2,2,1,128]{3,2,1,0:T(1,128)S(1)}, f32[2,2,1,128]{3,2,1,0:T(1,128)}, u32[]{:S(2)}) copy-start(f32[2,2,1,128]{3,2,1,0:T(1,128)} %get-tuple-element.63) | copy-start | bytes 6148
  113.2 6.1 %collective-permute-start.11 = (bf16[2,2,2,2,24,256]{5,4,3,2,1,0:T(8,128)(2,1)S(1)}, bf16[2,2,2,2,24,256]{5,4,3,2,1,0:T(8,128)(2,1)S(1)}, u32[]{:S(2)}, u32[]{:S(2)}) collective-permute-start(bf16[2,2,2,2,24,256]{5,4,3,2,1,0:T(8,128)(2,1)S(1)} %fusion.16), channel_id=1, source_target_pairs={{0,8},{4,12},{8,0},{12,4},{1,9},{5,13},{9,1},{13,5},{2,10},{6,14},... | collective-permute-start | bytes 589832 | tf_op jit(solution)/shard_map/ppermute | solution.py:31
  119.3 11.2 %copy-start.1 = (bf16[1024,1024]{1,0:T(8,128)(2,1)S(1)}, bf16[1024,1024]{1,0:T(8,128)(2,1)}, u32[]{:S(2)}) copy-start(bf16[1024,1024]{1,0:T(8,128)(2,1)} %get-tuple-element.45) | copy-start | bytes 6291460
  119.4 4.6 %collective-permute-start.14 = (bf16[2,2,2,24,512]{4,3,2,1,0:T(8,128)(2,1)S(1)}, bf16[2,2,2,24,512]{4,3,2,1,0:T(8,128)(2,1)S(1)}, u32[]{:S(2)}, u32[]{:S(2)}) collective-permute-start(bf16[2,2,2,24,512]{4,3,2,1,0:T(8,128)(2,1)S(1)} %fusion.18), channel_id=1, source_target_pairs={{0,4},{4,0},{8,12},{12,8},{1,5},{5,1},{9,13},{13,9},{2,6},{6,2},{1... | collective-permute-start | bytes 589832 | tf_op jit(solution)/shard_map/ppermute | solution.py:31
  124.1 3.6 %collective-permute-start.15 = (bf16[2,2,24,512]{3,2,1,0:T(8,128)(2,1)S(1)}, bf16[2,2,24,512]{3,2,1,0:T(8,128)(2,1)S(1)}, u32[]{:S(2)}, u32[]{:S(2)}) collective-permute-start(bf16[2,2,24,512]{3,2,1,0:T(8,128)(2,1)S(1)} %fusion.19), channel_id=1, source_target_pairs={{0,16},{16,0},{1,17},{17,1},{2,18},{18,2},{3,19},{19,3},{4,20},{20... | collective-permute-start | bytes 294920 | tf_op jit(solution)/shard_map/ppermute | solution.py:31
  128.0 10.1 %collective-permute-start.16 = (f32[2,2,2,6,512]{4,2,3,1,0:T(2,128)S(1)}, f32[2,2,2,6,512]{4,2,3,1,0:T(2,128)S(1)}, u32[]{:S(2)}, u32[]{:S(2)}) collective-permute-start(f32[2,2,2,6,512]{4,2,3,1,0:T(2,128)S(1)} %bitcast.118), channel_id=1, source_target_pairs={{0,1},{1,0},{2,3},{3,2},{4,5},{5,4},{6,7},{7,6},{8,9},{9,8},{10,11... | collective-permute-start | bytes 294920 | tf_op jit(solution)/shard_map/ppermute | solution.py:31
  134.4 24.7 %all-to-all-start.1 = ((bf16[8,128,1024]{2,1,0:T(8,128)(2,1)}), bf16[8,128,1024]{2,1,0:T(8,128)(2,1)S(1)}, u32[]{:S(2)}, u32[]{:S(2)}) async-start(bf16[8,128,1024]{2,1,0:T(8,128)(2,1)} %bitcast.33), calls=%async_computation.1 | async-start | bytes 4194304 | tf_op jit(solution)/shard_map/all_to_all | solution.py:35
  138.2 27.2 %copy-start = (bf16[1,128,1024]{2,1,0:T(8,128)(2,1)S(1)}, bf16[1,128,1024]{2,1,0:T(8,128)(2,1)}, u32[]{:S(2)}) copy-start(bf16[1,128,1024]{2,1,0:T(8,128)(2,1)} %param.9) | copy-start | bytes 786436
  138.2 27.2 %copy-start.8 = (f32[128]{0:T(128)S(1)}, f32[128]{0:T(128)}, u32[]{:S(2)}) copy-start(f32[128]{0:T(128)} %copy-done.7) | copy-start | bytes 1540
  138.2 5.2 %collective-permute-start.17 = (f32[40,512]{1,0:T(8,128)S(1)}, f32[40,512]{1,0:T(8,128)S(1)}, u32[]{:S(2)}, u32[]{:S(2)}) collective-permute-start(f32[40,512]{1,0:T(8,128)S(1)} %pad_maximum_fusion.2), channel_id=1, source_target_pairs={{0,64},{32,96},{64,0},{96,32},{128,192},{160,224},{192,128},{224,1... | collective-permute-start | bytes 245768 | tf_op jit(solution)/shard_map/ppermute | solution.py:31
  143.6 8.2 %collective-permute-start.18 = (f32[28,512]{1,0:T(8,128)S(1)}, f32[28,512]{1,0:T(8,128)S(1)}, u32[]{:S(2)}, u32[]{:S(2)}) collective-permute-start(f32[28,512]{1,0:T(8,128)S(1)} %pad_maximum_fusion.3), channel_id=1, source_target_pairs={{0,128},{32,160},{64,192},{96,224},{128,0},{160,32},{192,64},{224,... | collective-permute-start | bytes 172040 | tf_op jit(solution)/shard_map/ppermute | solution.py:31
  159.2 7.5 %collective-permute-start.20 = (f32[6,512]{1,0:T(8,128)S(1)}, f32[6,512]{1,0:T(8,128)S(1)}, u32[]{:S(2)}, u32[]{:S(2)}) collective-permute-start(f32[6,512]{1,0:T(8,128)S(1)} %bitcast.121), channel_id=1, source_target_pairs={{0,2},{2,0},{1,3},{3,1},{4,6},{6,4},{5,7},{7,5},{8,10},{10,8},{9,1... | collective-permute-start | bytes 36872 | tf_op jit(solution)/shard_map/ppermute | solution.py:31

commit v3 on v2

--- a/solution.py
+++ b/solution.py
@@ -36,20 +36,22 @@
 
 
 def gather(image, text):
+    copies = jnp.broadcast_to(text, (NX * NY, *text.shape))
+    near = exchange(copies, ("xl", "y")).reshape(NX * NY * ROWS, D_EMB)
     down, up = [image], [image]
     for k in range(3):
         down.append(shift(down[-1], "z", NZ, 1))
         up.append(shift(up[-1], "z", NZ, -1))
-        if k == 0:
-            copies = jnp.broadcast_to(text, (NX * NY, *text.shape))
-            down[1], up[1], copies = lax.optimization_barrier((down[1], up[1], copies))
-            near = exchange(copies, ("xl", "y")).reshape(NX * NY * ROWS, D_EMB)
         if k == 1:
-            down[2], up[2] = lax.optimization_barrier((down[2], up[2]))
-    down[3], up[3], near = lax.optimization_barrier((down[3], up[3], near))
-    far = [shift(down[3][:HALF], "z", NZ, 1), shift(up[3][HALF:], "z", NZ, -1)]
-    images = [image, down[1], up[1], down[2], up[2], down[3], up[3]] + far
+            down[-1], up[-1], near = lax.optimization_barrier((down[-1], up[-1], near))
+        elif k == 0:
+            down[-1], up[-1] = lax.optimization_barrier((down[-1], up[-1]))
+    images = [image, down[1], up[1], down[2], up[2], down[3], up[3]]
     return images, [near, flip(near, "core", NC)]
+
+
+def gather_last(below, above):
+    return [shift(below[:HALF], "z", NZ, 1), shift(above[HALF:], "z", NZ, -1)]
 
 
 def halve(w, dim, here, axis, n, bit, kind):
@@ -140,11 +142,13 @@
     return total
 
 
-def tile_kernel(n_images, weigh, scalars, numbers, *refs):
+def tile_kernel(n_images, n_early, scalars, numbers, *refs):
+    weigh = n_early > 0
     images, (w_img, *texts) = refs[:n_images], refs[n_images : n_images + 3]
     refs = refs[n_images + 3 :]
     if weigh:
-        early, (early_back, loss, coeffs, low_out, w_mine, w_other, image, back) = refs[:4], refs[4:]
+        early, early_back, refs = refs[:n_early], refs[n_early : n_early + 2], refs[n_early + 2 :]
+        loss, coeffs, low_out, w_mine, w_other, image, back = refs
     else:
         loss, coeffs, low_out, back_out, image = refs
     step = pl.program_id(0)
@@ -195,10 +199,15 @@
         half = D_EMB // 2
         for ref, c in ((w_other, 1 - core), (w_mine, core)):
             columns = pl.ds(pl.multiple_of(c * half, half), half)
-            right, early_right = back[:, columns], early_back[:, columns]
             for k in range(0, D_IMG, 512):
-                left = jnp.concatenate([e[:, k : k + 512] for e in early])
-                w = dot(image[:, k : k + 512], right, TN) + dot(left, early_right, TN)
+                at = slice(k, k + 512)
+                w = dot(image[:, at], back[:, columns], TN)
+                done = 0
+                for part in early_back:
+                    n = part.shape[0] // ROWS
+                    left = jnp.concatenate([e[:, at] for e in early[done : done + n]])
+                    w = w + dot(left, part[:, columns], TN)
+                    done += n
                 ref[k : k + 512, :] = w.astype(ref.dtype)
 
 
@@ -208,7 +217,7 @@
 
     rows = lambda n: pl.BlockSpec((STEP, n), lambda i: (i, 0))
     smem = pl.BlockSpec(memory_space=pltpu.SMEM)
-    half = IMGS // 2
+    half = sum(b.shape[0] for b in images)
     out_shape = [
         jax.ShapeDtypeStruct((8, half), F32),
         jax.ShapeDtypeStruct((half, TEXTS), BF),
@@ -222,7 +231,7 @@
         out_shape += [jax.ShapeDtypeStruct((half, D_EMB), BF)]
         out_specs += [rows(D_EMB)]
     else:
-        arrays += [*early[0], early[1]]
+        arrays += [*early[0], *early[1]]
         out_shape += [
             jax.ShapeDtypeStruct((D_IMG, D_EMB // 2), F32),
             jax.ShapeDtypeStruct((D_IMG, D_EMB // 2), BF),
@@ -231,7 +240,7 @@
         scratch += [pltpu.VMEM((half, D_EMB), BF)]
         flops += 2 * IMGS * D_EMB * D_IMG
     return pl.pallas_call(
-        functools.partial(tile_kernel, len(images), early is not None),
+        functools.partial(tile_kernel, len(images), len(early[0]) if early else 0),
         grid=(half // STEP,),
         in_specs=[smem, smem] + [whole(a) for a in arrays],
         out_specs=out_specs,
@@ -244,8 +253,9 @@
     )(scalars, numbers, *arrays)
 
 
-def text_kernel(coeffs_a, coeffs_b, low_a, low_b, mine, other):
-    total = dot(coeffs_a[...], low_a[...], TN) + dot(coeffs_b[...], low_b[...], TN)
+def text_kernel(*refs):
+    coeffs, low, (mine, other) = refs[:3], refs[3:6], refs[6:]
+    total = sum(dot(c[...], v[...], TN) for c, v in zip(coeffs, low))
     step, half = pl.program_id(0), pl.num_programs(0) // 2
 
     @pl.when(step < half)
@@ -259,14 +269,13 @@
 
 def text_directions(coeffs, low):
     block = 512
-    half = IMGS // 2
     steps = TEXTS // block // 2
-    column = pl.BlockSpec((half, block), lambda i: (0, (i + steps) % (2 * steps)))
-    keep = pl.BlockSpec((half, D_EMB), lambda i: (0, 0), pipeline_mode=pl.Buffered(1))
+    column = lambda c: pl.BlockSpec((c.shape[0], block), lambda i: (0, (i + steps) % (2 * steps)))
+    keep = lambda v: pl.BlockSpec(v.shape, lambda i: (0, 0), pipeline_mode=pl.Buffered(1))
     return pl.pallas_call(
         text_kernel,
         grid=(TEXTS // block,),
-        in_specs=[column, column, keep, keep],
+        in_specs=[*map(column, coeffs), *map(keep, low)],
         out_specs=[
             pl.BlockSpec((block, D_EMB), lambda i: (jnp.maximum(i - steps, 0), 0)),
             pl.BlockSpec((block, D_EMB), lambda i: (jnp.minimum(i, steps - 1), 0)),
@@ -296,13 +305,17 @@
     starts = lambda c: ((z * NX * NY + plane) * NC + c) * ROWS
     numbers = jnp.concatenate([starts(core), starts(1 - core), core[None]]).astype(jnp.int32)
 
-    early_loss, early_coeffs, early_low, early_back = tile(scalars, numbers, images[:4], w_img, texts)
-    late = tile(scalars, numbers, images[4:], w_img, texts, (images[:4], early_back))
-    late_loss, late_coeffs, late_low, w_mine, w_other = late
-    loss = jnp.concatenate([early_loss[0], late_loss[0]])
+    first, second = images[:4], images[4:6]
+    loss_a, coeffs_a, low_a, back_a = tile(scalars, numbers, first, w_img, texts)
+    below, above, back_a = lax.optimization_barrier((images[5], images[6], back_a))
+    last = [images[6], *gather_last(below, above)]
+    loss_b, coeffs_b, low_b, back_b = tile(scalars, numbers, second, w_img, texts)
+    early = (first + second, (back_a, back_b))
+    loss_c, coeffs_c, low_c, w_mine, w_other = tile(scalars, numbers, last, w_img, texts, early)
+    loss = jnp.concatenate([loss_a[0], loss_b[0], loss_c[0]])
     w = w_mine + flip(w_other, "core", NC).astype(F32)
-    late_coeffs, w = lax.optimization_barrier((late_coeffs, w))
-    t_mine, t_other = text_directions((early_coeffs, late_coeffs), (early_low, late_low))
+    coeffs_c, w = lax.optimization_barrier((coeffs_c, w))
+    t_mine, t_other = text_directions((coeffs_a, coeffs_b, coeffs_c), (low_a, low_b, low_c))
     t_sum = t_mine.astype(F32) + flip(t_other, "core", NC).astype(F32)
     blocks = t_sum.astype(BF).reshape(NX * NY, ROWS, D_EMB)
     weight_sum, losses, blocks = sum_weight(w, in_order(loss, z), blocks)

time: 168 us -> 165 us (0.982)
  waiting for transfers between devices: 54.9 us -> 50.6 us
  Pallas kernels: 39.3 us -> 42.8 us
  starting transfers between devices: 46.7 us -> 43.9 us
  local copies, waits for them, and re-layouts: 6.57 us -> 8.52 us
  other arithmetic: 17.3 us -> 15.6 us
    ppermute x8, waiting for transfers between devices: 23 us -> 17.4 us  [shift(): return lax.ppermute(x, axis, [(i, (i + by) % n) for i in range(n)])]
    pallas_call x3 -> x4, Pallas kernels: 39.3 us -> 42.8 us  [the longest x3 33.8 us: tile(): pl.pallas_call(functools.partial(tile_kernel, len(images), len(early[0])...]
    ppermute x13, starting transfers between devices: 22.9 us -> 19.6 us  [flip(): return lax.ppermute(x, axis, [(i, i ^ bit) for i in range(n)])]
  transfers between devices with their start and end apart: 23 -> 23, of which waited for: 13 -> 10; matrix products, arithmetic and copies ran while one was open for 9% -> 9% of each run, Pallas kernels for 13% -> 18%
where the time goes in v3:
time: 165 us; the launch traced here: 164 us
  waiting for transfers between devices  50.6 us (31%)
  starting transfers between devices  43.9 us (27%)
  Pallas kernels  42.8 us (26%)
  other arithmetic  15.6 us (9%)
  local copies, waits for them, and re-layouts  8.52 us (5%)
  between operations  2.59 us (2%)
    pallas_call x3, Pallas kernels, tile(): pl.pallas_call(functools.partial(tile_kernel, len(images), len(early[0])...  33.8 us
    ppermute x13, waiting for transfers between devices, flip(): return lax.ppermute(x, axis, [(i, i ^ bit) for i in range(n)])  21.6 us
    ppermute x13, starting transfers between devices, flip(): return lax.ppermute(x, axis, [(i, i ^ bit) for i in range(n)])  19.6 us
    ppermute x8, waiting for transfers between devices, shift(): return lax.ppermute(x, axis, [(i, (i + by) % n) for i in range(n)])  17.4 us
    ppermute x8, starting transfers between devices, shift(): return lax.ppermute(x, axis, [(i, (i + by) % n) for i in range(n)])  14.6 us
    all_to_all x2, waiting for transfers between devices, exchange(): return lax.all_to_all(x, axes, 0, 0)  11.6 us
    all_to_all x2, starting transfers between devices, exchange(): return lax.all_to_all(x, axes, 0, 0)  9.68 us
    pallas_call x1, Pallas kernels, text_directions(): pl.pallas_call(text_kernel, grid=(TEXTS // block,), in_specs=[*map(column...  9.06 us
  transfers between devices with their start and end apart: 23, of which 10 were waited for; matrix products, arithmetic and copies ran while one was open for 9% of the time, Pallas kernels for 18%

profile of v3, /device:TPU:1, one launch (start us, length us, event | category | flops | bytes accessed | tf_op | source)
XLA Modules:
  0.0 164.1 jit_solution(12556399325513567817)
XLA Ops:
  0.6 1.1 fusion.6
  1.7 0.5 copy-done.8
  2.2 1.1 fusion.4
  3.3 1.6 broadcast_in_dim.33
  4.9 6.1 %all-to-all-start = ((bf16[8,128,1024]{2,1,0:T(8,128)(2,1)}), bf16[8,128,1024]{2,1,0:T(8,128)(2,1)S(1)}, u32[]{:S(2)}, u32[]{:S(2)}) async-start(bf16[8,128,1024]{2,1,0:T(8,128)(2,1)} %broadcast_in_dim.33), calls=%async_computation | async-start | bytes 4194304 | tf_op jit(solution)/shard_map/all_to_all | solution.py:35
  11.1 0.1 select_convert_fusion
  11.2 1.7 %collective-permute-start = (bf16[128,1664]{1,0:T(8,128)(2,1)S(1)}, bf16[128,1664]{1,0:T(8,128)(2,1)S(1)}, u32[]{:S(2)}, u32[]{:S(2)}) collective-permute-start(bf16[128,1664]{1,0:T(8,128)(2,1)S(1)} %pad_maximum_fusion.refs_0_.refs_6_), channel_id=1, source_target_pairs={{0,32},{32,64},{64,96},{96,128},{128,160},{160,192},{192,224},{224... | collective-permute-start | bytes 1277960 | tf_op jit(solution)/shard_map/ppermute | solution.py:27
  12.9 4.0 %collective-permute-start.1 = (bf16[128,1664]{1,0:T(8,128)(2,1)S(1)}, bf16[128,1664]{1,0:T(8,128)(2,1)S(1)}, u32[]{:S(2)}, u32[]{:S(2)}) collective-permute-start(bf16[128,1664]{1,0:T(8,128)(2,1)S(1)} %pad_maximum_fusion.refs_0_.refs_6_), channel_id=1, source_target_pairs={{0,224},{32,0},{64,32},{96,64},{128,96},{160,128},{192,160},{224,1... | collective-permute-start | bytes 1277960 | tf_op jit(solution)/shard_map/ppermute | solution.py:27
  17.0 9.1 %collective-permute-done.refs_1_.refs_7_ = bf16[128,1664]{1,0:T(8,128)(2,1)S(1)} collective-permute-done((bf16[128,1664]{1,0:T(8,128)(2,1)S(1)}, bf16[128,1664]{1,0:T(8,128)(2,1)S(1)}, u32[]{:S(2)}, u32[]{:S(2)}) %collective-permute-start) | collective-permute-done | bytes 426016 | tf_op jit(solution)/shard_map/ppermute | solution.py:27
  26.1 0.1 collective-permute-start.2
  26.2 2.7 %collective-permute-start.3 = (bf16[128,1664]{1,0:T(8,128)(2,1)S(1)}, bf16[128,1664]{1,0:T(8,128)(2,1)}, u32[]{:S(2)}, u32[]{:S(2)}) collective-permute-start(bf16[128,1664]{1,0:T(8,128)(2,1)S(1)} %collective-permute-done.1.refs_2_.refs_8_), channel_id=1, source_target_pairs={{0,224},{32,0},{64,32},{96,64},{128,96},{160,128},{192,160},{224,1... | collective-permute-start | bytes 1277960 | tf_op jit(solution)/shard_map/ppermute | solution.py:27
  28.9 8.3 %collective-permute-done.2.refs_3_.refs_9_ = bf16[128,1664]{1,0:T(8,128)(2,1)S(1)} collective-permute-done((bf16[128,1664]{1,0:T(8,128)(2,1)S(1)}, bf16[128,1664]{1,0:T(8,128)(2,1)S(1)}, u32[]{:S(2)}, u32[]{:S(2)}) %collective-permute-start.2) | collective-permute-done | bytes 426016 | tf_op jit(solution)/shard_map/ppermute | solution.py:27
  37.2 0.8 copy-done.12
  37.9 2.6 %collective-permute-start.4 = (bf16[1024,1024]{1,0:T(8,128)(2,1)S(1)}, bf16[1024,1024]{1,0:T(8,128)(2,1)}, u32[]{:S(2)}, u32[]{:S(2)}) collective-permute-start(bf16[1024,1024]{1,0:T(8,128)(2,1)S(1)} %bitcast.111), channel_id=1, source_target_pairs={{0,2},{2,0},{1,3},{3,1},{4,6},{6,4},{5,7},{7,5},{8,10},{10,8},{9,1... | collective-permute-start | bytes 6291464 | tf_op jit(solution)/shard_map/ppermute | solution.py:31
  41.8 0.6 pad_maximum_fusion.4.scalars
  42.4 0.6 pad_add_fusion.numbers
  43.0 0.7 collective-permute-start.5
  43.8 2.4 %collective-permute-start.6 = (bf16[128,1664]{1,0:T(8,128)(2,1)}, bf16[128,1664]{1,0:T(8,128)(2,1)S(1)}, u32[]{:S(2)}, u32[]{:S(2)}) collective-permute-start(bf16[128,1664]{1,0:T(8,128)(2,1)} %collective-permute-done.3.refs_0_.refs_10_), channel_id=1, source_target_pairs={{0,224},{32,0},{64,32},{96,64},{128,96},{160,128},{192,160},{224,1... | collective-permute-start | bytes 1277960 | tf_op jit(solution)/shard_map/ppermute | solution.py:27
  46.1 12.1 %shard_map.94 = (f32[8,512]{1,0:T(8,128)}, bf16[512,2048]{1,0:T(8,128)(2,1)}, bf16[512,1024]{1,0:T(8,128)(2,1)}, bf16[512,1024]{1,0:T(8,128)(2,1)}) custom-call(f32[2]{0:T(128)} %pad_maximum_fusion.4.scalars, s32[17]{0:T(128)} %pad_add_fusion.numbers, bf16[128,1664]{1,0:T(8,128)(2,1)} %copy-done.3, bf16[128,1664]{1,0:T(8,128)(2,1)} %copy-done.10, ...), custom_call_target="tpu_custom_call" | custom-call | flops 5905580032 | bytes 16777216 | tf_op jit(solution)/shard_map/pallas_call | solution.py:242
  58.3 0.1 collective-permute-start.7
  58.5 2.9 %collective-permute-start.8 = (bf16[64,1664]{1,0:T(8,128)(2,1)S(1)}, bf16[64,1664]{1,0:T(8,128)(2,1)S(1)}, u32[]{:S(2)}, u32[]{:S(2)}) collective-permute-start(bf16[64,1664]{1,0:T(8,128)(2,1)S(1)} %slice.89), channel_id=1, source_target_pairs={{0,224},{32,0},{64,32},{96,64},{128,96},{160,128},{192,160},{224,1... | collective-permute-start | bytes 638984 | tf_op jit(solution)/shard_map/ppermute | solution.py:27
  61.4 8.0 %shard_map.95 = (f32[8,256]{1,0:T(8,128)}, bf16[256,2048]{1,0:T(8,128)(2,1)}, bf16[256,1024]{1,0:T(8,128)(2,1)}, bf16[256,1024]{1,0:T(8,128)(2,1)}) custom-call(f32[2]{0:T(128)} %pad_maximum_fusion.4.scalars, s32[17]{0:T(128)} %pad_add_fusion.numbers, bf16[128,1664]{1,0:T(8,128)(2,1)} %collective-permute-done.3.refs_0_.refs_10_, ...), custom_call_target="tpu_custom_call" | custom-call | flops 2952790016 | bytes 16777216 | tf_op jit(solution)/shard_map/pallas_call | solution.py:242
  69.4 0.7 copy-done.13
  70.1 13.6 %shard_map.96 = (f32[8,256]{1,0:T(8,128)}, bf16[256,2048]{1,0:T(8,128)(2,1)}, bf16[256,1024]{1,0:T(8,128)(2,1)}, f32[1536,512]{1,0:T(8,128)}, bf16[1536,512]{1,0:T(8,128)(2,1)}) custom-call(f32[2]{0:T(128)} %pad_maximum_fusion.4.scalars, s32[17]{0:T(128)} %pad_add_fusion.numbers, bf16[128,1664]{1,0:T(8,128)(2,1)} %copy-done.6, bf16[64,1664]{1,0:T(8,128)(2,1)} %copy-done.13, ...), custom_call_target="tpu_custom_call" | custom-call | flops 6174015488 | bytes 16777216 | tf_op jit(solution)/shard_map/pallas_call | solution.py:242
  83.8 0.9 collective-permute-start.9
  84.7 0.7 fusion.35
  85.4 0.7 fusion.34
  86.1 0.7 fusion.36
  86.9 0.6 constant_dynamic-slice_fusion.13
  87.5 0.4 collective-permute-done.9
  87.9 2.4 %convert_add_fusion = f32[1536,512]{1,0:T(8,128)S(1)} fusion(f32[1536,512]{1,0:T(8,128)} %get-tuple-element.44, bf16[1536,512]{1,0:T(8,128)(2,1)S(1)} %collective-permute-done.9), kind=kLoop, calls=%fused_computation.2 | loop fusion | flops 1572864 | bytes 7864320 | tf_op jit(solution)/shard_map/add | solution.py:316
  90.4 0.4 fusion.33
  90.8 0.8 pad_maximum_fusion.1
  91.6 2.8 %collective-permute-start.12 = (bf16[2,2,2,2,2,24,256]{6,5,4,3,1,0,2:T(8,128)(2,1)S(1)}, bf16[2,2,2,2,2,24,256]{6,5,4,3,1,0,2:T(8,128)(2,1)}, u32[]{:S(2)}, u32[]{:S(2)}) collective-permute-start(bf16[2,2,2,2,2,24,256]{6,5,4,3,1,0,2:T(8,128)(2,1)S(1)} %fusion.10), channel_id=1, source_target_pairs={{0,8},{4,12},{8,0},{12,4},{1,9},{5,13},{9,1},{13,5},{2,10},{6,14},... | collective-permute-start | bytes 1179656 | tf_op jit(solution)/shard_map/ppermute | solution.py:31
  94.4 9.1 %shard_map.97 = (bf16[1024,1024]{1,0:T(8,128)(2,1)}, bf16[1024,1024]{1,0:T(8,128)(2,1)}) custom-call(bf16[512,2048]{1,0:T(8,128)(2,1)} %get-tuple-element.47.refs_0_, bf16[256,2048]{1,0:T(8,128)(2,1)} %get-tuple-element.48.refs_1_, bf16[256,2048]{1,0:T(8,128)(2,1)} %get-tuple-element.49.refs_2_, bf16[512,1024]{1,0:T(8,128)(2,1)} %get-tuple-element.50.refs_3_, ...), custom_call_target="tpu_custom_call" | custom-call | flops 4294967296 | bytes 10485760 | tf_op jit(solution)/shard_map/pallas_call | solution.py:275
  103.5 0.7 collective-permute-start.19
  104.2 1.1 fusion
  105.3 1.8 %collective-permute-start.13 = (bf16[2,2,2,2,24,256]{5,4,3,2,1,0:T(8,128)(2,1)S(1)}, bf16[2,2,2,2,24,256]{5,4,3,2,1,0:T(8,128)(2,1)S(1)}, u32[]{:S(2)}, u32[]{:S(2)}) collective-permute-start(bf16[2,2,2,2,24,256]{5,4,3,2,1,0:T(8,128)(2,1)S(1)} %fusion.17), channel_id=1, source_target_pairs={{0,32},{32,0},{64,96},{96,64},{128,160},{160,128},{192,224},{224,1... | collective-permute-start | bytes 589832 | tf_op jit(solution)/shard_map/ppermute | solution.py:31
  107.1 1.0 slice.108
  108.2 0.1 convert_add_fusion.1
  108.3 0.7 slice_convert_fusion
  109.0 1.7 %collective-permute-start.11 = (bf16[2,2,2,2,24,256]{5,4,3,2,1,0:T(8,128)(2,1)S(1)}, bf16[2,2,2,2,24,256]{5,4,3,2,1,0:T(8,128)(2,1)S(1)}, u32[]{:S(2)}, u32[]{:S(2)}) collective-permute-start(bf16[2,2,2,2,24,256]{5,4,3,2,1,0:T(8,128)(2,1)S(1)} %fusion.16), channel_id=1, source_target_pairs={{0,8},{4,12},{8,0},{12,4},{1,9},{5,13},{9,1},{13,5},{2,10},{6,14},... | collective-permute-start | bytes 589832 | tf_op jit(solution)/shard_map/ppermute | solution.py:31
  110.7 0.8 collective-permute-done.13
  111.5 4.6 %collective-permute-done.11 = bf16[2,2,2,2,24,256]{5,4,3,2,1,0:T(8,128)(2,1)S(1)} collective-permute-done((bf16[2,2,2,2,24,256]{5,4,3,2,1,0:T(8,128)(2,1)S(1)}, bf16[2,2,2,2,24,256]{5,4,3,2,1,0:T(8,128)(2,1)S(1)}, u32[]{:S(2)}, u32[]{:S(2)}) %collective-permute-start.11) | collective-permute-done | bytes 196640 | tf_op jit(solution)/shard_map/ppermute | solution.py:31
  116.2 0.1 collective-permute-start.14
  116.3 4.5 %collective-permute-done.14 = bf16[2,2,2,24,512]{4,3,2,1,0:T(8,128)(2,1)S(1)} collective-permute-done((bf16[2,2,2,24,512]{4,3,2,1,0:T(8,128)(2,1)S(1)}, bf16[2,2,2,24,512]{4,3,2,1,0:T(8,128)(2,1)S(1)}, u32[]{:S(2)}, u32[]{:S(2)}) %collective-permute-start.14) | collective-permute-done | bytes 196640 | tf_op jit(solution)/shard_map/ppermute | solution.py:31
  120.9 1.3 collective-permute-start.15
  122.2 2.2 %collective-permute-done.15 = bf16[2,2,24,512]{3,2,1,0:T(8,128)(2,1)S(1)} collective-permute-done((bf16[2,2,24,512]{3,2,1,0:T(8,128)(2,1)S(1)}, bf16[2,2,24,512]{3,2,1,0:T(8,128)(2,1)S(1)}, u32[]{:S(2)}, u32[]{:S(2)}) %collective-permute-start.15) | collective-permute-done | bytes 98336 | tf_op jit(solution)/shard_map/ppermute | solution.py:31
  124.5 0.2 copy.38
  124.7 2.5 %collective-permute-start.16 = (f32[2,2,2,6,512]{4,2,3,1,0:T(2,128)S(1)}, f32[2,2,2,6,512]{4,2,3,1,0:T(2,128)S(1)}, u32[]{:S(2)}, u32[]{:S(2)}) collective-permute-start(f32[2,2,2,6,512]{4,2,3,1,0:T(2,128)S(1)} %bitcast.119), channel_id=1, source_target_pairs={{0,1},{1,0},{2,3},{3,2},{4,5},{5,4},{6,7},{7,6},{8,9},{9,8},{10,11... | collective-permute-start | bytes 294920 | tf_op jit(solution)/shard_map/ppermute | solution.py:31
  127.3 3.9 %add_convert_fusion = bf16[1024,1024]{1,0:T(8,128)(2,1)} fusion(bf16[1024,1024]{1,0:T(8,128)(2,1)} %collective-permute-done.19, bf16[1024,1024]{1,0:T(8,128)(2,1)S(1)} %copy-done.1), kind=kLoop, calls=%fused_computation.1 | loop fusion | flops 4194304 | bytes 6291456 | tf_op jit(solution)/shard_map/convert_element_type | solution.py:320
  131.2 3.6 %all-to-all-start.1 = ((bf16[8,128,1024]{2,1,0:T(8,128)(2,1)}), bf16[8,128,1024]{2,1,0:T(8,128)(2,1)S(1)}, u32[]{:S(2)}, u32[]{:S(2)}) async-start(bf16[8,128,1024]{2,1,0:T(8,128)(2,1)} %bitcast.33), calls=%async_computation.1 | async-start | bytes 4194304 | tf_op jit(solution)/shard_map/all_to_all | solution.py:35
  134.8 0.1 bitcast_add_fusion.3
  135.0 0.1 collective-permute-start.17
  135.1 4.8 %collective-permute-done.17 = f32[40,512]{1,0:T(8,128)S(1)} collective-permute-done((f32[40,512]{1,0:T(8,128)S(1)}, f32[40,512]{1,0:T(8,128)S(1)}, u32[]{:S(2)}, u32[]{:S(2)}) %collective-permute-start.17) | collective-permute-done | bytes 81952 | tf_op jit(solution)/shard_map/ppermute | solution.py:31
  140.1 3.2 %collective-permute-start.18 = (f32[28,512]{1,0:T(8,128)S(1)}, f32[28,512]{1,0:T(8,128)S(1)}, u32[]{:S(2)}, u32[]{:S(2)}) collective-permute-start(f32[28,512]{1,0:T(8,128)S(1)} %pad_maximum_fusion.3), channel_id=1, source_target_pairs={{0,128},{32,160},{64,192},{96,224},{128,0},{160,32},{192,64},{224,... | collective-permute-start | bytes 172040 | tf_op jit(solution)/shard_map/ppermute | solution.py:31
  143.3 4.3 %collective-permute-done.18 = f32[28,512]{1,0:T(8,128)S(1)} collective-permute-done((f32[28,512]{1,0:T(8,128)S(1)}, f32[28,512]{1,0:T(8,128)S(1)}, u32[]{:S(2)}, u32[]{:S(2)}) %collective-permute-start.18) | collective-permute-done | bytes 57376 | tf_op jit(solution)/shard_map/ppermute | solution.py:31
  147.7 0.5 fusion.31
  148.3 11.6 %all-to-all-done.1 = bf16[8,128,1024]{2,1,0:T(8,128)(2,1)S(1)} async-done(((bf16[8,128,1024]{2,1,0:T(8,128)(2,1)}), bf16[8,128,1024]{2,1,0:T(8,128)(2,1)S(1)}, u32[]{:S(2)}, u32[]{:S(2)}) %all-to-all-start.1) | async-done | bytes 2097184 | tf_op jit(solution)/shard_map/all_to_all | solution.py:35
  159.9 2.0 %collective-permute-start.20 = (f32[6,512]{1,0:T(8,128)S(1)}, f32[6,512]{1,0:T(8,128)S(1)}, u32[]{:S(2)}, u32[]{:S(2)}) collective-permute-start(f32[6,512]{1,0:T(8,128)S(1)} %bitcast.122), channel_id=1, source_target_pairs={{0,2},{2,0},{1,3},{3,1},{4,6},{6,4},{5,7},{7,5},{8,10},{10,8},{9,1... | collective-permute-start | bytes 36872 | tf_op jit(solution)/shard_map/ppermute | solution.py:31
  161.8 0.3 convert_reduce_fusion
  162.2 0.2 fusion.5
  162.4 1.0 fusion.9
  163.4 0.6 fusion.20
  (99 shorter events, 1.1 us)
Async XLA Ops:
  1.7 0.5 copy-start.8
  4.9 6.1 %copy-start.15 = (s32[1,128]{1,0:T(1,128)S(1)}, s32[1,128]{1,0:T(1,128)}, u32[]{:S(2)}) copy-start(s32[1,128]{1,0:T(1,128)} %param.10) | copy-start | bytes 1540
  4.9 6.2 %copy-start.4 = (bf16[1,128,1536]{2,1,0:T(8,128)(2,1)S(1)}, bf16[1,128,1536]{2,1,0:T(8,128)(2,1)}, u32[]{:S(2)}) copy-start(bf16[1,128,1536]{2,1,0:T(8,128)(2,1)} %param.7) | copy-start | bytes 1179652
  4.9 33.0 %all-to-all-start = ((bf16[8,128,1024]{2,1,0:T(8,128)(2,1)}), bf16[8,128,1024]{2,1,0:T(8,128)(2,1)S(1)}, u32[]{:S(2)}, u32[]{:S(2)}) async-start(bf16[8,128,1024]{2,1,0:T(8,128)(2,1)} %broadcast_in_dim.33), calls=%async_computation | async-start | bytes 4194304 | tf_op jit(solution)/shard_map/all_to_all | solution.py:35
  11.2 34.9 %copy-start.3 = (bf16[128,1664]{1,0:T(8,128)(2,1)}, bf16[128,1664]{1,0:T(8,128)(2,1)S(1)}, u32[]{:S(2)}) copy-start(bf16[128,1664]{1,0:T(8,128)(2,1)S(1)} %pad_maximum_fusion.refs_0_.refs_6_) | copy-start | bytes 1277956
  11.2 14.9 %collective-permute-start = (bf16[128,1664]{1,0:T(8,128)(2,1)S(1)}, bf16[128,1664]{1,0:T(8,128)(2,1)S(1)}, u32[]{:S(2)}, u32[]{:S(2)}) collective-permute-start(bf16[128,1664]{1,0:T(8,128)(2,1)S(1)} %pad_maximum_fusion.refs_0_.refs_6_), channel_id=1, source_target_pairs={{0,32},{32,64},{64,96},{96,128},{128,160},{160,192},{192,224},{224... | collective-permute-start | bytes 1277960 | tf_op jit(solution)/shard_map/ppermute | solution.py:27
  12.9 13.2 %collective-permute-start.1 = (bf16[128,1664]{1,0:T(8,128)(2,1)S(1)}, bf16[128,1664]{1,0:T(8,128)(2,1)S(1)}, u32[]{:S(2)}, u32[]{:S(2)}) collective-permute-start(bf16[128,1664]{1,0:T(8,128)(2,1)S(1)} %pad_maximum_fusion.refs_0_.refs_6_), channel_id=1, source_target_pairs={{0,224},{32,0},{64,32},{96,64},{128,96},{160,128},{192,160},{224,1... | collective-permute-start | bytes 1277960 | tf_op jit(solution)/shard_map/ppermute | solution.py:27
  26.1 20.0 %copy-start.10 = (bf16[128,1664]{1,0:T(8,128)(2,1)}, bf16[128,1664]{1,0:T(8,128)(2,1)S(1)}, u32[]{:S(2)}) copy-start(bf16[128,1664]{1,0:T(8,128)(2,1)S(1)} %collective-permute-done.refs_1_.refs_7_) | copy-start | bytes 1277956
  26.1 20.0 %copy-start.11 = (bf16[128,1664]{1,0:T(8,128)(2,1)}, bf16[128,1664]{1,0:T(8,128)(2,1)S(1)}, u32[]{:S(2)}) copy-start(bf16[128,1664]{1,0:T(8,128)(2,1)S(1)} %collective-permute-done.1.refs_2_.refs_8_) | copy-start | bytes 1277956
  26.1 11.0 %collective-permute-start.2 = (bf16[128,1664]{1,0:T(8,128)(2,1)S(1)}, bf16[128,1664]{1,0:T(8,128)(2,1)S(1)}, u32[]{:S(2)}, u32[]{:S(2)}) collective-permute-start(bf16[128,1664]{1,0:T(8,128)(2,1)S(1)} %collective-permute-done.refs_1_.refs_7_), channel_id=1, source_target_pairs={{0,32},{32,64},{64,96},{96,128},{128,160},{160,192},{192,224},{224... | collective-permute-start | bytes 1277960 | tf_op jit(solution)/shard_map/ppermute | solution.py:27
  26.2 11.7 %collective-permute-start.3 = (bf16[128,1664]{1,0:T(8,128)(2,1)S(1)}, bf16[128,1664]{1,0:T(8,128)(2,1)}, u32[]{:S(2)}, u32[]{:S(2)}) collective-permute-start(bf16[128,1664]{1,0:T(8,128)(2,1)S(1)} %collective-permute-done.1.refs_2_.refs_8_), channel_id=1, source_target_pairs={{0,224},{32,0},{64,32},{96,64},{128,96},{160,128},{192,160},{224,1... | collective-permute-start | bytes 1277960 | tf_op jit(solution)/shard_map/ppermute | solution.py:27
  37.1 0.8 copy-start.12
  37.9 8.2 %copy-start.2 = (bf16[8,128,1024]{2,1,0:T(8,128)(2,1)}, bf16[8,128,1024]{2,1,0:T(8,128)(2,1)S(1)}, u32[]{:S(2)}) copy-start(bf16[8,128,1024]{2,1,0:T(8,128)(2,1)S(1)} %all-to-all-done) | copy-start | bytes 6291460
  37.9 8.2 %collective-permute-start.4 = (bf16[1024,1024]{1,0:T(8,128)(2,1)S(1)}, bf16[1024,1024]{1,0:T(8,128)(2,1)}, u32[]{:S(2)}, u32[]{:S(2)}) collective-permute-start(bf16[1024,1024]{1,0:T(8,128)(2,1)S(1)} %bitcast.111), channel_id=1, source_target_pairs={{0,2},{2,0},{1,3},{3,1},{4,6},{6,4},{5,7},{7,5},{8,10},{10,8},{9,1... | collective-permute-start | bytes 6291464 | tf_op jit(solution)/shard_map/ppermute | solution.py:31
  43.0 15.3 %collective-permute-start.5 = (bf16[128,1664]{1,0:T(8,128)(2,1)}, bf16[128,1664]{1,0:T(8,128)(2,1)S(1)}, u32[]{:S(2)}, u32[]{:S(2)}) collective-permute-start(bf16[128,1664]{1,0:T(8,128)(2,1)} %copy-done.12), channel_id=1, source_target_pairs={{0,32},{32,64},{64,96},{96,128},{128,160},{160,192},{192,224},{224... | collective-permute-start | bytes 1277960 | tf_op jit(solution)/shard_map/ppermute | solution.py:27
  43.8 14.5 %collective-permute-start.6 = (bf16[128,1664]{1,0:T(8,128)(2,1)}, bf16[128,1664]{1,0:T(8,128)(2,1)S(1)}, u32[]{:S(2)}, u32[]{:S(2)}) collective-permute-start(bf16[128,1664]{1,0:T(8,128)(2,1)} %collective-permute-done.3.refs_0_.refs_10_), channel_id=1, source_target_pairs={{0,224},{32,0},{64,32},{96,64},{128,96},{160,128},{192,160},{224,1... | collective-permute-start | bytes 1277960 | tf_op jit(solution)/shard_map/ppermute | solution.py:27
  58.3 3.1 %copy-start.5 = (bf16[128,1664]{1,0:T(8,128)(2,1)}, bf16[128,1664]{1,0:T(8,128)(2,1)S(1)}, u32[]{:S(2)}) copy-start(bf16[128,1664]{1,0:T(8,128)(2,1)S(1)} %collective-permute-done.5.refs_1_.refs_11_) | copy-start | bytes 1277956
  58.3 11.1 %copy-start.6 = (bf16[128,1664]{1,0:T(8,128)(2,1)}, bf16[128,1664]{1,0:T(8,128)(2,1)S(1)}, u32[]{:S(2)}) copy-start(bf16[128,1664]{1,0:T(8,128)(2,1)S(1)} %collective-permute-done.6.refs_0_) | copy-start | bytes 1277956
  58.3 11.1 %collective-permute-start.7 = (bf16[64,1664]{1,0:T(8,128)(2,1)S(1)}, bf16[64,1664]{1,0:T(8,128)(2,1)S(1)}, u32[]{:S(2)}, u32[]{:S(2)}) collective-permute-start(bf16[64,1664]{1,0:T(8,128)(2,1)S(1)} %slice.88), channel_id=1, source_target_pairs={{0,32},{32,64},{64,96},{96,128},{128,160},{160,192},{192,224},{224... | collective-permute-start | bytes 638984 | tf_op jit(solution)/shard_map/ppermute | solution.py:27
  58.5 10.9 %collective-permute-start.8 = (bf16[64,1664]{1,0:T(8,128)(2,1)S(1)}, bf16[64,1664]{1,0:T(8,128)(2,1)S(1)}, u32[]{:S(2)}, u32[]{:S(2)}) collective-permute-start(bf16[64,1664]{1,0:T(8,128)(2,1)S(1)} %slice.89), channel_id=1, source_target_pairs={{0,224},{32,0},{64,32},{96,64},{128,96},{160,128},{192,160},{224,1... | collective-permute-start | bytes 638984 | tf_op jit(solution)/shard_map/ppermute | solution.py:27
  69.4 0.7 copy-start.13
  69.4 0.7 copy-start.14
  83.8 4.2 %collective-permute-start.9 = (bf16[1536,512]{1,0:T(8,128)(2,1)}, bf16[1536,512]{1,0:T(8,128)(2,1)S(1)}, u32[]{:S(2)}, u32[]{:S(2)}) collective-permute-start(bf16[1536,512]{1,0:T(8,128)(2,1)} %get-tuple-element.45), channel_id=1, source_target_pairs={{0,2},{2,0},{1,3},{3,1},{4,6},{6,4},{5,7},{7,5},{8,10},{10,8},{9,1... | collective-permute-start | bytes 4718600 | tf_op jit(solution)/shard_map/ppermute | solution.py:31
  91.6 15.6 %collective-permute-start.10 = (bf16[784,256]{1,0:T(8,128)(2,1)}, bf16[784,256]{1,0:T(8,128)(2,1)}, u32[]{:S(2)}, u32[]{:S(2)}) collective-permute-start(bf16[784,256]{1,0:T(8,128)(2,1)} %pad_maximum_fusion.1), channel_id=1, source_target_pairs={{0,32},{32,0},{64,96},{96,64},{128,160},{160,128},{192,224},{224,1... | collective-permute-start | bytes 1204232 | tf_op jit(solution)/shard_map/ppermute | solution.py:31
  91.6 12.5 %collective-permute-start.12 = (bf16[2,2,2,2,2,24,256]{6,5,4,3,1,0,2:T(8,128)(2,1)S(1)}, bf16[2,2,2,2,2,24,256]{6,5,4,3,1,0,2:T(8,128)(2,1)}, u32[]{:S(2)}, u32[]{:S(2)}) collective-permute-start(bf16[2,2,2,2,2,24,256]{6,5,4,3,1,0,2:T(8,128)(2,1)S(1)} %fusion.10), channel_id=1, source_target_pairs={{0,8},{4,12},{8,0},{12,4},{1,9},{5,13},{9,1},{13,5},{2,10},{6,14},... | collective-permute-start | bytes 1179656 | tf_op jit(solution)/shard_map/ppermute | solution.py:31
  103.5 23.8 %collective-permute-start.19 = (bf16[1024,1024]{1,0:T(8,128)(2,1)}, bf16[1024,1024]{1,0:T(8,128)(2,1)}, u32[]{:S(2)}, u32[]{:S(2)}) collective-permute-start(bf16[1024,1024]{1,0:T(8,128)(2,1)} %get-tuple-element.54), channel_id=1, source_target_pairs={{0,2},{2,0},{1,3},{3,1},{4,6},{6,4},{5,7},{7,5},{8,10},{10,8},{9,1... | collective-permute-start | bytes 6291464 | tf_op jit(solution)/shard_map/ppermute | solution.py:31
  105.3 6.2 %collective-permute-start.13 = (bf16[2,2,2,2,24,256]{5,4,3,2,1,0:T(8,128)(2,1)S(1)}, bf16[2,2,2,2,24,256]{5,4,3,2,1,0:T(8,128)(2,1)S(1)}, u32[]{:S(2)}, u32[]{:S(2)}) collective-permute-start(bf16[2,2,2,2,24,256]{5,4,3,2,1,0:T(8,128)(2,1)S(1)} %fusion.17), channel_id=1, source_target_pairs={{0,32},{32,0},{64,96},{96,64},{128,160},{160,128},{192,224},{224,1... | collective-permute-start | bytes 589832 | tf_op jit(solution)/shard_map/ppermute | solution.py:31
  108.3 8.0 %copy-start.7 = (f32[2,2,1,128]{3,2,1,0:T(1,128)S(1)}, f32[2,2,1,128]{3,2,1,0:T(1,128)}, u32[]{:S(2)}) copy-start(f32[2,2,1,128]{3,2,1,0:T(1,128)} %get-tuple-element.71) | copy-start | bytes 6148
  109.0 7.1 %collective-permute-start.11 = (bf16[2,2,2,2,24,256]{5,4,3,2,1,0:T(8,128)(2,1)S(1)}, bf16[2,2,2,2,24,256]{5,4,3,2,1,0:T(8,128)(2,1)S(1)}, u32[]{:S(2)}, u32[]{:S(2)}) collective-permute-start(bf16[2,2,2,2,24,256]{5,4,3,2,1,0:T(8,128)(2,1)S(1)} %fusion.16), channel_id=1, source_target_pairs={{0,8},{4,12},{8,0},{12,4},{1,9},{5,13},{9,1},{13,5},{2,10},{6,14},... | collective-permute-start | bytes 589832 | tf_op jit(solution)/shard_map/ppermute | solution.py:31
  116.1 11.1 %copy-start.1 = (bf16[1024,1024]{1,0:T(8,128)(2,1)S(1)}, bf16[1024,1024]{1,0:T(8,128)(2,1)}, u32[]{:S(2)}) copy-start(bf16[1024,1024]{1,0:T(8,128)(2,1)} %get-tuple-element.53) | copy-start | bytes 6291460
  116.2 4.6 %collective-permute-start.14 = (bf16[2,2,2,24,512]{4,3,2,1,0:T(8,128)(2,1)S(1)}, bf16[2,2,2,24,512]{4,3,2,1,0:T(8,128)(2,1)S(1)}, u32[]{:S(2)}, u32[]{:S(2)}) collective-permute-start(bf16[2,2,2,24,512]{4,3,2,1,0:T(8,128)(2,1)S(1)} %fusion.18), channel_id=1, source_target_pairs={{0,4},{4,0},{8,12},{12,8},{1,5},{5,1},{9,13},{13,9},{2,6},{6,2},{1... | collective-permute-start | bytes 589832 | tf_op jit(solution)/shard_map/ppermute | solution.py:31
  120.9 3.6 %collective-permute-start.15 = (bf16[2,2,24,512]{3,2,1,0:T(8,128)(2,1)S(1)}, bf16[2,2,24,512]{3,2,1,0:T(8,128)(2,1)S(1)}, u32[]{:S(2)}, u32[]{:S(2)}) collective-permute-start(bf16[2,2,24,512]{3,2,1,0:T(8,128)(2,1)S(1)} %fusion.19), channel_id=1, source_target_pairs={{0,16},{16,0},{1,17},{17,1},{2,18},{18,2},{3,19},{19,3},{4,20},{20... | collective-permute-start | bytes 294920 | tf_op jit(solution)/shard_map/ppermute | solution.py:31
  124.7 10.1 %collective-permute-start.16 = (f32[2,2,2,6,512]{4,2,3,1,0:T(2,128)S(1)}, f32[2,2,2,6,512]{4,2,3,1,0:T(2,128)S(1)}, u32[]{:S(2)}, u32[]{:S(2)}) collective-permute-start(f32[2,2,2,6,512]{4,2,3,1,0:T(2,128)S(1)} %bitcast.119), channel_id=1, source_target_pairs={{0,1},{1,0},{2,3},{3,2},{4,5},{5,4},{6,7},{7,6},{8,9},{9,8},{10,11... | collective-permute-start | bytes 294920 | tf_op jit(solution)/shard_map/ppermute | solution.py:31
  131.2 28.6 %all-to-all-start.1 = ((bf16[8,128,1024]{2,1,0:T(8,128)(2,1)}), bf16[8,128,1024]{2,1,0:T(8,128)(2,1)S(1)}, u32[]{:S(2)}, u32[]{:S(2)}) async-start(bf16[8,128,1024]{2,1,0:T(8,128)(2,1)} %bitcast.33), calls=%async_computation.1 | async-start | bytes 4194304 | tf_op jit(solution)/shard_map/all_to_all | solution.py:35
  134.9 27.2 %copy-start = (bf16[1,128,1024]{2,1,0:T(8,128)(2,1)S(1)}, bf16[1,128,1024]{2,1,0:T(8,128)(2,1)}, u32[]{:S(2)}) copy-start(bf16[1,128,1024]{2,1,0:T(8,128)(2,1)} %param.9) | copy-start | bytes 786436
  134.9 27.2 %copy-start.9 = (f32[128]{0:T(128)S(1)}, f32[128]{0:T(128)}, u32[]{:S(2)}) copy-start(f32[128]{0:T(128)} %copy-done.8) | copy-start | bytes 1540
  135.0 4.9 %collective-permute-start.17 = (f32[40,512]{1,0:T(8,128)S(1)}, f32[40,512]{1,0:T(8,128)S(1)}, u32[]{:S(2)}, u32[]{:S(2)}) collective-permute-start(f32[40,512]{1,0:T(8,128)S(1)} %pad_maximum_fusion.2), channel_id=1, source_target_pairs={{0,64},{32,96},{64,0},{96,32},{128,192},{160,224},{192,128},{224,1... | collective-permute-start | bytes 245768 | tf_op jit(solution)/shard_map/ppermute | solution.py:31
  140.1 7.5 %collective-permute-start.18 = (f32[28,512]{1,0:T(8,128)S(1)}, f32[28,512]{1,0:T(8,128)S(1)}, u32[]{:S(2)}, u32[]{:S(2)}) collective-permute-start(f32[28,512]{1,0:T(8,128)S(1)} %pad_maximum_fusion.3), channel_id=1, source_target_pairs={{0,128},{32,160},{64,192},{96,224},{128,0},{160,32},{192,64},{224,... | collective-permute-start | bytes 172040 | tf_op jit(solution)/shard_map/ppermute | solution.py:31
  159.9 3.6 %collective-permute-start.20 = (f32[6,512]{1,0:T(8,128)S(1)}, f32[6,512]{1,0:T(8,128)S(1)}, u32[]{:S(2)}, u32[]{:S(2)}) collective-permute-start(f32[6,512]{1,0:T(8,128)S(1)} %bitcast.122), channel_id=1, source_target_pairs={{0,2},{2,0},{1,3},{3,1},{4,6},{6,4},{5,7},{7,5},{8,10},{10,8},{9,1... | collective-permute-start | bytes 36872 | tf_op jit(solution)/shard_map/ppermute | solution.py:31

commit v4 on v3

--- a/solution.py
+++ b/solution.py
@@ -35,7 +35,7 @@
     return lax.all_to_all(x, axes, 0, 0)
 
 
-def gather(image, text):
+def gather(image, text, scalars, numbers):
     copies = jnp.broadcast_to(text, (NX * NY, *text.shape))
     near = exchange(copies, ("xl", "y")).reshape(NX * NY * ROWS, D_EMB)
     down, up = [image], [image]
@@ -45,9 +45,10 @@
         if k == 1:
             down[-1], up[-1], near = lax.optimization_barrier((down[-1], up[-1], near))
         elif k == 0:
-            down[-1], up[-1] = lax.optimization_barrier((down[-1], up[-1]))
+            tied = lax.optimization_barrier((down[-1], up[-1], scalars, numbers))
+            down[-1], up[-1], scalars, numbers = tied
     images = [image, down[1], up[1], down[2], up[2], down[3], up[3]]
-    return images, [near, flip(near, "core", NC)]
+    return images, [near, flip(near, "core", NC)], scalars, numbers
 
 
 def gather_last(below, above):
@@ -83,10 +84,10 @@
     half = D_EMB // 4
     z_bits = z // 4, lax.rem(z // 2, 2), lax.rem(z, 2)
     a, b = w[..., :half], w[..., half:]
-    a, losses = halve_both(a, 2, losses, z_bits[2], 1, BF)
+    a = halve(a, 2, z_bits[2], "z", NZ, 1, BF)
     b = halve(b, 4, y // 2, "y", NY, 2, BF)
     a = halve(a, 3, y // 2, "y", NY, 2, BF)
-    b = halve(b, 2, z_bits[2], "z", NZ, 1, BF)
+    b, losses = halve_both(b, 2, losses, z_bits[2], 1, BF)
     w = jnp.concatenate([a, b], axis=-1)
     blocks = exchange(blocks, ("xl", "y"))
     w = halve(w, 3, lax.rem(y, 2), "y", NY, 1, BF)
@@ -299,11 +300,10 @@
     raw = text_emb[0].astype(F32)
     text_inv = lax.rsqrt(jnp.sum(raw * raw, axis=-1, keepdims=True) + 1e-06)
     text_unit = raw * text_inv
-    images, texts = gather(own, text_unit.astype(BF))
-
     plane = np.arange(NX * NY, dtype=np.int32)
     starts = lambda c: ((z * NX * NY + plane) * NC + c) * ROWS
     numbers = jnp.concatenate([starts(core), starts(1 - core), core[None]]).astype(jnp.int32)
+    images, texts, scalars, numbers = gather(own, text_unit.astype(BF), scalars, numbers)
 
     first, second = images[:4], images[4:6]
     loss_a, coeffs_a, low_a, back_a = tile(scalars, numbers, first, w_img, texts)

time: 165 us -> 160 us (0.970)
  waiting for transfers between devices: 50.6 us -> 41.1 us
  starting transfers between devices: 43.9 us -> 50.3 us
    all_to_all x2, waiting for transfers between devices: 11.6 us -> 6.13 us  [exchange(): return lax.all_to_all(x, axes, 0, 0)]
    ppermute x13, starting transfers between devices: 19.6 us -> 24.2 us  [flip(): return lax.ppermute(x, axis, [(i, i ^ bit) for i in range(n)])]
    ppermute x8, waiting for transfers between devices: 17.4 us -> 15 us  [shift(): return lax.ppermute(x, axis, [(i, (i + by) % n) for i in range(n)])]
    ppermute x8, starting transfers between devices: 14.6 us -> 16.4 us  [shift(): return lax.ppermute(x, axis, [(i, (i + by) % n) for i in range(n)])]
  transfers between devices with their start and end apart: 23 -> 23, of which waited for: 10 -> 10; matrix products, arithmetic and copies ran while one was open for 9% -> 8% of each run, Pallas kernels for 18% -> 18%
where the time goes in v4:
time: 160 us; the launch traced here: 159 us
  starting transfers between devices  50.3 us (31%)
  Pallas kernels  42.7 us (27%)
  waiting for transfers between devices  41.1 us (26%)
  other arithmetic  14.2 us (9%)
  local copies, waits for them, and re-layouts  7.79 us (5%)
  between operations  2.55 us (2%)
    pallas_call x3, Pallas kernels, tile(): pl.pallas_call(functools.partial(tile_kernel, len(images), len(early[0])...  33.7 us
    ppermute x13, starting transfers between devices, flip(): return lax.ppermute(x, axis, [(i, i ^ bit) for i in range(n)])  24.2 us
    ppermute x13, waiting for transfers between devices, flip(): return lax.ppermute(x, axis, [(i, i ^ bit) for i in range(n)])  20 us
    ppermute x8, starting transfers between devices, shift(): return lax.ppermute(x, axis, [(i, (i + by) % n) for i in range(n)])  16.4 us
    ppermute x8, waiting for transfers between devices, shift(): return lax.ppermute(x, axis, [(i, (i + by) % n) for i in range(n)])  15 us
    all_to_all x2, starting transfers between devices, exchange(): return lax.all_to_all(x, axes, 0, 0)  9.68 us
    pallas_call x1, Pallas kernels, text_directions(): pl.pallas_call(text_kernel, grid=(TEXTS // block,), in_specs=[*map(column...  9.04 us
    all_to_all x2, waiting for transfers between devices, exchange(): return lax.all_to_all(x, axes, 0, 0)  6.13 us
  transfers between devices with their start and end apart: 23, of which 10 were waited for; matrix products, arithmetic and copies ran while one was open for 8% of the time, Pallas kernels for 18%

profile of v4, /device:TPU:1, one launch (start us, length us, event | category | flops | bytes accessed | tf_op | source)
XLA Modules:
  0.0 158.6 jit_solution(5346355266118672092)
XLA Ops:
  0.6 1.1 fusion.6
  1.7 1.1 fusion.4
  2.8 1.6 %broadcast_in_dim.33 = bf16[8,128,1024]{2,1,0:T(8,128)(2,1)} broadcast(bf16[128,1024]{1,0:T(8,128)(2,1)S(1)} %fusion.4), dimensions={1,2} | broadcast | bytes 2359296 | tf_op jit(solution)/shard_map/broadcast_in_dim | solution.py:39
  4.4 6.1 %all-to-all-start = ((bf16[8,128,1024]{2,1,0:T(8,128)(2,1)}), bf16[8,128,1024]{2,1,0:T(8,128)(2,1)S(1)}, u32[]{:S(2)}, u32[]{:S(2)}) async-start(bf16[8,128,1024]{2,1,0:T(8,128)(2,1)} %broadcast_in_dim.33), calls=%async_computation | async-start | bytes 4194304 | tf_op jit(solution)/shard_map/all_to_all | solution.py:35
  10.5 0.1 select_convert_fusion
  10.7 1.7 %collective-permute-start = (bf16[128,1664]{1,0:T(8,128)(2,1)S(1)}, bf16[128,1664]{1,0:T(8,128)(2,1)S(1)}, u32[]{:S(2)}, u32[]{:S(2)}) collective-permute-start(bf16[128,1664]{1,0:T(8,128)(2,1)S(1)} %pad_maximum_fusion.refs_0_.refs_6_), channel_id=1, source_target_pairs={{0,32},{32,64},{64,96},{96,128},{128,160},{160,192},{192,224},{224... | collective-permute-start | bytes 1277960 | tf_op jit(solution)/shard_map/ppermute | solution.py:27
  12.4 4.0 %collective-permute-start.1 = (bf16[128,1664]{1,0:T(8,128)(2,1)S(1)}, bf16[128,1664]{1,0:T(8,128)(2,1)S(1)}, u32[]{:S(2)}, u32[]{:S(2)}) collective-permute-start(bf16[128,1664]{1,0:T(8,128)(2,1)S(1)} %pad_maximum_fusion.refs_0_.refs_6_), channel_id=1, source_target_pairs={{0,224},{32,0},{64,32},{96,64},{128,96},{160,128},{192,160},{224,1... | collective-permute-start | bytes 1277960 | tf_op jit(solution)/shard_map/ppermute | solution.py:27
  17.8 0.6 pad_maximum_fusion.4.scalars
  18.4 0.6 pad_add_fusion.numbers
  19.0 6.6 %collective-permute-done.refs_1_.refs_7_ = bf16[128,1664]{1,0:T(8,128)(2,1)S(1)} collective-permute-done((bf16[128,1664]{1,0:T(8,128)(2,1)S(1)}, bf16[128,1664]{1,0:T(8,128)(2,1)S(1)}, u32[]{:S(2)}, u32[]{:S(2)}) %collective-permute-start) | collective-permute-done | bytes 426016 | tf_op jit(solution)/shard_map/ppermute | solution.py:27
  25.6 0.1 collective-permute-start.2
  25.7 2.7 %collective-permute-start.3 = (bf16[128,1664]{1,0:T(8,128)(2,1)S(1)}, bf16[128,1664]{1,0:T(8,128)(2,1)}, u32[]{:S(2)}, u32[]{:S(2)}) collective-permute-start(bf16[128,1664]{1,0:T(8,128)(2,1)S(1)} %collective-permute-done.1.refs_2_.refs_8_), channel_id=1, source_target_pairs={{0,224},{32,0},{64,32},{96,64},{128,96},{160,128},{192,160},{224,1... | collective-permute-start | bytes 1277960 | tf_op jit(solution)/shard_map/ppermute | solution.py:27
  28.3 8.4 %collective-permute-done.2.refs_3_.refs_9_ = bf16[128,1664]{1,0:T(8,128)(2,1)} collective-permute-done((bf16[128,1664]{1,0:T(8,128)(2,1)S(1)}, bf16[128,1664]{1,0:T(8,128)(2,1)}, u32[]{:S(2)}, u32[]{:S(2)}) %collective-permute-start.2) | collective-permute-done | bytes 426016 | tf_op jit(solution)/shard_map/ppermute | solution.py:27
  36.7 2.6 %collective-permute-start.4 = (bf16[1024,1024]{1,0:T(8,128)(2,1)S(1)}, bf16[1024,1024]{1,0:T(8,128)(2,1)S(1)}, u32[]{:S(2)}, u32[]{:S(2)}) collective-permute-start(bf16[1024,1024]{1,0:T(8,128)(2,1)S(1)} %bitcast.111), channel_id=1, source_target_pairs={{0,2},{2,0},{1,3},{3,1},{4,6},{6,4},{5,7},{7,5},{8,10},{10,8},{9,1... | collective-permute-start | bytes 6291464 | tf_op jit(solution)/shard_map/ppermute | solution.py:31
  39.3 1.4 collective-permute-start.5
  40.7 2.4 %collective-permute-start.6 = (bf16[128,1664]{1,0:T(8,128)(2,1)}, bf16[128,1664]{1,0:T(8,128)(2,1)S(1)}, u32[]{:S(2)}, u32[]{:S(2)}) collective-permute-start(bf16[128,1664]{1,0:T(8,128)(2,1)} %collective-permute-done.3.refs_0_.refs_10_), channel_id=1, source_target_pairs={{0,224},{32,0},{64,32},{96,64},{128,96},{160,128},{192,160},{224,1... | collective-permute-start | bytes 1277960 | tf_op jit(solution)/shard_map/ppermute | solution.py:27
  43.1 1.4 copy-done.7
  44.5 12.0 %shard_map.94 = (f32[8,512]{1,0:T(8,128)}, bf16[512,2048]{1,0:T(8,128)(2,1)}, bf16[512,1024]{1,0:T(8,128)(2,1)}, bf16[512,1024]{1,0:T(8,128)(2,1)}) custom-call(f32[2]{0:T(128)} %pad_maximum_fusion.4.scalars, s32[17]{0:T(128)} %pad_add_fusion.numbers, bf16[128,1664]{1,0:T(8,128)(2,1)} %copy-done.3, bf16[128,1664]{1,0:T(8,128)(2,1)} %copy-done.8, ...), custom_call_target="tpu_custom_call" | custom-call | flops 5905580032 | bytes 16777216 | tf_op jit(solution)/shard_map/pallas_call | solution.py:243
  56.6 1.5 collective-permute-start.7
  58.1 2.6 %collective-permute-start.8 = (bf16[64,1664]{1,0:T(8,128)(2,1)S(1)}, bf16[64,1664]{1,0:T(8,128)(2,1)S(1)}, u32[]{:S(2)}, u32[]{:S(2)}) collective-permute-start(bf16[64,1664]{1,0:T(8,128)(2,1)S(1)} %slice.89), channel_id=1, source_target_pairs={{0,224},{32,0},{64,32},{96,64},{128,96},{160,128},{192,160},{224,1... | collective-permute-start | bytes 638984 | tf_op jit(solution)/shard_map/ppermute | solution.py:27
  60.7 8.0 %shard_map.95 = (f32[8,256]{1,0:T(8,128)}, bf16[256,2048]{1,0:T(8,128)(2,1)}, bf16[256,1024]{1,0:T(8,128)(2,1)}, bf16[256,1024]{1,0:T(8,128)(2,1)}) custom-call(f32[2]{0:T(128)} %pad_maximum_fusion.4.scalars, s32[17]{0:T(128)} %pad_add_fusion.numbers, bf16[128,1664]{1,0:T(8,128)(2,1)} %collective-permute-done.3.refs_0_.refs_10_, ...), custom_call_target="tpu_custom_call" | custom-call | flops 2952790016 | bytes 16777216 | tf_op jit(solution)/shard_map/pallas_call | solution.py:243
  68.8 0.7 copy-done.10
  69.4 0.1 copy-done.11
  69.5 13.6 %shard_map.96 = (f32[8,256]{1,0:T(8,128)}, bf16[256,2048]{1,0:T(8,128)(2,1)}, bf16[256,1024]{1,0:T(8,128)(2,1)}, f32[1536,512]{1,0:T(8,128)}, bf16[1536,512]{1,0:T(8,128)(2,1)}) custom-call(f32[2]{0:T(128)} %pad_maximum_fusion.4.scalars, s32[17]{0:T(128)} %pad_add_fusion.numbers, bf16[128,1664]{1,0:T(8,128)(2,1)} %copy-done.6, bf16[64,1664]{1,0:T(8,128)(2,1)} %copy-done.10, ...), custom_call_target="tpu_custom_call" | custom-call | flops 6174015488 | bytes 16777216 | tf_op jit(solution)/shard_map/pallas_call | solution.py:243
  83.1 0.7 collective-permute-start.9
  83.8 0.7 fusion.35
  84.5 0.7 fusion.34
  85.2 0.7 fusion.36
  86.1 1.0 collective-permute-done.9
  87.1 2.4 %convert_add_fusion = f32[1536,512]{1,0:T(8,128)S(1)} fusion(f32[1536,512]{1,0:T(8,128)} %get-tuple-element.48, bf16[1536,512]{1,0:T(8,128)(2,1)S(1)} %collective-permute-done.9), kind=kLoop, calls=%fused_computation.2 | loop fusion | flops 1572864 | bytes 7864320 | tf_op jit(solution)/shard_map/add | solution.py:316
  89.5 0.4 fusion.33
  89.9 1.9 %collective-permute-start.10 = (bf16[2,2,2,2,2,24,256]{6,5,4,3,2,1,0:T(8,128)(2,1)S(1)}, bf16[2,2,2,2,2,24,256]{6,5,4,3,2,1,0:T(8,128)(2,1)S(1)}, u32[]{:S(2)}, u32[]{:S(2)}) collective-permute-start(bf16[2,2,2,2,2,24,256]{6,5,4,3,2,1,0:T(8,128)(2,1)S(1)} %fusion.10), channel_id=1, source_target_pairs={{0,8},{4,12},{8,0},{12,4},{1,9},{5,13},{9,1},{13,5},{2,10},{6,14},... | collective-permute-start | bytes 1179656 | tf_op jit(solution)/shard_map/ppermute | solution.py:31
  91.8 0.8 fusion.11
  92.6 0.2 collective-permute-start.12
  92.9 9.0 %shard_map.97 = (bf16[1024,1024]{1,0:T(8,128)(2,1)}, bf16[1024,1024]{1,0:T(8,128)(2,1)}) custom-call(bf16[512,2048]{1,0:T(8,128)(2,1)} %get-tuple-element.51.refs_0_, bf16[256,2048]{1,0:T(8,128)(2,1)} %get-tuple-element.52.refs_1_, bf16[256,2048]{1,0:T(8,128)(2,1)} %get-tuple-element.53.refs_2_, bf16[512,1024]{1,0:T(8,128)(2,1)} %get-tuple-element.54.refs_3_, ...), custom_call_target="tpu_custom_call" | custom-call | flops 4294967296 | bytes 10485760 | tf_op jit(solution)/shard_map/pallas_call | solution.py:276
  101.9 0.9 collective-permute-start.19
  102.8 0.1 collective-permute-done.12
  103.0 1.1 fusion
  104.1 1.2 collective-permute-start.13
  105.3 0.1 bitcast_add_fusion
  105.5 1.2 collective-permute-start.11
  106.7 3.8 %collective-permute-done.13 = bf16[2,2,2,2,24,256]{5,4,3,2,1,0:T(8,128)(2,1)S(1)} collective-permute-done((bf16[2,2,2,2,24,256]{5,4,3,2,1,0:T(8,128)(2,1)S(1)}, bf16[2,2,2,2,24,256]{5,4,3,2,1,0:T(8,128)(2,1)S(1)}, u32[]{:S(2)}, u32[]{:S(2)}) %collective-permute-start.13) | collective-permute-done | bytes 196640 | tf_op jit(solution)/shard_map/ppermute | solution.py:31
  110.8 0.6 collective-permute-start.14
  111.3 4.0 %collective-permute-done.14 = bf16[2,2,2,24,512]{4,3,2,1,0:T(8,128)(2,1)S(1)} collective-permute-done((bf16[2,2,2,24,512]{4,3,2,1,0:T(8,128)(2,1)S(1)}, bf16[2,2,2,24,512]{4,3,2,1,0:T(8,128)(2,1)S(1)}, u32[]{:S(2)}, u32[]{:S(2)}) %collective-permute-start.14) | collective-permute-done | bytes 196640 | tf_op jit(solution)/shard_map/ppermute | solution.py:31
  115.5 1.3 collective-permute-start.15
  116.8 2.3 %collective-permute-done.15 = bf16[2,2,24,512]{3,2,1,0:T(8,128)(2,1)S(1)} collective-permute-done((bf16[2,2,24,512]{3,2,1,0:T(8,128)(2,1)S(1)}, bf16[2,2,24,512]{3,2,1,0:T(8,128)(2,1)S(1)}, u32[]{:S(2)}, u32[]{:S(2)}) %collective-permute-start.15) | collective-permute-done | bytes 98336 | tf_op jit(solution)/shard_map/ppermute | solution.py:31
  119.0 0.2 copy.37
  119.2 0.1 copy.66
  119.3 2.5 %collective-permute-start.16 = (f32[2,2,2,6,512]{4,2,3,1,0:T(2,128)S(1)}, f32[2,2,2,6,512]{4,2,3,1,0:T(2,128)S(1)}, u32[]{:S(2)}, u32[]{:S(2)}) collective-permute-start(f32[2,2,2,6,512]{4,2,3,1,0:T(2,128)S(1)} %bitcast.119), channel_id=1, source_target_pairs={{0,1},{1,0},{2,3},{3,2},{4,5},{5,4},{6,7},{7,6},{8,9},{9,8},{10,11... | collective-permute-start | bytes 294920 | tf_op jit(solution)/shard_map/ppermute | solution.py:31
  121.8 3.9 %add_convert_fusion = bf16[1024,1024]{1,0:T(8,128)(2,1)} fusion(bf16[1024,1024]{1,0:T(8,128)(2,1)} %collective-permute-done.19, bf16[1024,1024]{1,0:T(8,128)(2,1)S(1)} %copy-done.1), kind=kLoop, calls=%fused_computation.1 | loop fusion | flops 4194304 | bytes 6291456 | tf_op jit(solution)/shard_map/convert_element_type | solution.py:320
  125.8 3.6 %all-to-all-start.1 = ((bf16[8,128,1024]{2,1,0:T(8,128)(2,1)}), bf16[8,128,1024]{2,1,0:T(8,128)(2,1)S(1)}, u32[]{:S(2)}, u32[]{:S(2)}) async-start(bf16[8,128,1024]{2,1,0:T(8,128)(2,1)} %bitcast.33), calls=%async_computation.1 | async-start | bytes 4194304 | tf_op jit(solution)/shard_map/all_to_all | solution.py:35
  129.4 0.1 bitcast_add_fusion.3
  129.5 4.6 %collective-permute-start.17 = (f32[40,512]{1,0:T(8,128)S(1)}, f32[40,512]{1,0:T(8,128)S(1)}, u32[]{:S(2)}, u32[]{:S(2)}) collective-permute-start(f32[40,512]{1,0:T(8,128)S(1)} %pad_maximum_fusion.2), channel_id=1, source_target_pairs={{0,64},{32,96},{64,0},{96,32},{128,192},{160,224},{192,128},{224,1... | collective-permute-start | bytes 245768 | tf_op jit(solution)/shard_map/ppermute | solution.py:31
  134.1 2.7 %collective-permute-done.17 = f32[40,512]{1,0:T(8,128)S(1)} collective-permute-done((f32[40,512]{1,0:T(8,128)S(1)}, f32[40,512]{1,0:T(8,128)S(1)}, u32[]{:S(2)}, u32[]{:S(2)}) %collective-permute-start.17) | collective-permute-done | bytes 81952 | tf_op jit(solution)/shard_map/ppermute | solution.py:31
  136.9 0.1 bitcast_add_fusion.4
  137.1 1.3 collective-permute-start.18
  138.3 6.0 %collective-permute-done.18 = f32[28,512]{1,0:T(8,128)S(1)} collective-permute-done((f32[28,512]{1,0:T(8,128)S(1)}, f32[28,512]{1,0:T(8,128)S(1)}, u32[]{:S(2)}, u32[]{:S(2)}) %collective-permute-start.18) | collective-permute-done | bytes 57376 | tf_op jit(solution)/shard_map/ppermute | solution.py:31
  144.4 0.5 fusion.31
  144.9 6.1 %all-to-all-done.1 = bf16[8,128,1024]{2,1,0:T(8,128)(2,1)S(1)} async-done(((bf16[8,128,1024]{2,1,0:T(8,128)(2,1)}), bf16[8,128,1024]{2,1,0:T(8,128)(2,1)S(1)}, u32[]{:S(2)}, u32[]{:S(2)}) %all-to-all-start.1) | async-done | bytes 2097184 | tf_op jit(solution)/shard_map/all_to_all | solution.py:35
  151.1 5.3 %collective-permute-start.20 = (f32[6,512]{1,0:T(8,128)S(1)}, f32[6,512]{1,0:T(8,128)S(1)}, u32[]{:S(2)}, u32[]{:S(2)}) collective-permute-start(f32[6,512]{1,0:T(8,128)S(1)} %bitcast.122), channel_id=1, source_target_pairs={{0,2},{2,0},{1,3},{3,1},{4,6},{6,4},{5,7},{7,5},{8,10},{10,8},{9,1... | collective-permute-start | bytes 36872 | tf_op jit(solution)/shard_map/ppermute | solution.py:31
  156.4 0.3 convert_reduce_fusion
  156.7 0.2 fusion.5
  157.0 1.0 fusion.9
  158.0 0.6 fusion.20
  (93 shorter events, 1.0 us)
Async XLA Ops:
  4.4 6.1 %copy-start.12 = (s32[1,128]{1,0:T(1,128)S(1)}, s32[1,128]{1,0:T(1,128)}, u32[]{:S(2)}) copy-start(s32[1,128]{1,0:T(1,128)} %param.10) | copy-start | bytes 1540
  4.4 6.2 %copy-start.4 = (bf16[1,128,1536]{2,1,0:T(8,128)(2,1)S(1)}, bf16[1,128,1536]{2,1,0:T(8,128)(2,1)}, u32[]{:S(2)}) copy-start(bf16[1,128,1536]{2,1,0:T(8,128)(2,1)} %param.7) | copy-start | bytes 1179652
  4.4 32.3 %all-to-all-start = ((bf16[8,128,1024]{2,1,0:T(8,128)(2,1)}), bf16[8,128,1024]{2,1,0:T(8,128)(2,1)S(1)}, u32[]{:S(2)}, u32[]{:S(2)}) async-start(bf16[8,128,1024]{2,1,0:T(8,128)(2,1)} %broadcast_in_dim.33), calls=%async_computation | async-start | bytes 4194304 | tf_op jit(solution)/shard_map/all_to_all | solution.py:35
  10.7 32.4 %copy-start.3 = (bf16[128,1664]{1,0:T(8,128)(2,1)}, bf16[128,1664]{1,0:T(8,128)(2,1)S(1)}, u32[]{:S(2)}) copy-start(bf16[128,1664]{1,0:T(8,128)(2,1)S(1)} %pad_maximum_fusion.refs_0_.refs_6_) | copy-start | bytes 1277956
  10.7 14.9 %collective-permute-start = (bf16[128,1664]{1,0:T(8,128)(2,1)S(1)}, bf16[128,1664]{1,0:T(8,128)(2,1)S(1)}, u32[]{:S(2)}, u32[]{:S(2)}) collective-permute-start(bf16[128,1664]{1,0:T(8,128)(2,1)S(1)} %pad_maximum_fusion.refs_0_.refs_6_), channel_id=1, source_target_pairs={{0,32},{32,64},{64,96},{96,128},{128,160},{160,192},{192,224},{224... | collective-permute-start | bytes 1277960 | tf_op jit(solution)/shard_map/ppermute | solution.py:27
  12.4 13.2 %collective-permute-start.1 = (bf16[128,1664]{1,0:T(8,128)(2,1)S(1)}, bf16[128,1664]{1,0:T(8,128)(2,1)S(1)}, u32[]{:S(2)}, u32[]{:S(2)}) collective-permute-start(bf16[128,1664]{1,0:T(8,128)(2,1)S(1)} %pad_maximum_fusion.refs_0_.refs_6_), channel_id=1, source_target_pairs={{0,224},{32,0},{64,32},{96,64},{128,96},{160,128},{192,160},{224,1... | collective-permute-start | bytes 1277960 | tf_op jit(solution)/shard_map/ppermute | solution.py:27
  25.6 17.5 %copy-start.8 = (bf16[128,1664]{1,0:T(8,128)(2,1)}, bf16[128,1664]{1,0:T(8,128)(2,1)S(1)}, u32[]{:S(2)}) copy-start(bf16[128,1664]{1,0:T(8,128)(2,1)S(1)} %collective-permute-done.refs_1_.refs_7_) | copy-start | bytes 1277956
  25.6 17.5 %copy-start.9 = (bf16[128,1664]{1,0:T(8,128)(2,1)}, bf16[128,1664]{1,0:T(8,128)(2,1)S(1)}, u32[]{:S(2)}) copy-start(bf16[128,1664]{1,0:T(8,128)(2,1)S(1)} %collective-permute-done.1.refs_2_.refs_8_) | copy-start | bytes 1277956
  25.6 11.2 %collective-permute-start.2 = (bf16[128,1664]{1,0:T(8,128)(2,1)S(1)}, bf16[128,1664]{1,0:T(8,128)(2,1)}, u32[]{:S(2)}, u32[]{:S(2)}) collective-permute-start(bf16[128,1664]{1,0:T(8,128)(2,1)S(1)} %collective-permute-done.refs_1_.refs_7_), channel_id=1, source_target_pairs={{0,32},{32,64},{64,96},{96,128},{128,160},{160,192},{192,224},{224... | collective-permute-start | bytes 1277960 | tf_op jit(solution)/shard_map/ppermute | solution.py:27
  25.7 11.1 %collective-permute-start.3 = (bf16[128,1664]{1,0:T(8,128)(2,1)S(1)}, bf16[128,1664]{1,0:T(8,128)(2,1)}, u32[]{:S(2)}, u32[]{:S(2)}) collective-permute-start(bf16[128,1664]{1,0:T(8,128)(2,1)S(1)} %collective-permute-done.1.refs_2_.refs_8_), channel_id=1, source_target_pairs={{0,224},{32,0},{64,32},{96,64},{128,96},{160,128},{192,160},{224,1... | collective-permute-start | bytes 1277960 | tf_op jit(solution)/shard_map/ppermute | solution.py:27
  36.7 6.4 %copy-start.2 = (bf16[8,128,1024]{2,1,0:T(8,128)(2,1)}, bf16[8,128,1024]{2,1,0:T(8,128)(2,1)S(1)}, u32[]{:S(2)}) copy-start(bf16[8,128,1024]{2,1,0:T(8,128)(2,1)S(1)} %all-to-all-done) | copy-start | bytes 6291460
  36.7 6.3 %collective-permute-start.4 = (bf16[1024,1024]{1,0:T(8,128)(2,1)S(1)}, bf16[1024,1024]{1,0:T(8,128)(2,1)S(1)}, u32[]{:S(2)}, u32[]{:S(2)}) collective-permute-start(bf16[1024,1024]{1,0:T(8,128)(2,1)S(1)} %bitcast.111), channel_id=1, source_target_pairs={{0,2},{2,0},{1,3},{3,1},{4,6},{6,4},{5,7},{7,5},{8,10},{10,8},{9,1... | collective-permute-start | bytes 6291464 | tf_op jit(solution)/shard_map/ppermute | solution.py:31
  39.3 17.2 %collective-permute-start.5 = (bf16[128,1664]{1,0:T(8,128)(2,1)}, bf16[128,1664]{1,0:T(8,128)(2,1)S(1)}, u32[]{:S(2)}, u32[]{:S(2)}) collective-permute-start(bf16[128,1664]{1,0:T(8,128)(2,1)} %collective-permute-done.2.refs_3_.refs_9_), channel_id=1, source_target_pairs={{0,32},{32,64},{64,96},{96,128},{128,160},{160,192},{192,224},{224... | collective-permute-start | bytes 1277960 | tf_op jit(solution)/shard_map/ppermute | solution.py:27
  40.7 15.8 %collective-permute-start.6 = (bf16[128,1664]{1,0:T(8,128)(2,1)}, bf16[128,1664]{1,0:T(8,128)(2,1)S(1)}, u32[]{:S(2)}, u32[]{:S(2)}) collective-permute-start(bf16[128,1664]{1,0:T(8,128)(2,1)} %collective-permute-done.3.refs_0_.refs_10_), channel_id=1, source_target_pairs={{0,224},{32,0},{64,32},{96,64},{128,96},{160,128},{192,160},{224,1... | collective-permute-start | bytes 1277960 | tf_op jit(solution)/shard_map/ppermute | solution.py:27
  43.1 1.4 copy-start.7
  56.5 4.2 %copy-start.5 = (bf16[128,1664]{1,0:T(8,128)(2,1)}, bf16[128,1664]{1,0:T(8,128)(2,1)S(1)}, u32[]{:S(2)}) copy-start(bf16[128,1664]{1,0:T(8,128)(2,1)S(1)} %collective-permute-done.5.refs_1_.refs_11_) | copy-start | bytes 1277956
  56.6 12.2 %copy-start.6 = (bf16[128,1664]{1,0:T(8,128)(2,1)}, bf16[128,1664]{1,0:T(8,128)(2,1)S(1)}, u32[]{:S(2)}) copy-start(bf16[128,1664]{1,0:T(8,128)(2,1)S(1)} %collective-permute-done.6.refs_0_) | copy-start | bytes 1277956
  56.6 12.1 %collective-permute-start.7 = (bf16[64,1664]{1,0:T(8,128)(2,1)S(1)}, bf16[64,1664]{1,0:T(8,128)(2,1)S(1)}, u32[]{:S(2)}, u32[]{:S(2)}) collective-permute-start(bf16[64,1664]{1,0:T(8,128)(2,1)S(1)} %slice.88), channel_id=1, source_target_pairs={{0,32},{32,64},{64,96},{96,128},{128,160},{160,192},{192,224},{224... | collective-permute-start | bytes 638984 | tf_op jit(solution)/shard_map/ppermute | solution.py:27
  58.1 10.6 %collective-permute-start.8 = (bf16[64,1664]{1,0:T(8,128)(2,1)S(1)}, bf16[64,1664]{1,0:T(8,128)(2,1)S(1)}, u32[]{:S(2)}, u32[]{:S(2)}) collective-permute-start(bf16[64,1664]{1,0:T(8,128)(2,1)S(1)} %slice.89), channel_id=1, source_target_pairs={{0,224},{32,0},{64,32},{96,64},{128,96},{160,128},{192,160},{224,1... | collective-permute-start | bytes 638984 | tf_op jit(solution)/shard_map/ppermute | solution.py:27
  68.7 0.7 copy-start.10
  68.7 0.7 copy-start.11
  83.1 3.9 %collective-permute-start.9 = (bf16[1536,512]{1,0:T(8,128)(2,1)}, bf16[1536,512]{1,0:T(8,128)(2,1)S(1)}, u32[]{:S(2)}, u32[]{:S(2)}) collective-permute-start(bf16[1536,512]{1,0:T(8,128)(2,1)} %get-tuple-element.49), channel_id=1, source_target_pairs={{0,2},{2,0},{1,3},{3,1},{4,6},{6,4},{5,7},{7,5},{8,10},{10,8},{9,1... | collective-permute-start | bytes 4718600 | tf_op jit(solution)/shard_map/ppermute | solution.py:31
  89.9 15.4 %collective-permute-start.10 = (bf16[2,2,2,2,2,24,256]{6,5,4,3,2,1,0:T(8,128)(2,1)S(1)}, bf16[2,2,2,2,2,24,256]{6,5,4,3,2,1,0:T(8,128)(2,1)S(1)}, u32[]{:S(2)}, u32[]{:S(2)}) collective-permute-start(bf16[2,2,2,2,2,24,256]{6,5,4,3,2,1,0:T(8,128)(2,1)S(1)} %fusion.10), channel_id=1, source_target_pairs={{0,8},{4,12},{8,0},{12,4},{1,9},{5,13},{9,1},{13,5},{2,10},{6,14},... | collective-permute-start | bytes 1179656 | tf_op jit(solution)/shard_map/ppermute | solution.py:31
  92.6 10.3 %collective-permute-start.12 = (bf16[2,2,2,2,2,24,256]{6,5,4,2,1,0,3:T(8,128)(2,1)}, bf16[2,2,2,2,2,24,256]{6,5,4,2,1,0,3:T(8,128)(2,1)}, u32[]{:S(2)}, u32[]{:S(2)}) collective-permute-start(bf16[2,2,2,2,2,24,256]{6,5,4,2,1,0,3:T(8,128)(2,1)} %fusion.11), channel_id=1, source_target_pairs={{0,32},{32,0},{64,96},{96,64},{128,160},{160,128},{192,224},{224,1... | collective-permute-start | bytes 1179656 | tf_op jit(solution)/shard_map/ppermute | solution.py:31
  101.9 19.9 %collective-permute-start.19 = (bf16[1024,1024]{1,0:T(8,128)(2,1)}, bf16[1024,1024]{1,0:T(8,128)(2,1)}, u32[]{:S(2)}, u32[]{:S(2)}) collective-permute-start(bf16[1024,1024]{1,0:T(8,128)(2,1)} %get-tuple-element.58), channel_id=1, source_target_pairs={{0,2},{2,0},{1,3},{3,1},{4,6},{6,4},{5,7},{7,5},{8,10},{10,8},{9,1... | collective-permute-start | bytes 6291464 | tf_op jit(solution)/shard_map/ppermute | solution.py:31
  104.1 6.5 %collective-permute-start.13 = (bf16[2,2,2,2,24,256]{5,4,3,2,1,0:T(8,128)(2,1)S(1)}, bf16[2,2,2,2,24,256]{5,4,3,2,1,0:T(8,128)(2,1)S(1)}, u32[]{:S(2)}, u32[]{:S(2)}) collective-permute-start(bf16[2,2,2,2,24,256]{5,4,3,2,1,0:T(8,128)(2,1)S(1)} %fusion.17), channel_id=1, source_target_pairs={{0,8},{4,12},{8,0},{12,4},{1,9},{5,13},{9,1},{13,5},{2,10},{6,14},... | collective-permute-start | bytes 589832 | tf_op jit(solution)/shard_map/ppermute | solution.py:31
  105.5 5.1 %collective-permute-start.11 = (bf16[400,256]{1,0:T(8,128)(2,1)S(1)}, bf16[400,256]{1,0:T(8,128)(2,1)S(1)}, u32[]{:S(2)}, u32[]{:S(2)}) collective-permute-start(bf16[400,256]{1,0:T(8,128)(2,1)S(1)} %pad_maximum_fusion.1), channel_id=1, source_target_pairs={{0,32},{32,0},{64,96},{96,64},{128,160},{160,128},{192,224},{224,1... | collective-permute-start | bytes 614408 | tf_op jit(solution)/shard_map/ppermute | solution.py:31
  110.7 11.1 %copy-start.1 = (bf16[1024,1024]{1,0:T(8,128)(2,1)S(1)}, bf16[1024,1024]{1,0:T(8,128)(2,1)}, u32[]{:S(2)}) copy-start(bf16[1024,1024]{1,0:T(8,128)(2,1)} %get-tuple-element.57) | copy-start | bytes 6291460
  110.8 4.6 %collective-permute-start.14 = (bf16[2,2,2,24,512]{4,3,2,1,0:T(8,128)(2,1)S(1)}, bf16[2,2,2,24,512]{4,3,2,1,0:T(8,128)(2,1)S(1)}, u32[]{:S(2)}, u32[]{:S(2)}) collective-permute-start(bf16[2,2,2,24,512]{4,3,2,1,0:T(8,128)(2,1)S(1)} %fusion.18), channel_id=1, source_target_pairs={{0,4},{4,0},{8,12},{12,8},{1,5},{5,1},{9,13},{13,9},{2,6},{6,2},{1... | collective-permute-start | bytes 589832 | tf_op jit(solution)/shard_map/ppermute | solution.py:31
  115.5 3.6 %collective-permute-start.15 = (bf16[2,2,24,512]{3,2,1,0:T(8,128)(2,1)S(1)}, bf16[2,2,24,512]{3,2,1,0:T(8,128)(2,1)S(1)}, u32[]{:S(2)}, u32[]{:S(2)}) collective-permute-start(bf16[2,2,24,512]{3,2,1,0:T(8,128)(2,1)S(1)} %fusion.19), channel_id=1, source_target_pairs={{0,16},{16,0},{1,17},{17,1},{2,18},{18,2},{3,19},{19,3},{4,20},{20... | collective-permute-start | bytes 294920 | tf_op jit(solution)/shard_map/ppermute | solution.py:31
  119.3 10.1 %collective-permute-start.16 = (f32[2,2,2,6,512]{4,2,3,1,0:T(2,128)S(1)}, f32[2,2,2,6,512]{4,2,3,1,0:T(2,128)S(1)}, u32[]{:S(2)}, u32[]{:S(2)}) collective-permute-start(f32[2,2,2,6,512]{4,2,3,1,0:T(2,128)S(1)} %bitcast.119), channel_id=1, source_target_pairs={{0,1},{1,0},{2,3},{3,2},{4,5},{5,4},{6,7},{7,6},{8,9},{9,8},{10,11... | collective-permute-start | bytes 294920 | tf_op jit(solution)/shard_map/ppermute | solution.py:31
  125.8 25.3 %all-to-all-start.1 = ((bf16[8,128,1024]{2,1,0:T(8,128)(2,1)}), bf16[8,128,1024]{2,1,0:T(8,128)(2,1)S(1)}, u32[]{:S(2)}, u32[]{:S(2)}) async-start(bf16[8,128,1024]{2,1,0:T(8,128)(2,1)} %bitcast.33), calls=%async_computation.1 | async-start | bytes 4194304 | tf_op jit(solution)/shard_map/all_to_all | solution.py:35
  129.5 27.2 %copy-start = (bf16[1,128,1024]{2,1,0:T(8,128)(2,1)S(1)}, bf16[1,128,1024]{2,1,0:T(8,128)(2,1)}, u32[]{:S(2)}) copy-start(bf16[1,128,1024]{2,1,0:T(8,128)(2,1)} %param.9) | copy-start | bytes 786436
  129.5 7.3 %collective-permute-start.17 = (f32[40,512]{1,0:T(8,128)S(1)}, f32[40,512]{1,0:T(8,128)S(1)}, u32[]{:S(2)}, u32[]{:S(2)}) collective-permute-start(f32[40,512]{1,0:T(8,128)S(1)} %pad_maximum_fusion.2), channel_id=1, source_target_pairs={{0,64},{32,96},{64,0},{96,32},{128,192},{160,224},{192,128},{224,1... | collective-permute-start | bytes 245768 | tf_op jit(solution)/shard_map/ppermute | solution.py:31
  137.1 7.3 %collective-permute-start.18 = (f32[28,512]{1,0:T(8,128)S(1)}, f32[28,512]{1,0:T(8,128)S(1)}, u32[]{:S(2)}, u32[]{:S(2)}) collective-permute-start(f32[28,512]{1,0:T(8,128)S(1)} %pad_maximum_fusion.3), channel_id=1, source_target_pairs={{0,128},{32,160},{64,192},{96,224},{128,0},{160,32},{192,64},{224,... | collective-permute-start | bytes 172040 | tf_op jit(solution)/shard_map/ppermute | solution.py:31
  151.1 6.9 %collective-permute-start.20 = (f32[6,512]{1,0:T(8,128)S(1)}, f32[6,512]{1,0:T(8,128)S(1)}, u32[]{:S(2)}, u32[]{:S(2)}) collective-permute-start(f32[6,512]{1,0:T(8,128)S(1)} %bitcast.122), channel_id=1, source_target_pairs={{0,2},{2,0},{1,3},{3,1},{4,6},{6,4},{5,7},{7,5},{8,10},{10,8},{9,1... | collective-permute-start | bytes 36872 | tf_op jit(solution)/shard_map/ppermute | solution.py:31

commit v5 on v4

--- a/solution.py
+++ b/solution.py
@@ -269,7 +269,7 @@
 
 
 def text_directions(coeffs, low):
-    block = 512
+    block = 256
     steps = TEXTS // block // 2
     column = lambda c: pl.BlockSpec((c.shape[0], block), lambda i: (0, (i + steps) % (2 * steps)))
     keep = lambda v: pl.BlockSpec(v.shape, lambda i: (0, 0), pipeline_mode=pl.Buffered(1))

time: 160 us -> 163 us (1.019)
  waiting for transfers between devices: 41.1 us -> 48.1 us
  starting transfers between devices: 50.3 us -> 45.6 us
    all_to_all x2, waiting for transfers between devices: 6.13 us -> 10.9 us  [exchange(): return lax.all_to_all(x, axes, 0, 0)]
    ppermute x13, starting transfers between devices: 24.2 us -> 19.5 us  [flip(): return lax.ppermute(x, axis, [(i, i ^ bit) for i in range(n)])]
    ppermute x13, waiting for transfers between devices: 20 us -> 22.2 us  [flip(): return lax.ppermute(x, axis, [(i, i ^ bit) for i in range(n)])]
  transfers between devices with their start and end apart: 23 -> 23, of which waited for: 10 -> 9; matrix products, arithmetic and copies ran while one was open for 8% -> 8% of each run, Pallas kernels for 18% -> 19%
where the time goes in v5:
time: 163 us; the launch traced here: 162 us
  waiting for transfers between devices  48.1 us (30%)
  starting transfers between devices  45.6 us (28%)
  Pallas kernels  44.2 us (27%)
  other arithmetic  14.2 us (9%)
  local copies, waits for them, and re-layouts  7.79 us (5%)
  between operations  2.55 us (2%)
    pallas_call x3, Pallas kernels, tile(): pl.pallas_call(functools.partial(tile_kernel, len(images), len(early[0])...  33.7 us
    ppermute x13, waiting for transfers between devices, flip(): return lax.ppermute(x, axis, [(i, i ^ bit) for i in range(n)])  22.2 us
    ppermute x13, starting transfers between devices, flip(): return lax.ppermute(x, axis, [(i, i ^ bit) for i in range(n)])  19.5 us
    ppermute x8, starting transfers between devices, shift(): return lax.ppermute(x, axis, [(i, (i + by) % n) for i in range(n)])  16.4 us
    ppermute x8, waiting for transfers between devices, shift(): return lax.ppermute(x, axis, [(i, (i + by) % n) for i in range(n)])  15 us
    all_to_all x2, waiting for transfers between devices, exchange(): return lax.all_to_all(x, axes, 0, 0)  10.9 us
    pallas_call x1, Pallas kernels, text_directions(): pl.pallas_call(text_kernel, grid=(TEXTS // block,), in_specs=[*map(column...  10.5 us
    all_to_all x2, starting transfers between devices, exchange(): return lax.all_to_all(x, axes, 0, 0)  9.68 us
  transfers between devices with their start and end apart: 23, of which 9 were waited for; matrix products, arithmetic and copies ran while one was open for 8% of the time, Pallas kernels for 19%

profile of v5, /device:TPU:1, one launch (start us, length us, event | category | flops | bytes accessed | tf_op | source)
XLA Modules:
  0.0 162.4 jit_solution(7907026890569856793)
XLA Ops:
  0.6 1.1 fusion.6
  1.7 1.1 fusion.4
  2.8 1.6 broadcast_in_dim.33
  4.4 6.1 %all-to-all-start = ((bf16[8,128,1024]{2,1,0:T(8,128)(2,1)}), bf16[8,128,1024]{2,1,0:T(8,128)(2,1)S(1)}, u32[]{:S(2)}, u32[]{:S(2)}) async-start(bf16[8,128,1024]{2,1,0:T(8,128)(2,1)} %broadcast_in_dim.33), calls=%async_computation | async-start | bytes 4194304 | tf_op jit(solution)/shard_map/all_to_all | solution.py:35
  10.5 0.1 select_convert_fusion
  10.7 1.7 %collective-permute-start = (bf16[128,1664]{1,0:T(8,128)(2,1)S(1)}, bf16[128,1664]{1,0:T(8,128)(2,1)S(1)}, u32[]{:S(2)}, u32[]{:S(2)}) collective-permute-start(bf16[128,1664]{1,0:T(8,128)(2,1)S(1)} %pad_maximum_fusion.refs_0_.refs_6_), channel_id=1, source_target_pairs={{0,32},{32,64},{64,96},{96,128},{128,160},{160,192},{192,224},{224... | collective-permute-start | bytes 1277960 | tf_op jit(solution)/shard_map/ppermute | solution.py:27
  12.4 4.0 %collective-permute-start.1 = (bf16[128,1664]{1,0:T(8,128)(2,1)S(1)}, bf16[128,1664]{1,0:T(8,128)(2,1)S(1)}, u32[]{:S(2)}, u32[]{:S(2)}) collective-permute-start(bf16[128,1664]{1,0:T(8,128)(2,1)S(1)} %pad_maximum_fusion.refs_0_.refs_6_), channel_id=1, source_target_pairs={{0,224},{32,0},{64,32},{96,64},{128,96},{160,128},{192,160},{224,1... | collective-permute-start | bytes 1277960 | tf_op jit(solution)/shard_map/ppermute | solution.py:27
  17.8 0.6 pad_maximum_fusion.4.scalars
  18.4 0.6 pad_add_fusion.numbers
  19.0 6.6 %collective-permute-done.refs_1_.refs_7_ = bf16[128,1664]{1,0:T(8,128)(2,1)S(1)} collective-permute-done((bf16[128,1664]{1,0:T(8,128)(2,1)S(1)}, bf16[128,1664]{1,0:T(8,128)(2,1)S(1)}, u32[]{:S(2)}, u32[]{:S(2)}) %collective-permute-start) | collective-permute-done | bytes 426016 | tf_op jit(solution)/shard_map/ppermute | solution.py:27
  25.6 0.1 collective-permute-start.2
  25.7 2.7 %collective-permute-start.3 = (bf16[128,1664]{1,0:T(8,128)(2,1)S(1)}, bf16[128,1664]{1,0:T(8,128)(2,1)}, u32[]{:S(2)}, u32[]{:S(2)}) collective-permute-start(bf16[128,1664]{1,0:T(8,128)(2,1)S(1)} %collective-permute-done.1.refs_2_.refs_8_), channel_id=1, source_target_pairs={{0,224},{32,0},{64,32},{96,64},{128,96},{160,128},{192,160},{224,1... | collective-permute-start | bytes 1277960 | tf_op jit(solution)/shard_map/ppermute | solution.py:27
  28.3 8.4 %collective-permute-done.2.refs_3_.refs_9_ = bf16[128,1664]{1,0:T(8,128)(2,1)} collective-permute-done((bf16[128,1664]{1,0:T(8,128)(2,1)S(1)}, bf16[128,1664]{1,0:T(8,128)(2,1)}, u32[]{:S(2)}, u32[]{:S(2)}) %collective-permute-start.2) | collective-permute-done | bytes 426016 | tf_op jit(solution)/shard_map/ppermute | solution.py:27
  36.7 2.6 %collective-permute-start.4 = (bf16[1024,1024]{1,0:T(8,128)(2,1)S(1)}, bf16[1024,1024]{1,0:T(8,128)(2,1)S(1)}, u32[]{:S(2)}, u32[]{:S(2)}) collective-permute-start(bf16[1024,1024]{1,0:T(8,128)(2,1)S(1)} %bitcast.111), channel_id=1, source_target_pairs={{0,2},{2,0},{1,3},{3,1},{4,6},{6,4},{5,7},{7,5},{8,10},{10,8},{9,1... | collective-permute-start | bytes 6291464 | tf_op jit(solution)/shard_map/ppermute | solution.py:31
  39.3 1.4 collective-permute-start.5
  40.7 2.4 %collective-permute-start.6 = (bf16[128,1664]{1,0:T(8,128)(2,1)}, bf16[128,1664]{1,0:T(8,128)(2,1)S(1)}, u32[]{:S(2)}, u32[]{:S(2)}) collective-permute-start(bf16[128,1664]{1,0:T(8,128)(2,1)} %collective-permute-done.3.refs_0_.refs_10_), channel_id=1, source_target_pairs={{0,224},{32,0},{64,32},{96,64},{128,96},{160,128},{192,160},{224,1... | collective-permute-start | bytes 1277960 | tf_op jit(solution)/shard_map/ppermute | solution.py:27
  43.1 1.4 copy-done.7
  44.5 12.0 %shard_map.94 = (f32[8,512]{1,0:T(8,128)}, bf16[512,2048]{1,0:T(8,128)(2,1)}, bf16[512,1024]{1,0:T(8,128)(2,1)}, bf16[512,1024]{1,0:T(8,128)(2,1)}) custom-call(f32[2]{0:T(128)} %pad_maximum_fusion.4.scalars, s32[17]{0:T(128)} %pad_add_fusion.numbers, bf16[128,1664]{1,0:T(8,128)(2,1)} %copy-done.3, bf16[128,1664]{1,0:T(8,128)(2,1)} %copy-done.8, ...), custom_call_target="tpu_custom_call" | custom-call | flops 5905580032 | bytes 16777216 | tf_op jit(solution)/shard_map/pallas_call | solution.py:243
  56.6 1.5 collective-permute-start.7
  58.1 2.6 %collective-permute-start.8 = (bf16[64,1664]{1,0:T(8,128)(2,1)S(1)}, bf16[64,1664]{1,0:T(8,128)(2,1)S(1)}, u32[]{:S(2)}, u32[]{:S(2)}) collective-permute-start(bf16[64,1664]{1,0:T(8,128)(2,1)S(1)} %slice.89), channel_id=1, source_target_pairs={{0,224},{32,0},{64,32},{96,64},{128,96},{160,128},{192,160},{224,1... | collective-permute-start | bytes 638984 | tf_op jit(solution)/shard_map/ppermute | solution.py:27
  60.7 8.0 %shard_map.95 = (f32[8,256]{1,0:T(8,128)}, bf16[256,2048]{1,0:T(8,128)(2,1)}, bf16[256,1024]{1,0:T(8,128)(2,1)}, bf16[256,1024]{1,0:T(8,128)(2,1)}) custom-call(f32[2]{0:T(128)} %pad_maximum_fusion.4.scalars, s32[17]{0:T(128)} %pad_add_fusion.numbers, bf16[128,1664]{1,0:T(8,128)(2,1)} %collective-permute-done.3.refs_0_.refs_10_, ...), custom_call_target="tpu_custom_call" | custom-call | flops 2952790016 | bytes 16777216 | tf_op jit(solution)/shard_map/pallas_call | solution.py:243
  68.8 0.7 copy-done.10
  69.4 0.1 copy-done.11
  69.5 13.6 %shard_map.96 = (f32[8,256]{1,0:T(8,128)}, bf16[256,2048]{1,0:T(8,128)(2,1)}, bf16[256,1024]{1,0:T(8,128)(2,1)}, f32[1536,512]{1,0:T(8,128)}, bf16[1536,512]{1,0:T(8,128)(2,1)}) custom-call(f32[2]{0:T(128)} %pad_maximum_fusion.4.scalars, s32[17]{0:T(128)} %pad_add_fusion.numbers, bf16[128,1664]{1,0:T(8,128)(2,1)} %copy-done.6, bf16[64,1664]{1,0:T(8,128)(2,1)} %copy-done.10, ...), custom_call_target="tpu_custom_call" | custom-call | flops 6174015488 | bytes 16777216 | tf_op jit(solution)/shard_map/pallas_call | solution.py:243
  83.1 0.7 collective-permute-start.9
  83.8 0.7 fusion.35
  84.5 0.7 fusion.34
  85.2 0.7 fusion.36
  86.1 1.0 collective-permute-done.9
  87.1 2.4 %convert_add_fusion = f32[1536,512]{1,0:T(8,128)S(1)} fusion(f32[1536,512]{1,0:T(8,128)} %get-tuple-element.48, bf16[1536,512]{1,0:T(8,128)(2,1)S(1)} %collective-permute-done.9), kind=kLoop, calls=%fused_computation.2 | loop fusion | flops 1572864 | bytes 7864320 | tf_op jit(solution)/shard_map/add | solution.py:316
  89.5 0.4 fusion.33
  89.9 0.1 fusion.10
  89.9 1.9 %collective-permute-start.10 = (bf16[2,2,2,2,2,24,256]{6,5,4,3,2,1,0:T(8,128)(2,1)S(1)}, bf16[2,2,2,2,2,24,256]{6,5,4,3,2,1,0:T(8,128)(2,1)S(1)}, u32[]{:S(2)}, u32[]{:S(2)}) collective-permute-start(bf16[2,2,2,2,2,24,256]{6,5,4,3,2,1,0:T(8,128)(2,1)S(1)} %fusion.10), channel_id=1, source_target_pairs={{0,8},{4,12},{8,0},{12,4},{1,9},{5,13},{9,1},{13,5},{2,10},{6,14},... | collective-permute-start | bytes 1179656 | tf_op jit(solution)/shard_map/ppermute | solution.py:31
  91.8 0.8 fusion.11
  92.6 0.2 collective-permute-start.12
  92.9 10.5 %shard_map.97 = (bf16[1024,1024]{1,0:T(8,128)(2,1)}, bf16[1024,1024]{1,0:T(8,128)(2,1)}) custom-call(bf16[512,2048]{1,0:T(8,128)(2,1)} %get-tuple-element.51.refs_0_, bf16[256,2048]{1,0:T(8,128)(2,1)} %get-tuple-element.52.refs_1_, bf16[256,2048]{1,0:T(8,128)(2,1)} %get-tuple-element.53.refs_2_, bf16[512,1024]{1,0:T(8,128)(2,1)} %get-tuple-element.54.refs_3_, ...), custom_call_target="tpu_custom_call" | custom-call | flops 4294967296 | bytes 10485760 | tf_op jit(solution)/shard_map/pallas_call | solution.py:276
  103.4 0.9 collective-permute-start.19
  104.3 1.1 fusion
  105.5 0.8 collective-permute-start.13
  106.2 0.1 bitcast_add_fusion
  106.4 1.8 %collective-permute-start.11 = (bf16[400,256]{1,0:T(8,128)(2,1)S(1)}, bf16[400,256]{1,0:T(8,128)(2,1)S(1)}, u32[]{:S(2)}, u32[]{:S(2)}) collective-permute-start(bf16[400,256]{1,0:T(8,128)(2,1)S(1)} %pad_maximum_fusion.1), channel_id=1, source_target_pairs={{0,32},{32,0},{64,96},{96,64},{128,160},{160,128},{192,224},{224,1... | collective-permute-start | bytes 614408 | tf_op jit(solution)/shard_map/ppermute | solution.py:31
  108.2 5.2 %collective-permute-done.13 = bf16[2,2,2,2,24,256]{5,4,3,2,1,0:T(8,128)(2,1)S(1)} collective-permute-done((bf16[2,2,2,2,24,256]{5,4,3,2,1,0:T(8,128)(2,1)S(1)}, bf16[2,2,2,2,24,256]{5,4,3,2,1,0:T(8,128)(2,1)S(1)}, u32[]{:S(2)}, u32[]{:S(2)}) %collective-permute-start.13) | collective-permute-done | bytes 196640 | tf_op jit(solution)/shard_map/ppermute | solution.py:31
  113.6 0.3 collective-permute-start.14
  113.9 5.2 %collective-permute-done.14 = bf16[2,2,2,24,512]{4,3,2,1,0:T(8,128)(2,1)S(1)} collective-permute-done((bf16[2,2,2,24,512]{4,3,2,1,0:T(8,128)(2,1)S(1)}, bf16[2,2,2,24,512]{4,3,2,1,0:T(8,128)(2,1)S(1)}, u32[]{:S(2)}, u32[]{:S(2)}) %collective-permute-start.14) | collective-permute-done | bytes 196640 | tf_op jit(solution)/shard_map/ppermute | solution.py:31
  119.2 1.3 collective-permute-start.15
  120.5 2.2 %collective-permute-done.15 = bf16[2,2,24,512]{3,2,1,0:T(8,128)(2,1)S(1)} collective-permute-done((bf16[2,2,24,512]{3,2,1,0:T(8,128)(2,1)S(1)}, bf16[2,2,24,512]{3,2,1,0:T(8,128)(2,1)S(1)}, u32[]{:S(2)}, u32[]{:S(2)}) %collective-permute-start.15) | collective-permute-done | bytes 98336 | tf_op jit(solution)/shard_map/ppermute | solution.py:31
  122.8 0.2 copy.37
  123.0 0.1 copy.66
  123.0 2.6 %collective-permute-start.16 = (f32[2,2,2,6,512]{4,2,3,1,0:T(2,128)S(1)}, f32[2,2,2,6,512]{4,2,3,1,0:T(2,128)S(1)}, u32[]{:S(2)}, u32[]{:S(2)}) collective-permute-start(f32[2,2,2,6,512]{4,2,3,1,0:T(2,128)S(1)} %bitcast.119), channel_id=1, source_target_pairs={{0,1},{1,0},{2,3},{3,2},{4,5},{5,4},{6,7},{7,6},{8,9},{9,8},{10,11... | collective-permute-start | bytes 294920 | tf_op jit(solution)/shard_map/ppermute | solution.py:31
  125.6 3.9 %add_convert_fusion = bf16[1024,1024]{1,0:T(8,128)(2,1)} fusion(bf16[1024,1024]{1,0:T(8,128)(2,1)} %collective-permute-done.19, bf16[1024,1024]{1,0:T(8,128)(2,1)S(1)} %copy-done.1), kind=kLoop, calls=%fused_computation.1 | loop fusion | flops 4194304 | bytes 6291456 | tf_op jit(solution)/shard_map/convert_element_type | solution.py:320
  129.5 3.6 %all-to-all-start.1 = ((bf16[8,128,1024]{2,1,0:T(8,128)(2,1)}), bf16[8,128,1024]{2,1,0:T(8,128)(2,1)S(1)}, u32[]{:S(2)}, u32[]{:S(2)}) async-start(bf16[8,128,1024]{2,1,0:T(8,128)(2,1)} %bitcast.33), calls=%async_computation.1 | async-start | bytes 4194304 | tf_op jit(solution)/shard_map/all_to_all | solution.py:35
  133.1 0.1 bitcast_add_fusion.3
  133.3 3.2 %collective-permute-start.17 = (f32[40,512]{1,0:T(8,128)S(1)}, f32[40,512]{1,0:T(8,128)S(1)}, u32[]{:S(2)}, u32[]{:S(2)}) collective-permute-start(f32[40,512]{1,0:T(8,128)S(1)} %pad_maximum_fusion.2), channel_id=1, source_target_pairs={{0,64},{32,96},{64,0},{96,32},{128,192},{160,224},{192,128},{224,1... | collective-permute-start | bytes 245768 | tf_op jit(solution)/shard_map/ppermute | solution.py:31
  136.5 2.7 %collective-permute-done.17 = f32[40,512]{1,0:T(8,128)S(1)} collective-permute-done((f32[40,512]{1,0:T(8,128)S(1)}, f32[40,512]{1,0:T(8,128)S(1)}, u32[]{:S(2)}, u32[]{:S(2)}) %collective-permute-start.17) | collective-permute-done | bytes 81952 | tf_op jit(solution)/shard_map/ppermute | solution.py:31
  139.3 0.1 bitcast_add_fusion.4
  139.5 1.4 collective-permute-start.18
  140.8 5.8 %collective-permute-done.18 = f32[28,512]{1,0:T(8,128)S(1)} collective-permute-done((f32[28,512]{1,0:T(8,128)S(1)}, f32[28,512]{1,0:T(8,128)S(1)}, u32[]{:S(2)}, u32[]{:S(2)}) %collective-permute-start.18) | collective-permute-done | bytes 57376 | tf_op jit(solution)/shard_map/ppermute | solution.py:31
  146.7 0.5 fusion.31
  147.3 10.9 %all-to-all-done.1 = bf16[8,128,1024]{2,1,0:T(8,128)(2,1)S(1)} async-done(((bf16[8,128,1024]{2,1,0:T(8,128)(2,1)}), bf16[8,128,1024]{2,1,0:T(8,128)(2,1)S(1)}, u32[]{:S(2)}, u32[]{:S(2)}) %all-to-all-start.1) | async-done | bytes 2097184 | tf_op jit(solution)/shard_map/all_to_all | solution.py:35
  158.3 1.9 %collective-permute-start.20 = (f32[6,512]{1,0:T(8,128)S(1)}, f32[6,512]{1,0:T(8,128)S(1)}, u32[]{:S(2)}, u32[]{:S(2)}) collective-permute-start(f32[6,512]{1,0:T(8,128)S(1)} %bitcast.122), channel_id=1, source_target_pairs={{0,2},{2,0},{1,3},{3,1},{4,6},{6,4},{5,7},{7,5},{8,10},{10,8},{9,1... | collective-permute-start | bytes 36872 | tf_op jit(solution)/shard_map/ppermute | solution.py:31
  160.2 0.3 convert_reduce_fusion
  160.5 0.2 fusion.5
  160.7 1.0 fusion.9
  161.8 0.6 fusion.20
  (93 shorter events, 0.9 us)
Async XLA Ops:
  4.4 6.1 %copy-start.12 = (s32[1,128]{1,0:T(1,128)S(1)}, s32[1,128]{1,0:T(1,128)}, u32[]{:S(2)}) copy-start(s32[1,128]{1,0:T(1,128)} %param.10) | copy-start | bytes 1540
  4.4 6.2 %copy-start.4 = (bf16[1,128,1536]{2,1,0:T(8,128)(2,1)S(1)}, bf16[1,128,1536]{2,1,0:T(8,128)(2,1)}, u32[]{:S(2)}) copy-start(bf16[1,128,1536]{2,1,0:T(8,128)(2,1)} %param.7) | copy-start | bytes 1179652
  4.4 32.3 %all-to-all-start = ((bf16[8,128,1024]{2,1,0:T(8,128)(2,1)}), bf16[8,128,1024]{2,1,0:T(8,128)(2,1)S(1)}, u32[]{:S(2)}, u32[]{:S(2)}) async-start(bf16[8,128,1024]{2,1,0:T(8,128)(2,1)} %broadcast_in_dim.33), calls=%async_computation | async-start | bytes 4194304 | tf_op jit(solution)/shard_map/all_to_all | solution.py:35
  10.7 32.4 %copy-start.3 = (bf16[128,1664]{1,0:T(8,128)(2,1)}, bf16[128,1664]{1,0:T(8,128)(2,1)S(1)}, u32[]{:S(2)}) copy-start(bf16[128,1664]{1,0:T(8,128)(2,1)S(1)} %pad_maximum_fusion.refs_0_.refs_6_) | copy-start | bytes 1277956
  10.7 14.9 %collective-permute-start = (bf16[128,1664]{1,0:T(8,128)(2,1)S(1)}, bf16[128,1664]{1,0:T(8,128)(2,1)S(1)}, u32[]{:S(2)}, u32[]{:S(2)}) collective-permute-start(bf16[128,1664]{1,0:T(8,128)(2,1)S(1)} %pad_maximum_fusion.refs_0_.refs_6_), channel_id=1, source_target_pairs={{0,32},{32,64},{64,96},{96,128},{128,160},{160,192},{192,224},{224... | collective-permute-start | bytes 1277960 | tf_op jit(solution)/shard_map/ppermute | solution.py:27
  12.4 13.2 %collective-permute-start.1 = (bf16[128,1664]{1,0:T(8,128)(2,1)S(1)}, bf16[128,1664]{1,0:T(8,128)(2,1)S(1)}, u32[]{:S(2)}, u32[]{:S(2)}) collective-permute-start(bf16[128,1664]{1,0:T(8,128)(2,1)S(1)} %pad_maximum_fusion.refs_0_.refs_6_), channel_id=1, source_target_pairs={{0,224},{32,0},{64,32},{96,64},{128,96},{160,128},{192,160},{224,1... | collective-permute-start | bytes 1277960 | tf_op jit(solution)/shard_map/ppermute | solution.py:27
  25.6 17.5 %copy-start.8 = (bf16[128,1664]{1,0:T(8,128)(2,1)}, bf16[128,1664]{1,0:T(8,128)(2,1)S(1)}, u32[]{:S(2)}) copy-start(bf16[128,1664]{1,0:T(8,128)(2,1)S(1)} %collective-permute-done.refs_1_.refs_7_) | copy-start | bytes 1277956
  25.6 17.5 %copy-start.9 = (bf16[128,1664]{1,0:T(8,128)(2,1)}, bf16[128,1664]{1,0:T(8,128)(2,1)S(1)}, u32[]{:S(2)}) copy-start(bf16[128,1664]{1,0:T(8,128)(2,1)S(1)} %collective-permute-done.1.refs_2_.refs_8_) | copy-start | bytes 1277956
  25.6 11.2 %collective-permute-start.2 = (bf16[128,1664]{1,0:T(8,128)(2,1)S(1)}, bf16[128,1664]{1,0:T(8,128)(2,1)}, u32[]{:S(2)}, u32[]{:S(2)}) collective-permute-start(bf16[128,1664]{1,0:T(8,128)(2,1)S(1)} %collective-permute-done.refs_1_.refs_7_), channel_id=1, source_target_pairs={{0,32},{32,64},{64,96},{96,128},{128,160},{160,192},{192,224},{224... | collective-permute-start | bytes 1277960 | tf_op jit(solution)/shard_map/ppermute | solution.py:27
  25.7 11.1 %collective-permute-start.3 = (bf16[128,1664]{1,0:T(8,128)(2,1)S(1)}, bf16[128,1664]{1,0:T(8,128)(2,1)}, u32[]{:S(2)}, u32[]{:S(2)}) collective-permute-start(bf16[128,1664]{1,0:T(8,128)(2,1)S(1)} %collective-permute-done.1.refs_2_.refs_8_), channel_id=1, source_target_pairs={{0,224},{32,0},{64,32},{96,64},{128,96},{160,128},{192,160},{224,1... | collective-permute-start | bytes 1277960 | tf_op jit(solution)/shard_map/ppermute | solution.py:27
  36.7 6.4 %copy-start.2 = (bf16[8,128,1024]{2,1,0:T(8,128)(2,1)}, bf16[8,128,1024]{2,1,0:T(8,128)(2,1)S(1)}, u32[]{:S(2)}) copy-start(bf16[8,128,1024]{2,1,0:T(8,128)(2,1)S(1)} %all-to-all-done) | copy-start | bytes 6291460
  36.7 6.3 %collective-permute-start.4 = (bf16[1024,1024]{1,0:T(8,128)(2,1)S(1)}, bf16[1024,1024]{1,0:T(8,128)(2,1)S(1)}, u32[]{:S(2)}, u32[]{:S(2)}) collective-permute-start(bf16[1024,1024]{1,0:T(8,128)(2,1)S(1)} %bitcast.111), channel_id=1, source_target_pairs={{0,2},{2,0},{1,3},{3,1},{4,6},{6,4},{5,7},{7,5},{8,10},{10,8},{9,1... | collective-permute-start | bytes 6291464 | tf_op jit(solution)/shard_map/ppermute | solution.py:31
  39.3 17.2 %collective-permute-start.5 = (bf16[128,1664]{1,0:T(8,128)(2,1)}, bf16[128,1664]{1,0:T(8,128)(2,1)S(1)}, u32[]{:S(2)}, u32[]{:S(2)}) collective-permute-start(bf16[128,1664]{1,0:T(8,128)(2,1)} %collective-permute-done.2.refs_3_.refs_9_), channel_id=1, source_target_pairs={{0,32},{32,64},{64,96},{96,128},{128,160},{160,192},{192,224},{224... | collective-permute-start | bytes 1277960 | tf_op jit(solution)/shard_map/ppermute | solution.py:27
  40.7 15.8 %collective-permute-start.6 = (bf16[128,1664]{1,0:T(8,128)(2,1)}, bf16[128,1664]{1,0:T(8,128)(2,1)S(1)}, u32[]{:S(2)}, u32[]{:S(2)}) collective-permute-start(bf16[128,1664]{1,0:T(8,128)(2,1)} %collective-permute-done.3.refs_0_.refs_10_), channel_id=1, source_target_pairs={{0,224},{32,0},{64,32},{96,64},{128,96},{160,128},{192,160},{224,1... | collective-permute-start | bytes 1277960 | tf_op jit(solution)/shard_map/ppermute | solution.py:27
  43.1 1.4 copy-start.7
  56.5 4.2 %copy-start.5 = (bf16[128,1664]{1,0:T(8,128)(2,1)}, bf16[128,1664]{1,0:T(8,128)(2,1)S(1)}, u32[]{:S(2)}) copy-start(bf16[128,1664]{1,0:T(8,128)(2,1)S(1)} %collective-permute-done.5.refs_1_.refs_11_) | copy-start | bytes 1277956
  56.6 12.2 %copy-start.6 = (bf16[128,1664]{1,0:T(8,128)(2,1)}, bf16[128,1664]{1,0:T(8,128)(2,1)S(1)}, u32[]{:S(2)}) copy-start(bf16[128,1664]{1,0:T(8,128)(2,1)S(1)} %collective-permute-done.6.refs_0_) | copy-start | bytes 1277956
  56.6 12.1 %collective-permute-start.7 = (bf16[64,1664]{1,0:T(8,128)(2,1)S(1)}, bf16[64,1664]{1,0:T(8,128)(2,1)S(1)}, u32[]{:S(2)}, u32[]{:S(2)}) collective-permute-start(bf16[64,1664]{1,0:T(8,128)(2,1)S(1)} %slice.88), channel_id=1, source_target_pairs={{0,32},{32,64},{64,96},{96,128},{128,160},{160,192},{192,224},{224... | collective-permute-start | bytes 638984 | tf_op jit(solution)/shard_map/ppermute | solution.py:27
  58.1 10.6 %collective-permute-start.8 = (bf16[64,1664]{1,0:T(8,128)(2,1)S(1)}, bf16[64,1664]{1,0:T(8,128)(2,1)S(1)}, u32[]{:S(2)}, u32[]{:S(2)}) collective-permute-start(bf16[64,1664]{1,0:T(8,128)(2,1)S(1)} %slice.89), channel_id=1, source_target_pairs={{0,224},{32,0},{64,32},{96,64},{128,96},{160,128},{192,160},{224,1... | collective-permute-start | bytes 638984 | tf_op jit(solution)/shard_map/ppermute | solution.py:27
  68.7 0.7 copy-start.10
  68.7 0.7 copy-start.11
  83.1 3.9 %collective-permute-start.9 = (bf16[1536,512]{1,0:T(8,128)(2,1)}, bf16[1536,512]{1,0:T(8,128)(2,1)S(1)}, u32[]{:S(2)}, u32[]{:S(2)}) collective-permute-start(bf16[1536,512]{1,0:T(8,128)(2,1)} %get-tuple-element.49), channel_id=1, source_target_pairs={{0,2},{2,0},{1,3},{3,1},{4,6},{6,4},{5,7},{7,5},{8,10},{10,8},{9,1... | collective-permute-start | bytes 4718600 | tf_op jit(solution)/shard_map/ppermute | solution.py:31
  89.9 16.3 %collective-permute-start.10 = (bf16[2,2,2,2,2,24,256]{6,5,4,3,2,1,0:T(8,128)(2,1)S(1)}, bf16[2,2,2,2,2,24,256]{6,5,4,3,2,1,0:T(8,128)(2,1)S(1)}, u32[]{:S(2)}, u32[]{:S(2)}) collective-permute-start(bf16[2,2,2,2,2,24,256]{6,5,4,3,2,1,0:T(8,128)(2,1)S(1)} %fusion.10), channel_id=1, source_target_pairs={{0,8},{4,12},{8,0},{12,4},{1,9},{5,13},{9,1},{13,5},{2,10},{6,14},... | collective-permute-start | bytes 1179656 | tf_op jit(solution)/shard_map/ppermute | solution.py:31
  92.6 11.7 %collective-permute-start.12 = (bf16[2,2,2,2,2,24,256]{6,5,4,2,1,0,3:T(8,128)(2,1)}, bf16[2,2,2,2,2,24,256]{6,5,4,2,1,0,3:T(8,128)(2,1)}, u32[]{:S(2)}, u32[]{:S(2)}) collective-permute-start(bf16[2,2,2,2,2,24,256]{6,5,4,2,1,0,3:T(8,128)(2,1)} %fusion.11), channel_id=1, source_target_pairs={{0,32},{32,0},{64,96},{96,64},{128,160},{160,128},{192,224},{224,1... | collective-permute-start | bytes 1179656 | tf_op jit(solution)/shard_map/ppermute | solution.py:31
  103.4 22.2 %collective-permute-start.19 = (bf16[1024,1024]{1,0:T(8,128)(2,1)}, bf16[1024,1024]{1,0:T(8,128)(2,1)}, u32[]{:S(2)}, u32[]{:S(2)}) collective-permute-start(bf16[1024,1024]{1,0:T(8,128)(2,1)} %get-tuple-element.58), channel_id=1, source_target_pairs={{0,2},{2,0},{1,3},{3,1},{4,6},{6,4},{5,7},{7,5},{8,10},{10,8},{9,1... | collective-permute-start | bytes 6291464 | tf_op jit(solution)/shard_map/ppermute | solution.py:31
  105.5 7.9 %collective-permute-start.13 = (bf16[2,2,2,2,24,256]{5,4,3,2,1,0:T(8,128)(2,1)S(1)}, bf16[2,2,2,2,24,256]{5,4,3,2,1,0:T(8,128)(2,1)S(1)}, u32[]{:S(2)}, u32[]{:S(2)}) collective-permute-start(bf16[2,2,2,2,24,256]{5,4,3,2,1,0:T(8,128)(2,1)S(1)} %fusion.17), channel_id=1, source_target_pairs={{0,8},{4,12},{8,0},{12,4},{1,9},{5,13},{9,1},{13,5},{2,10},{6,14},... | collective-permute-start | bytes 589832 | tf_op jit(solution)/shard_map/ppermute | solution.py:31
  106.4 7.0 %collective-permute-start.11 = (bf16[400,256]{1,0:T(8,128)(2,1)S(1)}, bf16[400,256]{1,0:T(8,128)(2,1)S(1)}, u32[]{:S(2)}, u32[]{:S(2)}) collective-permute-start(bf16[400,256]{1,0:T(8,128)(2,1)S(1)} %pad_maximum_fusion.1), channel_id=1, source_target_pairs={{0,32},{32,0},{64,96},{96,64},{128,160},{160,128},{192,224},{224,1... | collective-permute-start | bytes 614408 | tf_op jit(solution)/shard_map/ppermute | solution.py:31
  113.6 12.1 %copy-start.1 = (bf16[1024,1024]{1,0:T(8,128)(2,1)S(1)}, bf16[1024,1024]{1,0:T(8,128)(2,1)}, u32[]{:S(2)}) copy-start(bf16[1024,1024]{1,0:T(8,128)(2,1)} %get-tuple-element.57) | copy-start | bytes 6291460
  113.6 5.5 %collective-permute-start.14 = (bf16[2,2,2,24,512]{4,3,2,1,0:T(8,128)(2,1)S(1)}, bf16[2,2,2,24,512]{4,3,2,1,0:T(8,128)(2,1)S(1)}, u32[]{:S(2)}, u32[]{:S(2)}) collective-permute-start(bf16[2,2,2,24,512]{4,3,2,1,0:T(8,128)(2,1)S(1)} %fusion.18), channel_id=1, source_target_pairs={{0,4},{4,0},{8,12},{12,8},{1,5},{5,1},{9,13},{13,9},{2,6},{6,2},{1... | collective-permute-start | bytes 589832 | tf_op jit(solution)/shard_map/ppermute | solution.py:31
  119.2 3.6 %collective-permute-start.15 = (bf16[2,2,24,512]{3,2,1,0:T(8,128)(2,1)S(1)}, bf16[2,2,24,512]{3,2,1,0:T(8,128)(2,1)S(1)}, u32[]{:S(2)}, u32[]{:S(2)}) collective-permute-start(bf16[2,2,24,512]{3,2,1,0:T(8,128)(2,1)S(1)} %fusion.19), channel_id=1, source_target_pairs={{0,16},{16,0},{1,17},{17,1},{2,18},{18,2},{3,19},{19,3},{4,20},{20... | collective-permute-start | bytes 294920 | tf_op jit(solution)/shard_map/ppermute | solution.py:31
  123.0 10.1 %collective-permute-start.16 = (f32[2,2,2,6,512]{4,2,3,1,0:T(2,128)S(1)}, f32[2,2,2,6,512]{4,2,3,1,0:T(2,128)S(1)}, u32[]{:S(2)}, u32[]{:S(2)}) collective-permute-start(f32[2,2,2,6,512]{4,2,3,1,0:T(2,128)S(1)} %bitcast.119), channel_id=1, source_target_pairs={{0,1},{1,0},{2,3},{3,2},{4,5},{5,4},{6,7},{7,6},{8,9},{9,8},{10,11... | collective-permute-start | bytes 294920 | tf_op jit(solution)/shard_map/ppermute | solution.py:31
  129.5 28.7 %all-to-all-start.1 = ((bf16[8,128,1024]{2,1,0:T(8,128)(2,1)}), bf16[8,128,1024]{2,1,0:T(8,128)(2,1)S(1)}, u32[]{:S(2)}, u32[]{:S(2)}) async-start(bf16[8,128,1024]{2,1,0:T(8,128)(2,1)} %bitcast.33), calls=%async_computation.1 | async-start | bytes 4194304 | tf_op jit(solution)/shard_map/all_to_all | solution.py:35
  133.3 27.2 %copy-start = (bf16[1,128,1024]{2,1,0:T(8,128)(2,1)S(1)}, bf16[1,128,1024]{2,1,0:T(8,128)(2,1)}, u32[]{:S(2)}) copy-start(bf16[1,128,1024]{2,1,0:T(8,128)(2,1)} %param.9) | copy-start | bytes 786436
  133.3 5.9 %collective-permute-start.17 = (f32[40,512]{1,0:T(8,128)S(1)}, f32[40,512]{1,0:T(8,128)S(1)}, u32[]{:S(2)}, u32[]{:S(2)}) collective-permute-start(f32[40,512]{1,0:T(8,128)S(1)} %pad_maximum_fusion.2), channel_id=1, source_target_pairs={{0,64},{32,96},{64,0},{96,32},{128,192},{160,224},{192,128},{224,1... | collective-permute-start | bytes 245768 | tf_op jit(solution)/shard_map/ppermute | solution.py:31
  139.5 7.2 %collective-permute-start.18 = (f32[28,512]{1,0:T(8,128)S(1)}, f32[28,512]{1,0:T(8,128)S(1)}, u32[]{:S(2)}, u32[]{:S(2)}) collective-permute-start(f32[28,512]{1,0:T(8,128)S(1)} %pad_maximum_fusion.3), channel_id=1, source_target_pairs={{0,128},{32,160},{64,192},{96,224},{128,0},{160,32},{192,64},{224,... | collective-permute-start | bytes 172040 | tf_op jit(solution)/shard_map/ppermute | solution.py:31
  158.3 3.5 %collective-permute-start.20 = (f32[6,512]{1,0:T(8,128)S(1)}, f32[6,512]{1,0:T(8,128)S(1)}, u32[]{:S(2)}, u32[]{:S(2)}) collective-permute-start(f32[6,512]{1,0:T(8,128)S(1)} %bitcast.122), channel_id=1, source_target_pairs={{0,2},{2,0},{1,3},{3,1},{4,6},{6,4},{5,7},{7,5},{8,10},{10,8},{9,1... | collective-permute-start | bytes 36872 | tf_op jit(solution)/shard_map/ppermute | solution.py:31
